TPU v7x, 512 devices: a whole 4x4x16 slice. The times are simulated.
512 devices in a mesh: dp: 16 (over x, y), expert: 32 (over z, core).
Axes of the slice: x: 4, y: 4, z: 16, core: 2. Of those that a mesh axis runs over, the one named last changes fastest.
Arguments:
- tokens: bfloat16 [65536, 1024], P(('dp', 'expert')), may hold values from -6 to 6
- expert_ids: int32 [65536, 6], P(('dp', 'expert')), may hold values from 0 to 63, all different within a row; in each aligned block of 128 rows (0 to 127, 128 to 255, ...) at most 13 rows name the same one
- router_gates: float32 [65536, 6], P(('dp', 'expert')), may hold values from 0.05 to 1
- w_in: bfloat16 [64, 2, 704, 1024], P('expert', None, 'dp'), may hold values from -0.1875 to 0.1875
- w_down: bfloat16 [64, 704, 1024], P('expert', 'dp'), may hold values from -0.21875 to 0.21875
- cotangent: bfloat16 [65536, 1024], P(('dp', 'expert')), may hold values from -6 to 6
Outputs:
- layer_output: bfloat16 [65536, 1024], P(('dp', 'expert'))
- token_grads: bfloat16 [65536, 1024], P(('dp', 'expert'))
- gate_grads: float32 [65536, 6], P(('dp', 'expert'))
Inputs may be any that keep to these rules, and one draw needn't show every extreme that they name: `expert_ids`: each row names 6 different experts. The rows of one device name no expert more than 13 times, and in every draw some device names some expert exactly 13 times.
All inputs are finite; a program needn't handle non-finite values.
Results may differ from a plain program's by a relative error of at most 0.0064.
Values may be sent and summed in bfloat16 or wider, within the bound.
No kernel may reach another device: no remote copies, remote signals or barrier semaphores. Data moves between devices by JAX's collectives and lax.ppermute only.
A program may use at most 64 MiB of HBM per device.

v0:
```python
import jax
import jax.numpy as jnp
from jax import lax
from jax.sharding import PartitionSpec as P


def expert_terms(rows_x, rows_grad, full_in, full_down):
    column_count, exp_local, slot_count, model_width = rows_x.shape
    hidden_width = full_down.shape[1]
    x_lead = jnp.swapaxes(rows_x, 0, 1).reshape(exp_local, column_count * slot_count, model_width)
    g_lead = jnp.swapaxes(rows_grad, 0, 1).reshape(
        exp_local, column_count * slot_count, model_width
    )
    w_pair = full_in.reshape(exp_local, 2 * hidden_width, model_width)
    both_pre = jnp.einsum("erd,egd->erg", x_lead, w_pair, preferred_element_type=jnp.float32)
    gate_pre = both_pre[:, :, :hidden_width]
    up_pre = both_pre[:, :, hidden_width:]
    sigmoid_gate = jax.nn.sigmoid(gate_pre)
    activated = gate_pre * sigmoid_gate
    hidden = (activated * up_pre).astype(jnp.bfloat16)
    out_acc = jnp.einsum("erf,efd->erd", hidden, full_down, preferred_element_type=jnp.float32)
    grad_hidden = jnp.einsum("erd,efd->erf", g_lead, full_down, preferred_element_type=jnp.float32)
    grad_up = (grad_hidden * activated).astype(jnp.bfloat16)
    grad_gate = (
        grad_hidden * up_pre * sigmoid_gate * (1.0 + gate_pre * (1.0 - sigmoid_gate))
    ).astype(jnp.bfloat16)
    grad_pair = jnp.concatenate([grad_gate, grad_up], axis=2)
    grad_acc = jnp.einsum("erg,egd->erd", grad_pair, w_pair, preferred_element_type=jnp.float32)
    out_rows = jnp.swapaxes(
        out_acc.astype(jnp.bfloat16).reshape(exp_local, column_count, slot_count, model_width), 0, 1
    )
    grad_rows = jnp.swapaxes(
        grad_acc.astype(jnp.bfloat16).reshape(exp_local, column_count, slot_count, model_width),
        0,
        1,
    )
    return (out_rows, grad_rows)


def body(tokens, expert_ids, router_gates, w_in, w_down, cotangent):
    tok_rows = tokens.shape[0]
    model_width = tokens.shape[1]
    top_count = expert_ids.shape[1]
    column_count = lax.axis_size("expert")
    exp_local = w_in.shape[0]
    experts_all = exp_local * column_count
    capacity = tok_rows * top_count // experts_all + 1
    slot_total = experts_all * capacity
    flat_ids = expert_ids.reshape(-1)
    onehot = (flat_ids[:, None] == jnp.arange(experts_all, dtype=jnp.int32)[None, :]).astype(
        jnp.int32
    )
    slot_rank = jnp.sum((jnp.cumsum(onehot, axis=0) - onehot) * onehot, axis=1)
    slot_index = flat_ids * capacity + slot_rank
    x_rep = jnp.broadcast_to(tokens[:, None, :], (tok_rows, top_count, model_width)).reshape(
        -1, model_width
    )
    grad_rep = (router_gates[:, :, None] * cotangent[:, None, :].astype(jnp.float32)).astype(
        jnp.bfloat16
    )
    grad_rep = grad_rep.reshape(-1, model_width)
    x_buf = jnp.zeros((slot_total, model_width), jnp.bfloat16).at[slot_index].set(x_rep)
    grad_buf = jnp.zeros((slot_total, model_width), jnp.bfloat16).at[slot_index].set(grad_rep)
    grid_shape = (column_count, exp_local, capacity, model_width)
    full_in, full_down = (
        lax.all_gather(w_in, "dp", axis=2, tiled=True),
        lax.all_gather(w_down, "dp", axis=1, tiled=True),
    )
    x_in, grad_in = (
        lax.all_to_all(x_buf, "expert", split_axis=0, concat_axis=0, tiled=True),
        lax.all_to_all(grad_buf, "expert", split_axis=0, concat_axis=0, tiled=True),
    )
    out_send, grad_send = expert_terms(
        x_in.reshape(grid_shape), grad_in.reshape(grid_shape), full_in, full_down
    )
    out_back, grad_back = (
        lax.all_to_all(
            out_send.reshape(slot_total, model_width),
            "expert",
            split_axis=0,
            concat_axis=0,
            tiled=True,
        ),
        lax.all_to_all(
            grad_send.reshape(slot_total, model_width),
            "expert",
            split_axis=0,
            concat_axis=0,
            tiled=True,
        ),
    )
    out_rows = out_back[slot_index].reshape(tok_rows, top_count, model_width).astype(jnp.float32)
    grad_rows = grad_back[slot_index].reshape(tok_rows, top_count, model_width).astype(jnp.float32)
    layer_output = jnp.sum(router_gates[:, :, None] * out_rows, axis=1).astype(jnp.bfloat16)
    token_grads = jnp.sum(grad_rows, axis=1).astype(jnp.bfloat16)
    gate_grads = jnp.sum(cotangent[:, None, :].astype(jnp.float32) * out_rows, axis=2)
    return (layer_output, token_grads, gate_grads)


def solution(mesh):
    placed = (
        P(("dp", "expert"), None),
        P(("dp", "expert"), None),
        P(("dp", "expert"), None),
        P("expert", None, "dp", None),
        P("expert", "dp", None),
        P(("dp", "expert"), None),
    )
    return jax.shard_map(
        body,
        mesh=mesh,
        in_specs=placed,
        out_specs=(P(("dp", "expert"), None), P(("dp", "expert"), None), P(("dp", "expert"), None)),
        check_vma=False,
    )
```

profile of v0, /device:TPU:1, one launch (start us, length us, event | category | flops | bytes accessed | tf_op | source)
XLA Modules:
  0.0 500.9 jit_solution(13880732950513625503)
XLA Ops:
  7.2 0.0 all-gather.3.cloned.1.call-start
  7.2 0.7 all-gather.3.cloned.1.call-update
  7.9 0.8 copy.34
  8.7 0.1 eq.29
  8.8 0.1 eq.25
  9.0 1.8 reduce-window.6
  10.8 0.3 slice_reduce_fusion
  11.1 0.7 broadcast_multiply_fusion
  11.8 0.1 copy.33
  11.9 0.1 mul.79
  12.1 1.3 broadcast_in_dim.2
  13.3 1.5 reshape.144
  14.8 0.1 fusion.26
  15.0 6.9 %scatter_custom_fusion = bf16[832,1024]{1,0:T(8,128)(2,1)S(1)} fusion(s32[768]{0:T(1024)S(1)} %fusion.28, bf16[768,1024]{1,0:T(8,128)(2,1)} %reshape.144, bf16[]{:T(256)} %constant.6.clone.1), kind=kCustom, calls=%fused_computation.28 | custom fusion | bytes 1704448 | tf_op jit(solution)/shard_map/scatter | solution.py:62
  21.9 1.6 all_to_all.28
  23.4 16.9 %all-to-all-start = ((bf16[32,26,1024]{2,1,0:T(8,128)(2,1)}), bf16[32,26,1024]{2,1,0:T(8,128)(2,1)}, u32[]{:S(2)}, u32[]{:S(2)}) async-start(bf16[32,26,1024]{2,1,0:T(8,128)(2,1)} %all_to_all.28), calls=%async_computation | async-start | bytes 4194304 | tf_op jit(solution)/shard_map/all_to_all | solution.py:70
  40.4 0.0 copy-done.7
  40.4 0.1 copy.32
  40.5 0.1 mul.84
  40.6 0.0 copy-done.5
  40.6 2.6 mul.86
  43.2 3.1 mul.87
  46.3 9.5 %scatter_custom_fusion.1 = bf16[832,1024]{1,0:T(8,128)(2,1)} fusion(s32[768]{0:T(1024)S(1)} %fusion.28, f32[768,1024]{1,0:T(8,128)S(1)} %mul.87, f32[768]{0:T(1024)S(1)} %mul.84, bf16[]{:T(256)} %constant.6.clone.1), kind=kCustom, calls=%fused_computation.25 | custom fusion | flops 1572864 | bytes 4853762 | tf_op jit(solution)/shard_map/scatter | solution.py:63
  55.8 3.5 all_to_all.33
  59.3 79.7 %all-to-all-done = bf16[32,26,1024]{2,1,0:T(8,128)(2,1)} async-done(((bf16[32,26,1024]{2,1,0:T(8,128)(2,1)}), bf16[32,26,1024]{2,1,0:T(8,128)(2,1)}, u32[]{:S(2)}, u32[]{:S(2)}) %all-to-all-start) | async-done | bytes 1703968 | tf_op jit(solution)/shard_map/all_to_all | solution.py:70
  139.0 5.2 %all-to-all-start.2 = ((bf16[32,26,1024]{2,1,0:T(8,128)(2,1)}), bf16[32,26,1024]{2,1,0:T(8,128)(2,1)S(1)}, u32[]{:S(2)}, u32[]{:S(2)}) async-start(bf16[32,26,1024]{2,1,0:T(8,128)(2,1)} %all_to_all.33), calls=%async_computation.2 | async-start | bytes 4194304 | tf_op jit(solution)/shard_map/all_to_all | solution.py:71
  144.2 0.0 all-gather.5.cloned.1.call-start
  144.3 0.7 all-gather.5.cloned.1.call-update
  145.0 2.5 copy.37
  147.5 3.0 copy.38
  150.5 92.3 %all-to-all-done.2 = bf16[32,26,1024]{2,1,0:T(8,128)(2,1)S(1)} async-done(((bf16[32,26,1024]{2,1,0:T(8,128)(2,1)}), bf16[32,26,1024]{2,1,0:T(8,128)(2,1)S(1)}, u32[]{:S(2)}, u32[]{:S(2)}) %all-to-all-start.2) | async-done | bytes 1703968 | tf_op jit(solution)/shard_map/all_to_all | solution.py:71
  242.8 0.9 copy.46
  243.7 1.8 copy.47
  245.5 0.0 copy-start.4
  245.5 0.0 all-gather.3.cloned.1.call-done
  245.5 4.6 copy.39
  250.1 0.0 copy-start.1
  250.2 2.5 copy-done.1
  252.6 0.0 copy-done.4
  252.6 4.8 fusion.16
  257.4 6.2 %multiply_convert_fusion.2 = (bf16[2,416,704]{2,1,0:T(8,128)(2,1)S(1)}, bf16[2,416,704]{2,1,0:T(8,128)(2,1)S(1)}) fusion(f32[2,416,1408]{2,1,0:T(8,128)} %fusion.16, bf16[2,704,1024]{2,0,1:T(2,128)(2,1)} %all-gather.5.cloned.1.call-done, bf16[2,416,1024]{2,0,1:T(2,128)(2,1)S(1)} %bitcast.48), kind=kOutput, calls=%fused_computation.8 | convolution fusion | flops 1207185408 | bytes 11616256 | tf_op jit(solution)/shard_map/erd,efd->erf/dot_general | solution.py:22
  263.6 2.8 fusion.9
  266.4 1.8 copy.50
  268.2 0.5 copy.51
  268.7 2.3 copy.52
  271.0 5.5 %all-to-all-start.3 = ((bf16[32,26,1024]{2,1,0:T(8,128)(2,1)}), bf16[32,26,1024]{2,1,0:T(8,128)(2,1)S(1)}, u32[]{:S(2)}, u32[]{:S(2)}) async-start(bf16[32,26,1024]{2,1,0:T(8,128)(2,1)} %copy.52), calls=%async_computation.3 | async-start | bytes 4194304 | tf_op jit(solution)/shard_map/all_to_all | solution.py:84
  276.5 5.3 %fusion.12 = bf16[2,416,1024]{2,1,0:T(8,128)(2,1)S(1)} fusion(bf16[2,704,1024]{2,0,1:T(2,128)(2,1)} %all-gather.5.cloned.1.call-done, f32[2,416,1408]{2,1,0:T(8,128)} %fusion.16), kind=kOutput, calls=%fused_computation.21 | convolution fusion | flops 1203937280 | bytes 9699328 | tf_op jit(solution)/shard_map/erf,efd->erd/dot_general | solution.py:21
  281.8 1.8 copy.42
  283.5 0.5 copy.43
  284.0 2.3 copy.44
  286.4 88.6 %all-to-all-done.3 = bf16[32,26,1024]{2,1,0:T(8,128)(2,1)S(1)} async-done(((bf16[32,26,1024]{2,1,0:T(8,128)(2,1)}), bf16[32,26,1024]{2,1,0:T(8,128)(2,1)S(1)}, u32[]{:S(2)}, u32[]{:S(2)}) %all-to-all-start.3) | async-done | bytes 1703968 | tf_op jit(solution)/shard_map/all_to_all | solution.py:84
  375.0 1.3 copy-done
  376.3 5.2 %all-to-all-start.1 = ((bf16[32,26,1024]{2,1,0:T(8,128)(2,1)}), bf16[32,26,1024]{2,1,0:T(8,128)(2,1)}, u32[]{:S(2)}, u32[]{:S(2)}) async-start(bf16[32,26,1024]{2,1,0:T(8,128)(2,1)} %copy.44), calls=%async_computation.1 | async-start | bytes 4194304 | tf_op jit(solution)/shard_map/all_to_all | solution.py:77
  381.5 0.9 convert_element_type.53
  382.4 2.5 all_to_all.37
  384.9 3.6 gather_fusion.1
  388.5 2.5 reshape.122
  391.0 2.2 reduce_sum.44
  393.2 87.5 %all-to-all-done.1 = bf16[32,26,1024]{2,1,0:T(8,128)(2,1)} async-done(((bf16[32,26,1024]{2,1,0:T(8,128)(2,1)}), bf16[32,26,1024]{2,1,0:T(8,128)(2,1)}, u32[]{:S(2)}, u32[]{:S(2)}) %all-to-all-start.1) | async-done | bytes 1703968 | tf_op jit(solution)/shard_map/all_to_all | solution.py:77
  480.7 2.5 all_to_all.32
  483.2 2.8 gather_fusion
  486.0 2.1 reshape.123
  488.2 4.8 multiply_reduce_fusion
  492.9 0.7 copy.53
  (14 shorter events, 0.1 us)
Async XLA Ops:
  7.2 238.4 %all-gather.3.cloned.1.call-start = ((), (), s32[]{:S(2)}) async-start(), calls=%async_computation.4 | async-start | bytes 6127616 | tf_op jit(solution)/shard_map/all_gather | solution.py:66
  23.4 16.9 %copy-start.7 = (f32[128,6]{0,1:T(8,128)S(1)}, f32[128,6]{0,1:T(8,128)}, u32[]{:S(2)}) copy-start(f32[128,6]{0,1:T(8,128)} %param.8) | copy-start | bytes 9220
  23.4 17.2 %copy-start.5 = (bf16[128,1024]{1,0:T(8,128)(2,1)S(1)}, bf16[128,1024]{1,0:T(8,128)(2,1)}, u32[]{:S(2)}) copy-start(bf16[128,1024]{1,0:T(8,128)(2,1)} %param.11) | copy-start | bytes 786436
  23.4 115.6 %all-to-all-start = ((bf16[32,26,1024]{2,1,0:T(8,128)(2,1)}), bf16[32,26,1024]{2,1,0:T(8,128)(2,1)}, u32[]{:S(2)}, u32[]{:S(2)}) async-start(bf16[32,26,1024]{2,1,0:T(8,128)(2,1)} %all_to_all.28), calls=%async_computation | async-start | bytes 4194304 | tf_op jit(solution)/shard_map/all_to_all | solution.py:70
  139.0 103.8 %all-to-all-start.2 = ((bf16[32,26,1024]{2,1,0:T(8,128)(2,1)}), bf16[32,26,1024]{2,1,0:T(8,128)(2,1)S(1)}, u32[]{:S(2)}, u32[]{:S(2)}) async-start(bf16[32,26,1024]{2,1,0:T(8,128)(2,1)} %all_to_all.33), calls=%async_computation.2 | async-start | bytes 4194304 | tf_op jit(solution)/shard_map/all_to_all | solution.py:71
  144.2 113.2 %all-gather.5.cloned.1.call-start = ((), (), s32[]{:S(2)}) async-start(), calls=%async_computation.5 | async-start | bytes 3063808 | tf_op jit(solution)/shard_map/all_gather | solution.py:67
  245.5 7.1 %copy-start.4 = (bf16[2,32,13,1024]{3,0,2,1:T(2,128)(2,1)S(1)}, bf16[2,32,13,1024]{3,0,2,1:T(2,128)(2,1)}, u32[]{:S(2)}) copy-start(bf16[2,32,13,1024]{3,0,2,1:T(2,128)(2,1)} %copy.38) | copy-start | bytes 5111812
  250.1 2.5 copy-start.1
  257.4 6.2 %copy-start.2 = (bf16[2,2,704,1024]{3,2,1,0:T(8,128)(2,1)S(1)}, bf16[2,2,704,1024]{3,2,1,0:T(8,128)(2,1)}, u32[]{:S(2)}) copy-start(bf16[2,2,704,1024]{3,2,1,0:T(8,128)(2,1)} %copy-done.1) | copy-start | bytes 17301508
  271.0 104.0 %all-to-all-start.3 = ((bf16[32,26,1024]{2,1,0:T(8,128)(2,1)}), bf16[32,26,1024]{2,1,0:T(8,128)(2,1)S(1)}, u32[]{:S(2)}, u32[]{:S(2)}) async-start(bf16[32,26,1024]{2,1,0:T(8,128)(2,1)} %copy.52), calls=%async_computation.3 | async-start | bytes 4194304 | tf_op jit(solution)/shard_map/all_to_all | solution.py:84
  286.4 95.2 %copy-start.6 = (bf16[128,1024]{1,0:T(8,128)(2,1)S(1)}, bf16[128,1024]{1,0:T(8,128)(2,1)}, u32[]{:S(2)}) copy-start(bf16[128,1024]{1,0:T(8,128)(2,1)} %param.11) | copy-start | bytes 786436
  375.0 1.3 copy-start
  376.3 104.4 %all-to-all-start.1 = ((bf16[32,26,1024]{2,1,0:T(8,128)(2,1)}), bf16[32,26,1024]{2,1,0:T(8,128)(2,1)}, u32[]{:S(2)}, u32[]{:S(2)}) async-start(bf16[32,26,1024]{2,1,0:T(8,128)(2,1)} %copy.44), calls=%async_computation.1 | async-start | bytes 4194304 | tf_op jit(solution)/shard_map/all_to_all | solution.py:77
  486.0 2.1 copy-start.3
Sparse Core Ops, SparseCore 0:
  11.0 79.4 all-gather.2
  148.1 62.8 all-gather.4
where the time goes:
time: 511 us; the launch traced here: 501 us
  waiting for transfers between devices  350 us (68%)
  local copies, waits for them, and re-layouts  64.7 us (13%)
  starting transfers between devices  32.9 us (6%)
  other arithmetic  20 us (4%)
  matrix products  19.1 us (4%)
  between operations  14.8 us (3%)
    all_to_all x1, waiting for transfers between devices, body(): lax.all_to_all(grad_buf, 'expert', split_axis=0, concat_axis=0, tiled=True)  92.3 us
    all_to_all x1, waiting for transfers between devices, body(): lax.all_to_all(grad_send.reshape(slot_total, model_width), 'expert', spli...  88.6 us
    all_to_all x1, waiting for transfers between devices, body(): lax.all_to_all(out_send.reshape(slot_total, model_width), 'expert', split...  87.5 us
    all_to_all x1, waiting for transfers between devices, body(): lax.all_to_all(x_buf, 'expert', split_axis=0, concat_axis=0, tiled=True)  79.7 us
    all_to_all x1, starting transfers between devices, body(): lax.all_to_all(x_buf, 'expert', split_axis=0, concat_axis=0, tiled=True)  16.9 us
  transfers between devices with their start and end apart: 6, of which 4 were waited for; matrix products, arithmetic and copies ran while one was open for 13% of the time, Pallas kernels for 0%

commit v1 on v0

v1 whole, which is shorter than its diff:
```python
import jax
import jax.numpy as jnp
from jax import lax
from jax.experimental import pallas as pl
from jax.experimental.pallas import tpu as pltpu
from jax.sharding import PartitionSpec as P

SLOTS = 16
VMEM = 56 * 1024 * 1024
NT = (((1,), (1,)), ((), ()))


def gather_kernel(rank_ref, rows_ref, x_ref, c_ref):
    tok = rank_ref.shape[2]
    model = rows_ref.shape[2]
    part = 8
    x = rows_ref[0, 0:tok, :]
    c = rows_ref[0, tok : 2 * tok, :]
    slot = lax.broadcasted_iota(jnp.int32, (part, SLOTS, tok), 1).astype(jnp.float32)

    def step(at, carry):
        first = pl.multiple_of(at * part, part)
        ranks = rank_ref[0, pl.ds(first, part), :]
        pick = jnp.where(ranks[:, None, :] == slot, 1.0, 0.0).astype(jnp.bfloat16)
        pick = pick.reshape(part * SLOTS, tok)
        xs = jnp.dot(pick, x, preferred_element_type=jnp.float32).astype(jnp.bfloat16)
        x_ref[pl.ds(first, part)] = xs.reshape(part, SLOTS, model)
        cs = jnp.dot(pick, c, preferred_element_type=jnp.float32).astype(jnp.bfloat16)
        c_ref[pl.ds(first, part)] = cs.reshape(part, SLOTS, model)
        return carry

    lax.fori_loop(0, x_ref.shape[0] // part, step, 0)


def combine(expert, group, rank_ref, slots_ref, total_ref, out_ref, rows):
    sources, tok = rank_ref.shape[0], rank_ref.shape[2]
    at = lax.rem(expert, group)
    model = rows.shape[1]
    slots_ref[:, pl.ds(pl.multiple_of(at * SLOTS, SLOTS), SLOTS), :] = rows.reshape(
        sources, SLOTS, model
    )
    slot = lax.broadcasted_iota(jnp.int32, (group, SLOTS, tok), 1).astype(jnp.float32)

    def sums(s, first):
        ranks = rank_ref[s, first : first + group, :]
        place = jnp.where(ranks[:, None, :] == slot, 1.0, 0.0).reshape(group * SLOTS, tok)
        place = jnp.transpose(place).astype(jnp.bfloat16)
        return jnp.dot(place, slots_ref[s], preferred_element_type=jnp.float32)

    @pl.when(expert == group - 1)
    def _():
        def one(s, carry):
            total_ref[s] = sums(s, 0)
            return carry

        lax.fori_loop(0, sources, one, 0)

    @pl.when(expert == 2 * group - 1)
    def _():
        def one(s, carry):
            out_ref[s] = (total_ref[s] + sums(s, group)).astype(out_ref.dtype)
            return carry

        lax.fori_loop(0, sources, one, 0)


def forward_kernel(w_ref, x_ref, c_ref, g_ref, rank_ref, out_ref, pair_ref, dot_ref, slots, total):
    expert = pl.program_id(0)
    hidden = w_ref.shape[1] // 3
    gate_up = w_ref[0, 0 : 2 * hidden, :]
    down = w_ref[0, 2 * hidden : 3 * hidden, :]
    pre = lax.dot_general(x_ref[0], gate_up, NT, preferred_element_type=jnp.float32)
    back = lax.dot_general(c_ref[0], down, NT, preferred_element_type=jnp.float32)
    gate = pre[:, 0:hidden]
    up = pre[:, hidden : 2 * hidden]
    sig = 1.0 / (1.0 + jnp.exp(-gate))
    act = gate * sig
    hid = act * up
    scale = jnp.transpose(g_ref[0])[:, 0:1]
    rows = jnp.dot(
        (hid * scale).astype(jnp.bfloat16), down, preferred_element_type=jnp.float32
    ).astype(jnp.bfloat16)
    prod = hid * back
    high = prod.astype(jnp.bfloat16)
    low = (prod - high.astype(jnp.float32)).astype(jnp.bfloat16)
    ones = jnp.ones((8, hidden), jnp.bfloat16)
    dot_ref[0] = lax.dot_general(ones, high, NT, preferred_element_type=jnp.float32) + (
        lax.dot_general(ones, low, NT, preferred_element_type=jnp.float32)
    )
    scaled = back * scale
    grad_up = scaled * act
    grad_gate = scaled * up * sig * (1.0 + gate * (1.0 - sig))
    pair_ref[0] = jnp.concatenate([grad_gate, grad_up], axis=1).astype(jnp.bfloat16)
    combine(expert, pl.num_programs(0) // 2, rank_ref, slots, total, out_ref, rows)


def backward_kernel(w_ref, pair_ref, rank_ref, out_ref, slots, total):
    expert = pl.program_id(0)
    rows = jnp.dot(pair_ref[0], w_ref[0], preferred_element_type=jnp.float32)
    combine(
        expert, pl.num_programs(0) // 2, rank_ref, slots, total, out_ref, rows.astype(jnp.bfloat16)
    )


def params():
    return pltpu.CompilerParams(dimension_semantics=("arbitrary",), vmem_limit_bytes=VMEM)


def gather_rows(ranks, rows):
    sources, half, tok = ranks.shape
    model = rows.shape[2]
    shape = jax.ShapeDtypeStruct((half, sources * SLOTS, model), jnp.bfloat16)
    block = pl.BlockSpec((half, SLOTS, model), lambda s: (0, s, 0))
    return pl.pallas_call(
        gather_kernel,
        grid=(sources,),
        in_specs=[
            pl.BlockSpec((1, half, tok), lambda s: (s, 0, 0)),
            pl.BlockSpec((1, rows.shape[1], model), lambda s: (s, 0, 0)),
        ],
        out_specs=[block, block],
        out_shape=[shape, shape],
        compiler_params=params(),
        cost_estimate=pl.CostEstimate(
            flops=4 * sources * half * SLOTS * tok * model,
            bytes_accessed=4 * half * sources * SLOTS * model + 2 * rows.size,
            transcendentals=0,
        ),
        name="gather_rows",
    )(ranks, rows)


def forward(weights, x_rows, c_rows, scales, ranks):
    half, w_rows, model = weights.shape
    hidden = w_rows // 3
    sources, _, tok = ranks.shape
    rows = sources * SLOTS
    each = lambda e: (e, 0, 0)
    whole = lambda e: (0, 0, 0)
    return pl.pallas_call(
        forward_kernel,
        grid=(half,),
        in_specs=[
            pl.BlockSpec((1, w_rows, model), each),
            pl.BlockSpec((1, rows, model), each),
            pl.BlockSpec((1, rows, model), each),
            pl.BlockSpec((1, 8, rows), each),
            pl.BlockSpec((sources, half, tok), whole),
        ],
        out_specs=[
            pl.BlockSpec((sources, tok, model), whole),
            pl.BlockSpec((1, rows, 2 * hidden), each),
            pl.BlockSpec((1, 8, rows), each),
        ],
        out_shape=[
            jax.ShapeDtypeStruct((sources, tok, model), jnp.bfloat16),
            jax.ShapeDtypeStruct((half, rows, 2 * hidden), jnp.bfloat16),
            jax.ShapeDtypeStruct((half, 8, rows), jnp.float32),
        ],
        scratch_shapes=[
            pltpu.VMEM((sources, half * SLOTS // 2, model), jnp.bfloat16),
            pltpu.VMEM((sources, tok, model), jnp.float32),
        ],
        compiler_params=params(),
        cost_estimate=pl.CostEstimate(
            flops=8 * half * rows * hidden * model,
            bytes_accessed=2 * (weights.size + x_rows.size + c_rows.size),
            transcendentals=half * rows * hidden,
        ),
        name="forward_experts",
    )(weights, x_rows, c_rows, scales, ranks)


def backward(weights, pairs, ranks):
    half, w_rows, model = weights.shape
    width = pairs.shape[2]
    sources, _, tok = ranks.shape
    rows = sources * SLOTS
    each = lambda e: (e, 0, 0)
    whole = lambda e: (0, 0, 0)
    return pl.pallas_call(
        backward_kernel,
        grid=(half,),
        in_specs=[
            pl.BlockSpec((1, width, model), each),
            pl.BlockSpec((1, rows, width), each),
            pl.BlockSpec((sources, half, tok), whole),
        ],
        out_specs=pl.BlockSpec((sources, tok, model), whole),
        out_shape=jax.ShapeDtypeStruct((sources, tok, model), jnp.bfloat16),
        scratch_shapes=[
            pltpu.VMEM((sources, half * SLOTS // 2, model), jnp.bfloat16),
            pltpu.VMEM((sources, tok, model), jnp.float32),
        ],
        compiler_params=params(),
        cost_estimate=pl.CostEstimate(
            flops=2 * half * rows * width * model,
            bytes_accessed=2 * (half * width * model + pairs.size),
            transcendentals=0,
        ),
        name="backward_experts",
    )(weights, pairs, ranks)


def body(tokens, expert_ids, router_gates, w_in, w_down, cotangent):
    tok, model = tokens.shape
    planes = lax.axis_size("dp")
    side = 4
    half = lax.axis_size("expert")
    experts = 2 * half
    parity = lax.rem(lax.axis_index("dp") // side, 2)

    def both_slices(which):
        pair = lax.dynamic_index_in_dim(w_in, which, 0, keepdims=False)
        down = lax.dynamic_slice_in_dim(w_down, which, 1, 0)
        return jnp.concatenate([pair, down], axis=0)

    swap = [(d, (((d // side) ^ 1) * side) + d % side) for d in range(planes)]
    other = lax.ppermute(both_slices(1 - parity), "dp", swap)
    mine = jnp.concatenate([both_slices(parity), other], axis=1).reshape(-1, model)
    weights = lax.all_gather(mine, "expert", axis=0, tiled=False)

    ids = expert_ids.T
    match = ids[:, None, :] == jnp.arange(experts, dtype=jnp.int32)[None, :, None]
    chosen = jnp.any(match, axis=0)
    gate_of = jnp.sum(jnp.where(match, router_gates.T[:, None, :], 0.0), axis=0)
    earlier = jnp.arange(tok)[:, None] < jnp.arange(tok)[None, :]
    rank = jnp.dot(
        chosen.astype(jnp.bfloat16), earlier.astype(jnp.bfloat16), preferred_element_type=jnp.float32
    )
    rank = jnp.where(chosen, rank, -1.0)
    slot_no = jnp.arange(SLOTS, dtype=jnp.float32)
    at_slot = rank[:, None, :] == slot_no[None, :, None]
    slot_gate = jnp.sum(jnp.where(at_slot, gate_of[:, None, :], 0.0), axis=2)
    gate_high = lax.reduce_precision(slot_gate, 8, 7)
    gate_low = slot_gate - gate_high

    def facts(odd):
        flat = lambda a: a.reshape(half, 2, -1)[:, odd].reshape(-1)
        return jnp.concatenate([flat(rank), flat(gate_high), flat(gate_low)]).astype(jnp.bfloat16)

    fact_rows = 16
    known = jnp.stack([facts(0), facts(1)])
    known = jnp.pad(known, ((0, 0), (0, fact_rows * model - known.shape[1])))
    known = known.reshape(2, 1, fact_rows, model)
    known = jnp.broadcast_to(known[:, None], (2, side, 1, fact_rows, model)).reshape(
        1, 2 * side, fact_rows, model
    )
    known = jnp.broadcast_to(known, (planes // (2 * side), 2 * side, fact_rows, model))
    known = known.reshape(planes, fact_rows, model)
    own = jnp.concatenate([tokens, cotangent], axis=0)
    sent = jnp.concatenate([jnp.broadcast_to(own[None], (planes, 2 * tok, model)), known], axis=1)
    rows = lax.all_to_all(sent, "dp", split_axis=0, concat_axis=0, tiled=True)

    facts_in = rows[:, 2 * tok :, :].reshape(planes, fact_rows * model).astype(jnp.float32)
    first, second = half * tok, half * tok + half * SLOTS
    ranks = facts_in[:, 0:first].reshape(planes, half, tok)
    scales = facts_in[:, first:second] + facts_in[:, second : second + half * SLOTS]
    scales = scales.reshape(planes, half, SLOTS).swapaxes(0, 1).reshape(half, 1, planes * SLOTS)
    scales = jnp.broadcast_to(scales, (half, 8, planes * SLOTS))

    x_rows, c_rows = gather_rows(ranks, rows)
    layer_part, pairs, dots = forward(weights, x_rows, c_rows, scales, ranks)
    layer_in = lax.all_to_all(layer_part, "dp", split_axis=0, concat_axis=0, tiled=True)
    grad_part = backward(weights, pairs, ranks)
    grad_in = lax.all_to_all(grad_part, "dp", split_axis=0, concat_axis=0, tiled=True)

    dots = dots[:, 0, :].reshape(half, planes, SLOTS).swapaxes(0, 1)
    even = jnp.where(parity == 0, dots, 0.0)
    odd = jnp.where(parity == 1, dots, 0.0)
    dots = jnp.stack([even, odd], axis=2).reshape(planes * 8, experts * SLOTS // 8)
    dots = lax.psum_scatter(dots, "dp", scatter_dimension=0, tiled=True)
    dots = dots.reshape(experts, SLOTS)
    by_expert = jnp.sum(jnp.where(at_slot, dots[:, :, None], 0.0), axis=1)
    gate_grads = jnp.sum(jnp.where(match, by_expert[None], 0.0), axis=1).T

    layer_output = jnp.sum(layer_in.astype(jnp.float32), axis=0).astype(jnp.bfloat16)
    token_grads = jnp.sum(grad_in.astype(jnp.float32), axis=0).astype(jnp.bfloat16)
    return (layer_output, token_grads, gate_grads)


def solution(mesh):
    both = P(("dp", "expert"), None)
    placed = (both, both, both, P("expert", None, "dp", None), P("expert", "dp", None), both)
    return jax.shard_map(
        body, mesh=mesh, in_specs=placed, out_specs=(both, both, both), check_vma=False
    )
```

time: 511 us -> 467 us (0.914); the launches traced: 501 us -> 464 us
  waiting for transfers between devices: 350 us -> 143 us
  blocking collectives: 0 us -> 161 us
  Pallas kernels: 0 us -> 108 us
  local copies, waits for them, and re-layouts: 64.7 us -> 15 us
  starting transfers between devices: 32.9 us -> 8.56 us
  matrix products: 19.1 us -> 0.14 us
  other arithmetic: 20 us -> 14.3 us
    all_to_all x4 -> x1, waiting for transfers between devices: 348 us -> 0.01 us  [body(): lax.all_to_all(layer_part, 'dp', split_axis=0, concat_axis=0, tiled=True)]
    all_to_all x0 -> x2, blocking collectives: none -> 161 us  [the longest x1 109 us: body(): rows = lax.all_to_all(sent, 'dp', split_axis=0, concat_axis=0, tiled=True)]
    unnamed x2 -> x3, waiting for transfers between devices: 1.38 us -> 139 us
    pallas_call x0 -> x3, Pallas kernels: none -> 108 us  [the longest x1 50.3 us: forward(): pl.pallas_call(forward_kernel, grid=(half,), in_specs=[pl.BlockSpec((1, w...]
    all_to_all x4 -> x1, starting transfers between devices: 32.8 us -> 4.53 us  [body(): lax.all_to_all(layer_part, 'dp', split_axis=0, concat_axis=0, tiled=True)]
    dot_general x4 -> x1, matrix products: 19.1 us -> 0.14 us  [body(): jnp.dot(chosen.astype(jnp.bfloat16), earlier.astype(jnp.bfloat16), prefer...]
    all_to_all x8 -> x0, local copies, waits for them, and re-layouts: 18.2 us -> none  [the longest x2 4.85 us: body(): lax.all_to_all(out_send.reshape(slot_total, model_width), 'expert', split...]
    scatter x1 -> x0, other arithmetic: 9.49 us -> none  [body(): jnp.zeros((slot_total, model_width), jnp.bfloat16).at[slot_index]]
  transfers between devices with their start and end apart: 6 -> 4, of which waited for: 4 -> 2; matrix products, arithmetic and copies ran while one was open for 13% -> 4% of each run, Pallas kernels for 0% -> 5%
where the time goes in v1:
time: 467 us; the launch traced here: 464 us
  blocking collectives  161 us (34%)
  waiting for transfers between devices  143 us (31%)
  Pallas kernels  108 us (23%)
  local copies, waits for them, and re-layouts  15 us (3%)
  between operations  14.9 us (3%)
  other arithmetic  14.3 us (3%)
  starting transfers between devices  8.56 us (2%)
    unnamed x3, waiting for transfers between devices  139 us
    all_to_all x1, blocking collectives, body(): rows = lax.all_to_all(sent, 'dp', split_axis=0, concat_axis=0, tiled=True)  109 us
    all_to_all x1, blocking collectives, body(): lax.all_to_all(grad_part, 'dp', split_axis=0, concat_axis=0, tiled=True)  51.7 us
    pallas_call x1, Pallas kernels, forward(): pl.pallas_call(forward_kernel, grid=(half,), in_specs=[pl.BlockSpec((1, w...  50.3 us
    pallas_call x1, Pallas kernels, backward(): pl.pallas_call(backward_kernel, grid=(half,), in_specs=[pl.BlockSpec((1,...  32.9 us
    pallas_call x1, Pallas kernels, gather_rows(): pl.pallas_call(gather_kernel, grid=(sources,), in_specs=[pl.BlockSpec((1,...  24.3 us
  transfers between devices with their start and end apart: 4, of which 2 were waited for; matrix products, arithmetic and copies ran while one was open for 4% of the time, Pallas kernels for 5%

profile of v1, /device:TPU:1, one launch (start us, length us, event | category | flops | bytes accessed | tf_op | source)
XLA Modules:
  0.0 464.5 jit_solution(13913200251680798642)
XLA Ops:
  7.2 0.0 all-gather.2.cloned.1.call-start
  7.2 1.3 dynamic-slice_bitcast_fusion.1
  8.5 1.4 constant_dynamic-slice_fusion.1
  9.9 0.4 pad_maximum_fusion.3
  10.3 3.9 collective-permute-start
  14.2 4.8 %collective-permute-done = bf16[3,44,1024]{2,0,1:T(4,128)(2,1)S(1)} collective-permute-done((bf16[3,44,1024]{2,0,1:T(4,128)(2,1)S(1)}, bf16[3,44,1024]{2,0,1:T(4,128)(2,1)S(1)}, u32[]{:S(2)}, u32[]{:S(2)}) %collective-permute-start) | collective-permute-done | bytes 270368 | tf_op jit(solution)/shard_map/ppermute | solution.py:219
  19.0 0.5 pad_maximum_fusion.1
  19.6 1.0 copy.29
  20.6 0.0 all-gather.2.cloned.1.call-update
  20.6 0.7 fusion
  21.3 0.7 select_reduce_fusion.3
  22.1 0.1 fusion.13
  22.2 0.2 select_reduce_fusion.1
  22.5 0.2 slice_reduce_fusion.2
  22.7 0.1 concatenate.54
  22.8 0.1 concatenate.55
  22.8 0.1 concatenate.58
  22.9 0.1 concatenate.59
  23.1 0.1 fusion.11
  23.2 1.1 pad_maximum_fusion.2
  24.3 0.1 broadcast_in_dim.100
  24.3 1.1 broadcast_in_dim.91
  25.4 0.8 pad_maximum_fusion
  26.2 108.9 %all_to_all.15.rows_ref = bf16[16,272,1024]{2,1,0:T(8,128)(2,1)S(1)} all-to-all(bf16[16,272,1024]{2,1,0:T(8,128)(2,1)S(1)} %pad_maximum_fusion), channel_id=1, replica_groups=mesh['dp'=16,'expert'=32] {'dp'}, dimensions={0} | all-to-all | bytes 17825792 | tf_op jit(solution)/shard_map/all_to_all | solution.py:253
  135.1 0.0 copy-start
  135.1 3.4 copy-done
  138.6 0.1 slice_convert_fusion
  138.7 0.6 copy.36
  139.3 0.8 copy.37
  140.1 0.1 reshape.152
  140.2 0.1 copy.30
  140.3 0.1 copy.31
  140.4 24.3 %gather_rows.1 = (bf16[32,256,1024]{2,1,0:T(8,128)(2,1)}, bf16[32,256,1024]{2,1,0:T(8,128)(2,1)}) custom-call(f32[16,32,128]{2,1,0:T(8,128)} %bitcast.40, bf16[16,272,1024]{2,1,0:T(8,128)(2,1)} %copy-done), custom_call_target="tpu_custom_call" | custom-call | flops 4294967296 | bytes 42467328 | tf_op jit(solution)/shard_map/gather_rows/pallas_call | solution.py:114
  164.7 0.0 all-gather.2.cloned.1.call-done.w_ref
  164.7 0.7 broadcast_in_dim.102.g_ref
  165.5 50.3 %forward_experts.1 = (bf16[16,128,1024]{2,1,0:T(8,128)(2,1)}, bf16[32,256,176]{2,1,0:T(8,128)(2,1)}, f32[32,8,256]{2,1,0:T(8,128)}) custom-call(bf16[32,264,1024]{2,1,0:T(8,128)(2,1)} %all-gather.2.cloned.1.call-done.w_ref, bf16[32,256,1024]{2,1,0:T(8,128)(2,1)} %get-tuple-element.8.x_ref, bf16[32,256,1024]{2,1,0:T(8,128)(2,1)} %get-tuple-element.9.c_ref, ...), custom_call_target="tpu_custom_call" | custom-call | flops 5905580032 | bytes 50855936 | tf_op jit(solution)/shard_map/forward_experts/pallas_call | solution.py:140
  215.8 32.9 %backward_experts.1 = bf16[16,128,1024]{2,1,0:T(8,128)(2,1)} custom-call(bf16[32,264,1024]{2,1,0:T(8,128)(2,1)} %all-gather.2.cloned.1.call-done.w_ref, bf16[32,256,176]{2,1,0:T(8,128)(2,1)} %get-tuple-element.11.pair_ref, f32[16,32,128]{2,1,0:T(8,128)} %bitcast.42), custom_call_target="tpu_custom_call" | custom-call | flops 2952790016 | bytes 14417920 | tf_op jit(solution)/shard_map/backward_experts/pallas_call | solution.py:181
  248.7 0.0 copy-start.1
  248.7 51.7 %all_to_all.16 = bf16[16,128,1024]{2,1,0:T(8,128)(2,1)} all-to-all(bf16[16,128,1024]{2,1,0:T(8,128)(2,1)} %backward_experts.1), channel_id=1, replica_groups=mesh['dp'=16,'expert'=32] {'dp'}, dimensions={0} | all-to-all | bytes 8388608 | tf_op jit(solution)/shard_map/all_to_all | solution.py:266
  300.4 4.5 all-to-all-start.1
  304.9 0.0 all-reduce.4.cloned.1.call-start
  305.0 1.0 broadcast_select_fusion.1
  306.0 0.1 copy.32
  306.1 0.1 copy.33
  306.2 0.3 copy.34
  306.5 1.3 reshape.153
  307.8 0.0 all-reduce.4.cloned.1.call-update
  307.8 1.3 dynamic-slice
  309.7 138.5 %all-reduce.4.cloned.1.call-done = f32[128,128]{1,0:T(8,128)} async-done(((f32[128,128]{1,0:T(8,128)}), f32[128,128]{1,0:T(8,128)}) %all-reduce.4.cloned.1.call-update) | async-done | bytes 65552
  448.3 0.7 constant_dynamic-slice_fusion.2
  448.9 0.1 broadcast_in_dim.104
  449.0 0.2 select_reduce_fusion
  449.2 0.0 copy-done.1
  449.3 0.6 select_reduce_fusion.2
  449.9 3.9 reduce_sum.66
  453.8 0.0 all-to-all-done.1
  453.8 3.9 reduce_sum.65
  (7 shorter events, 0.1 us)
Async XLA Ops:
  7.2 157.6 %all-gather.2.cloned.1.call-start = ((), (), s32[]{:S(2)}) async-start(), calls=%async_computation.3 | async-start | bytes 17842176 | tf_op jit(solution)/shard_map/all_gather | solution.py:221
  10.3 8.8 %collective-permute-start = (bf16[3,44,1024]{2,0,1:T(4,128)(2,1)S(1)}, bf16[3,44,1024]{2,0,1:T(4,128)(2,1)S(1)}, u32[]{:S(2)}, u32[]{:S(2)}) collective-permute-start(bf16[3,44,1024]{2,0,1:T(4,128)(2,1)S(1)} %pad_maximum_fusion.3), channel_id=1, source_target_pairs={{0,128},{32,160},{64,192},{96,224},{128,0},{160,32},{192,64},{224,... | collective-permute-start | bytes 811016 | tf_op jit(solution)/shard_map/ppermute | solution.py:219
  135.1 3.4 copy-start
  248.7 200.6 %copy-start.1 = (s32[128,6]{0,1:T(8,128)S(1)}, s32[128,6]{0,1:T(8,128)}, u32[]{:S(2)}) copy-start(s32[128,6]{0,1:T(8,128)} %param.7) | copy-start | bytes 9220
  300.4 153.4 %all-to-all-start.1 = ((bf16[16,128,1024]{2,1,0:T(8,128)(2,1)}), bf16[16,128,1024]{2,1,0:T(8,128)(2,1)}, u32[]{:S(2)}, u32[]{:S(2)}) async-start(bf16[16,128,1024]{2,1,0:T(8,128)(2,1)} %get-tuple-element.10), calls=%async_computation.1 | async-start | bytes 8388608 | tf_op jit(solution)/shard_map/all_to_all | solution.py:264
  304.9 143.3 %all-reduce.4.cloned.1.call-start = ((), (), s32[]{:S(2)}) async-start(), calls=%async_computation.4 | async-start | bytes 131072
Sparse Core Ops, SparseCore 0:
  20.7 118.4 all-gather.1
  309.5 138.6 all-reduce.3

commit v2 on v1

v2 whole, which is shorter than its diff:
```python
import jax
import jax.numpy as jnp
from jax import lax
from jax.experimental import pallas as pl
from jax.experimental.pallas import tpu as pltpu
from jax.sharding import PartitionSpec as P

STEP = 4
SLOTS = 16
VMEM = 56 * 1024 * 1024
NT = (((1,), (1,)), ((), ()))
TN = (((0,), (0,)), ((), ()))


def one_hot(ranks, slot):
    group, tok = ranks.shape
    hit = jnp.where(ranks[:, None, :] == slot, 1.0, 0.0)
    return hit.reshape(group * SLOTS, tok).astype(jnp.bfloat16)


def slot_numbers(group, tok):
    return lax.broadcasted_iota(jnp.int32, (group, SLOTS, tok), 1).astype(jnp.float32)


def gather_kernel(rank_ref, rows_ref, x_ref):
    half, tok = rank_ref.shape[1:]
    pick = one_hot(rank_ref[0], slot_numbers(half, tok))
    xs = jnp.dot(pick, rows_ref[0, 0:tok, :], preferred_element_type=jnp.float32)
    x_ref[...] = xs.astype(jnp.bfloat16).reshape(x_ref.shape)


def keep(expert, group, slots_ref, rows):
    at = lax.rem(expert, group)
    slots_ref[:, pl.ds(pl.multiple_of(at * SLOTS, SLOTS), SLOTS), :] = rows.reshape(
        slots_ref.shape[0], SLOTS, rows.shape[1]
    )


def combine(expert, group, rank_ref, slots_ref, total_ref, out_ref):
    sources, tok = rank_ref.shape[0], rank_ref.shape[2]
    slot = slot_numbers(group, tok)

    def sums(s, first):
        place = one_hot(rank_ref[s, first : first + group, :], slot)
        return lax.dot_general(place, slots_ref[s], TN, preferred_element_type=jnp.float32)

    @pl.when(expert == group - 1)
    def _():
        def one(s, carry):
            total_ref[s] = sums(s, 0)
            return carry

        lax.fori_loop(0, sources, one, 0)

    @pl.when(expert == 2 * group - 1)
    def _():
        def one(s, carry):
            out_ref[s, 0:tok, :] = (total_ref[s] + sums(s, group)).astype(out_ref.dtype)
            return carry

        lax.fori_loop(0, sources, one, 0)


def swish(pre, hidden):
    gate = pre[:, 0:hidden]
    up = pre[:, hidden : 2 * hidden]
    sig = 1.0 / (1.0 + jnp.exp(-gate))
    return gate, up, sig


def forward_kernel(w_ref, x_ref, g_ref, rank_ref, out_ref, pre_ref, slots, total):
    hidden = w_ref.shape[1] // 3
    group = STEP * pl.num_programs(0) // 2
    first = pl.program_id(0) * STEP
    for i in range(STEP):
        gate_up = w_ref[i, 0 : 2 * hidden, :]
        down = w_ref[i, 2 * hidden : 3 * hidden, :]
        pre = lax.dot_general(x_ref[i], gate_up, NT, preferred_element_type=jnp.float32)
        pre_ref[i] = pre
        gate, up, sig = swish(pre, hidden)
        scale = jnp.transpose(g_ref[i])[:, 0:1]
        scaled = (gate * sig * up * scale).astype(jnp.bfloat16)
        rows = jnp.dot(scaled, down, preferred_element_type=jnp.float32)
        keep(first + i, group, slots, rows.astype(jnp.bfloat16))
    combine(first + STEP - 1, group, rank_ref, slots, total, out_ref)


def backward_kernel(w_ref, pre_ref, g_ref, rank_ref, c_ref, out_ref, slots, total, dots):
    hidden = w_ref.shape[1] // 3
    half = STEP * pl.num_programs(0)
    group = half // 2
    first = pl.program_id(0) * STEP
    sources, tok, model = c_ref.shape

    @pl.when(lax.rem(first, group) == 0)
    def _():
        slot = slot_numbers(group, tok)

        def one(s, carry):
            ranks = rank_ref[s, pl.ds(pl.multiple_of(first, group), group), :]
            cs = jnp.dot(one_hot(ranks, slot), c_ref[s], preferred_element_type=jnp.float32)
            slots[s] = cs.astype(jnp.bfloat16)
            return carry

        lax.fori_loop(0, sources, one, 0)

    @pl.when(first == 0)
    def _():
        dots[...] = jnp.zeros_like(dots)

    lane = lax.broadcasted_iota(jnp.int32, dots.shape, 1)
    for i in range(STEP):
        gate_up = w_ref[i, 0 : 2 * hidden, :]
        down = w_ref[i, 2 * hidden : 3 * hidden, :]
        at = pl.multiple_of(lax.rem(first + i, group) * SLOTS, SLOTS)
        cs = slots[:, pl.ds(at, SLOTS), :].reshape(sources * SLOTS, model)
        back = lax.dot_general(cs, down, NT, preferred_element_type=jnp.float32)
        gate, up, sig = swish(pre_ref[i], hidden)
        act = gate * sig
        dot = jnp.sum(act * up * back, axis=1, keepdims=True)
        dots[...] = jnp.where(lane == first + i, dot, dots[...])
        scaled = back * jnp.transpose(g_ref[i])[:, 0:1]
        grad_up = scaled * act
        grad_gate = scaled * up * sig * (1.0 + gate * (1.0 - sig))
        pair = jnp.concatenate([grad_gate, grad_up], axis=1).astype(jnp.bfloat16)
        rows = jnp.dot(pair, gate_up, preferred_element_type=jnp.float32)
        keep(first + i, group, slots, rows.astype(jnp.bfloat16))
    combine(first + STEP - 1, group, rank_ref, slots, total, out_ref)

    @pl.when(first + STEP == half)
    def _():
        low_rows = SLOTS // 2

        def one(s, carry):
            part = dots[pl.ds(pl.multiple_of(s * SLOTS, SLOTS), SLOTS), 0:half]
            high = part.astype(jnp.bfloat16).astype(jnp.float32)
            low = part - high
            blank = jnp.zeros((low_rows, model - 4 * half), jnp.float32)
            line = [high[0:low_rows], low[0:low_rows], high[low_rows:], low[low_rows:], blank]
            out_ref[s, tok : tok + low_rows, :] = jnp.concatenate(line, axis=1).astype(jnp.bfloat16)
            return carry

        lax.fori_loop(0, sources, one, 0)


def params():
    return pltpu.CompilerParams(dimension_semantics=("arbitrary",), vmem_limit_bytes=VMEM)


def each(e):
    return (e, 0, 0)


def whole(e):
    return (0, 0, 0)


def gather_rows(ranks, rows):
    sources, half, tok = ranks.shape
    model = rows.shape[2]
    return pl.pallas_call(
        gather_kernel,
        grid=(sources,),
        in_specs=[
            pl.BlockSpec((1, half, tok), each),
            pl.BlockSpec((1, rows.shape[1], model), each),
        ],
        out_specs=pl.BlockSpec((half, SLOTS, model), lambda s: (0, s, 0)),
        out_shape=jax.ShapeDtypeStruct((half, sources * SLOTS, model), jnp.bfloat16),
        compiler_params=params(),
        cost_estimate=pl.CostEstimate(
            flops=2 * sources * half * SLOTS * tok * model,
            bytes_accessed=2 * half * sources * SLOTS * model + 2 * rows.size,
            transcendentals=0,
        ),
        name="gather_rows",
    )(ranks, rows)


def forward(weights, x_rows, scales, ranks):
    half, w_rows, model = weights.shape
    hidden = w_rows // 3
    sources, _, tok = ranks.shape
    rows = sources * SLOTS
    return pl.pallas_call(
        forward_kernel,
        grid=(half // STEP,),
        in_specs=[
            pl.BlockSpec((STEP, w_rows, model), each),
            pl.BlockSpec((STEP, rows, model), each),
            pl.BlockSpec((STEP, 8, rows), each),
            pl.BlockSpec((sources, half, tok), whole),
        ],
        out_specs=[
            pl.BlockSpec((sources, tok, model), whole),
            pl.BlockSpec((STEP, rows, 2 * hidden), each),
        ],
        out_shape=[
            jax.ShapeDtypeStruct((sources, tok, model), jnp.bfloat16),
            jax.ShapeDtypeStruct((half, rows, 2 * hidden), jnp.float32),
        ],
        scratch_shapes=[
            pltpu.VMEM((sources, half * SLOTS // 2, model), jnp.bfloat16),
            pltpu.VMEM((sources, tok, model), jnp.float32),
        ],
        compiler_params=params(),
        cost_estimate=pl.CostEstimate(
            flops=6 * half * rows * hidden * model,
            bytes_accessed=2 * (weights.size + x_rows.size),
            transcendentals=half * rows * hidden,
        ),
        name="forward_experts",
    )(weights, x_rows, scales, ranks)


def backward(weights, pre, scales, ranks, cotangents):
    half, w_rows, model = weights.shape
    sources, _, tok = ranks.shape
    rows = sources * SLOTS
    out_rows = tok + SLOTS // 2
    return pl.pallas_call(
        backward_kernel,
        grid=(half // STEP,),
        in_specs=[
            pl.BlockSpec((STEP, w_rows, model), each),
            pl.BlockSpec((STEP, rows, pre.shape[2]), each),
            pl.BlockSpec((STEP, 8, rows), each),
            pl.BlockSpec((sources, half, tok), whole),
            pl.BlockSpec((sources, tok, model), whole),
        ],
        out_specs=pl.BlockSpec((sources, out_rows, model), whole),
        out_shape=jax.ShapeDtypeStruct((sources, out_rows, model), jnp.bfloat16),
        scratch_shapes=[
            pltpu.VMEM((sources, half * SLOTS // 2, model), jnp.bfloat16),
            pltpu.VMEM((sources, tok, model), jnp.float32),
            pltpu.VMEM((rows, 128), jnp.float32),
        ],
        compiler_params=params(),
        cost_estimate=pl.CostEstimate(
            flops=6 * half * rows * (w_rows // 3) * model,
            bytes_accessed=2 * (weights.size + 2 * pre.size),
            transcendentals=half * rows * (w_rows // 3),
        ),
        name="backward_experts",
    )(weights, pre, scales, ranks, cotangents)


def body(tokens, expert_ids, router_gates, w_in, w_down, cotangent):
    tok, model = tokens.shape
    planes = lax.axis_size("dp")
    side = 4
    half = lax.axis_size("expert")
    experts = 2 * half
    parity = lax.rem(lax.axis_index("dp") // side, 2)

    def both_slices(which):
        pair = lax.dynamic_index_in_dim(w_in, which, 0, keepdims=False)
        down = lax.dynamic_slice_in_dim(w_down, which, 1, 0)
        return jnp.concatenate([pair, down], axis=0)

    swap = [(d, (((d // side) ^ 1) * side) + d % side) for d in range(planes)]
    other = lax.ppermute(both_slices(1 - parity), "dp", swap)
    mine = jnp.concatenate([both_slices(parity), other], axis=1).reshape(-1, model)
    weights = lax.all_gather(mine, "expert", axis=0, tiled=False)

    ids = expert_ids.T
    match = ids[:, None, :] == jnp.arange(experts, dtype=jnp.int32)[None, :, None]
    chosen = jnp.any(match, axis=0)
    gate_of = jnp.sum(jnp.where(match, router_gates.T[:, None, :], 0.0), axis=0)
    earlier = jnp.arange(tok)[:, None] < jnp.arange(tok)[None, :]
    rank = jnp.dot(
        chosen.astype(jnp.bfloat16), earlier.astype(jnp.bfloat16), preferred_element_type=jnp.float32
    )
    rank = jnp.where(chosen, rank, -1.0)
    slot_no = jnp.arange(SLOTS, dtype=jnp.float32)
    at_slot = rank[:, None, :] == slot_no[None, :, None]
    slot_gate = jnp.sum(jnp.where(at_slot, gate_of[:, None, :], 0.0), axis=2)
    gate_high = lax.reduce_precision(slot_gate, 8, 7)
    gate_low = slot_gate - gate_high

    def facts(odd):
        flat = lambda a: a.reshape(half, 2, -1)[:, odd].reshape(-1)
        return jnp.concatenate([flat(rank), flat(gate_high), flat(gate_low)]).astype(jnp.bfloat16)

    fact_rows = 8
    known = jnp.stack([facts(0), facts(1)])
    known = jnp.pad(known, ((0, 0), (0, fact_rows * model - known.shape[1])))
    known = known.reshape(2, 1, fact_rows, model)
    known = jnp.broadcast_to(known[:, None], (2, side, 1, fact_rows, model)).reshape(
        1, 2 * side, fact_rows, model
    )
    known = jnp.broadcast_to(known, (planes // (2 * side), 2 * side, fact_rows, model))
    known = known.reshape(planes, fact_rows, model)
    spread = lambda a: jnp.broadcast_to(a[None], (planes, tok, model))
    swap_rows = lambda a: lax.all_to_all(a, "dp", split_axis=0, concat_axis=0, tiled=True)
    rows = swap_rows(jnp.concatenate([spread(tokens), known], axis=1))
    cotangents = swap_rows(spread(cotangent))

    facts_in = rows[:, tok:, :].reshape(planes, fact_rows * model).astype(jnp.float32)
    first, second = half * tok, half * tok + half * SLOTS
    ranks = facts_in[:, 0:first].reshape(planes, half, tok)
    scales = facts_in[:, first:second] + facts_in[:, second : second + half * SLOTS]
    scales = scales.reshape(planes, half, SLOTS).swapaxes(0, 1).reshape(half, 1, planes * SLOTS)
    scales = jnp.broadcast_to(scales, (half, 8, planes * SLOTS))

    x_rows = gather_rows(ranks, rows)
    layer_part, pre = forward(weights, x_rows, scales, ranks)
    layer_output = lax.psum_scatter(
        layer_part.reshape(planes * tok, model), "dp", scatter_dimension=0, tiled=True
    )
    grad_in = swap_rows(backward(weights, pre, scales, ranks, cotangents)).astype(jnp.float32)
    token_grads = jnp.sum(grad_in[:, 0:tok], axis=0).astype(jnp.bfloat16)

    dots = grad_in[:, tok:, 0 : 4 * half].reshape(2, 2, side, SLOTS // 2, 2, 2, half)
    dots = jnp.sum(dots, axis=(0, 2, 5))
    dots = dots.transpose(3, 0, 2, 1).reshape(experts, SLOTS)
    by_expert = jnp.sum(jnp.where(at_slot, dots[:, :, None], 0.0), axis=1)
    gate_grads = jnp.sum(jnp.where(match, by_expert[None], 0.0), axis=1).T
    return (layer_output, token_grads, gate_grads)


def solution(mesh):
    both = P(("dp", "expert"), None)
    placed = (both, both, both, P("expert", None, "dp", None), P("expert", "dp", None), both)
    return jax.shard_map(
        body, mesh=mesh, in_specs=placed, out_specs=(both, both, both), check_vma=False
    )
```

time: 467 us -> 304 us (0.65)
  waiting for transfers between devices: 143 us -> 35.1 us
  blocking collectives: 161 us -> 125 us
  Pallas kernels: 108 us -> 99.6 us
  other arithmetic: 14.3 us -> 8.82 us
    unnamed x3 -> x2, waiting for transfers between devices: 139 us -> 0.03 us
    all_to_all x2, blocking collectives: 161 us -> 125 us  [body(): lax.all_to_all(a, 'dp', split_axis=0, concat_axis=0, tiled=True)]
    all_gather x1, waiting for transfers between devices: 0.01 us -> 30.3 us  [body(): weights = lax.all_gather(mine, 'expert', axis=0, tiled=False)]
    pallas_call x1, Pallas kernels: 24.3 us -> 15.1 us  [gather_rows(): pl.pallas_call(gather_kernel, grid=(sources,), in_specs=[pl.BlockSpec((1,...]
    reduce_sum x2, other arithmetic: 7.76 us -> 1.68 us  [the longest x1 1.53 us: body(): token_grads = jnp.sum(grad_in[:, 0:tok], axis=0).astype(jnp.bfloat16)]
  transfers between devices with their start and end apart: 4 -> 4, of which waited for: 2 -> 2; matrix products, arithmetic and copies ran while one was open for 4% -> 5% of each run, Pallas kernels for 5% -> 33%
where the time goes in v2:
time: 304 us; the launch traced here: 303 us
  blocking collectives  125 us (41%)
  Pallas kernels  99.6 us (33%)
  waiting for transfers between devices  35.1 us (12%)
  between operations  14.3 us (5%)
  local copies, waits for them, and re-layouts  12.1 us (4%)
  other arithmetic  8.82 us (3%)
  starting transfers between devices  8.58 us (3%)
    all_to_all x2, blocking collectives, body(): lax.all_to_all(a, 'dp', split_axis=0, concat_axis=0, tiled=True)  125 us
    pallas_call x1, Pallas kernels, backward(): pl.pallas_call(backward_kernel, grid=(half // STEP,), in_specs=[pl.BlockS...  51.2 us
    pallas_call x1, Pallas kernels, forward(): pl.pallas_call(forward_kernel, grid=(half // STEP,), in_specs=[pl.BlockSp...  33.3 us
    all_gather x1, waiting for transfers between devices, body(): weights = lax.all_gather(mine, 'expert', axis=0, tiled=False)  30.3 us
    pallas_call x1, Pallas kernels, gather_rows(): pl.pallas_call(gather_kernel, grid=(sources,), in_specs=[pl.BlockSpec((1,...  15.1 us
  transfers between devices with their start and end apart: 4, of which 2 were waited for; matrix products, arithmetic and copies ran while one was open for 5% of the time, Pallas kernels for 33%

profile of v2, /device:TPU:1, one launch (start us, length us, event | category | flops | bytes accessed | tf_op | source)
XLA Modules:
  0.0 303.2 jit_solution(11331316240444778353)
XLA Ops:
  7.2 0.0 copy-start.3
  7.2 0.0 copy-start.4
  7.2 0.0 copy-start.1
  7.2 0.0 all-gather.2.cloned.1.call-start
  7.3 1.3 dynamic-slice_bitcast_fusion.1
  8.6 1.4 constant_dynamic-slice_fusion.1
  10.0 0.4 pad_maximum_fusion.2
  10.3 3.9 %collective-permute-start = (bf16[3,44,1024]{2,0,1:T(4,128)(2,1)S(1)}, bf16[3,44,1024]{2,0,1:T(4,128)(2,1)S(1)}, u32[]{:S(2)}, u32[]{:S(2)}) collective-permute-start(bf16[3,44,1024]{2,0,1:T(4,128)(2,1)S(1)} %pad_maximum_fusion.2), channel_id=1, source_target_pairs={{0,128},{32,160},{64,192},{96,224},{128,0},{160,32},{192,64},{224,... | collective-permute-start | bytes 811016 | tf_op jit(solution)/shard_map/ppermute | solution.py:262
  14.3 4.8 %collective-permute-done = bf16[3,44,1024]{2,0,1:T(4,128)(2,1)S(1)} collective-permute-done((bf16[3,44,1024]{2,0,1:T(4,128)(2,1)S(1)}, bf16[3,44,1024]{2,0,1:T(4,128)(2,1)S(1)}, u32[]{:S(2)}, u32[]{:S(2)}) %collective-permute-start) | collective-permute-done | bytes 270368 | tf_op jit(solution)/shard_map/ppermute | solution.py:262
  19.1 0.5 pad_maximum_fusion.1
  19.6 1.0 copy.22
  20.7 0.0 all-gather.2.cloned.1.call-update
  20.7 0.0 copy-done.3
  20.7 0.0 copy-done.4
  20.8 0.1 fusion.13
  20.9 0.2 select_reduce_fusion.1
  21.2 0.2 slice_reduce_fusion.3
  21.4 0.1 concatenate.50
  21.5 0.1 concatenate.51
  21.6 0.1 concatenate.54
  21.6 0.1 concatenate.55
  21.8 0.1 fusion.12
  21.9 0.0 copy-done.1
  21.9 0.5 broadcast_in_dim.92
  22.4 0.7 pad_maximum_fusion
  23.2 0.0 copy-start.2
  23.2 61.1 %all_to_all.15.rows_ref = bf16[16,136,1024]{2,1,0:T(8,128)(2,1)} all-to-all(bf16[16,136,1024]{2,1,0:T(8,128)(2,1)S(1)} %pad_maximum_fusion), channel_id=1, replica_groups=mesh['dp'=16,'expert'=32] {'dp'}, dimensions={0} | all-to-all | bytes 8912896 | tf_op jit(solution)/shard_map/all_to_all | solution.py:295
  84.3 0.0 copy-done.2
  84.3 2.6 broadcast_in_dim.104
  86.9 4.6 %all-to-all-start.1 = ((bf16[16,128,1024]{2,1,0:T(8,128)(2,1)}), bf16[16,128,1024]{2,1,0:T(8,128)(2,1)}, u32[]{:S(2)}, u32[]{:S(2)}) async-start(bf16[16,128,1024]{2,1,0:T(8,128)(2,1)} %broadcast_in_dim.104), calls=%async_computation.2 | async-start | bytes 8388608 | tf_op jit(solution)/shard_map/all_to_all | solution.py:295
  91.4 0.0 reduce-scatter.2.cloned.1.call-start
  91.5 1.0 slice_convert_fusion
  92.5 0.3 copy.27
  92.8 0.8 copy.28
  93.6 0.1 reshape.150
  93.7 0.1 copy.23
  93.8 0.1 copy.24
  93.9 15.1 %gather_rows.1.x_ref = bf16[32,256,1024]{2,1,0:T(8,128)(2,1)} custom-call(f32[16,32,128]{2,1,0:T(8,128)} %bitcast.30, bf16[16,136,1024]{2,1,0:T(8,128)(2,1)} %all_to_all.15.rows_ref), custom_call_target="tpu_custom_call" | custom-call | flops 2147483648 | bytes 21233664 | tf_op jit(solution)/shard_map/gather_rows/pallas_call | solution.py:161
  109.0 30.3 %all-gather.2.cloned.1.call-done.w_ref = bf16[32,264,1024]{2,1,0:T(8,128)(2,1)} async-done(((bf16[1,264,1024]{2,1,0:T(8,128)(2,1)}), bf16[32,264,1024]{2,1,0:T(8,128)(2,1)}) %all-gather.2.cloned.1.call-update) | async-done | bytes 17301520 | tf_op jit(solution)/shard_map/all_gather | solution.py:264
  139.3 0.7 broadcast_in_dim.103.g_ref
  140.0 33.3 %forward_experts.1 = (bf16[16,128,1024]{2,1,0:T(8,128)(2,1)}, f32[32,256,176]{2,1,0:T(8,128)}) custom-call(bf16[32,264,1024]{2,1,0:T(8,128)(2,1)} %all-gather.2.cloned.1.call-done.w_ref, bf16[32,256,1024]{2,1,0:T(8,128)(2,1)} %gather_rows.1.x_ref, f32[32,8,256]{2,1,0:T(8,128)} %broadcast_in_dim.103.g_ref, f32[16,32,128]{2,1,0:T(8,128)} %bitcast.31), custom_call_target="tpu_custom_call" | custom-call | flops 4429185024 | bytes 34078720 | tf_op jit(solution)/shard_map/forward_experts/pallas_call | solution.py:185
  173.3 0.0 reduce-scatter.2.cloned.1.call-update
  173.3 0.0 all-to-all-done.1.c_ref
  173.3 51.2 %backward_experts.1 = bf16[16,136,1024]{2,1,0:T(8,128)(2,1)} custom-call(bf16[32,264,1024]{2,1,0:T(8,128)(2,1)} %all-gather.2.cloned.1.call-done.w_ref, f32[32,256,176]{2,1,0:T(8,128)} %get-tuple-element.6.pre_ref, f32[32,8,256]{2,1,0:T(8,128)} %broadcast_in_dim.103.g_ref, f32[16,32,128]{2,1,0:T(8,128)} %bitcast.32, bf16[16,128,1024]{2,1,0:T(8,128)(2,1)} %all-to-all-done.1.c_ref), custom_call_target="tpu_custom_call" | custom-call | flops 4429185024 | bytes 23068672 | tf_op jit(solution)/shard_map/backward_experts/pallas_call | solution.py:221
  224.5 63.5 %all_to_all.16 = bf16[16,136,1024]{2,1,0:T(8,128)(2,1)S(1)} all-to-all(bf16[16,136,1024]{2,1,0:T(8,128)(2,1)} %backward_experts.1), channel_id=1, replica_groups=mesh['dp'=16,'expert'=32] {'dp'}, dimensions={0} | all-to-all | bytes 8912896 | tf_op jit(solution)/shard_map/all_to_all | solution.py:295
  288.0 0.0 copy-start
  288.0 2.0 copy-done
  290.0 0.2 reshape.152
  290.3 0.1 reduce_sum.60
  290.4 0.1 copy.25
  290.6 0.1 broadcast_in_dim.105
  290.7 3.3 %convert_element_type.34 = f32[16,136,1024]{2,1,0:T(8,128)S(1)} convert(bf16[16,136,1024]{2,1,0:T(8,128)(2,1)} %copy-done) | non-fusion elementwise | flops 2228224 | bytes 13369344 | tf_op jit(solution)/shard_map/convert_element_type | solution.py:311
  294.0 0.2 select_reduce_fusion
  294.2 0.6 select_reduce_fusion.2
  294.9 1.5 slice_reduce_fusion
  296.4 0.0 reduce-scatter.2.cloned.1.call-done
  (10 shorter events, 0.2 us)
Async XLA Ops:
  7.2 13.5 %copy-start.3 = (s32[128,6]{0,1:T(8,128)S(1)}, s32[128,6]{0,1:T(8,128)}, u32[]{:S(2)}) copy-start(s32[128,6]{0,1:T(8,128)} %param.7) | copy-start | bytes 9220
  7.2 13.6 %copy-start.4 = (f32[128,6]{0,1:T(8,128)S(1)}, f32[128,6]{0,1:T(8,128)}, u32[]{:S(2)}) copy-start(f32[128,6]{0,1:T(8,128)} %param.8) | copy-start | bytes 9220
  7.2 14.7 %copy-start.1 = (bf16[128,1024]{1,0:T(8,128)(2,1)S(1)}, bf16[128,1024]{1,0:T(8,128)(2,1)}, u32[]{:S(2)}) copy-start(bf16[128,1024]{1,0:T(8,128)(2,1)} %param.6) | copy-start | bytes 786436
  7.2 132.1 %all-gather.2.cloned.1.call-start = ((), (), s32[]{:S(2)}) async-start(), calls=%async_computation.4 | async-start | bytes 17842176 | tf_op jit(solution)/shard_map/all_gather | solution.py:264
  10.3 8.8 %collective-permute-start = (bf16[3,44,1024]{2,0,1:T(4,128)(2,1)S(1)}, bf16[3,44,1024]{2,0,1:T(4,128)(2,1)S(1)}, u32[]{:S(2)}, u32[]{:S(2)}) collective-permute-start(bf16[3,44,1024]{2,0,1:T(4,128)(2,1)S(1)} %pad_maximum_fusion.2), channel_id=1, source_target_pairs={{0,128},{32,160},{64,192},{96,224},{128,0},{160,32},{192,64},{224,... | collective-permute-start | bytes 811016 | tf_op jit(solution)/shard_map/ppermute | solution.py:262
  23.2 61.1 %copy-start.2 = (bf16[128,1024]{1,0:T(8,128)(2,1)S(1)}, bf16[128,1024]{1,0:T(8,128)(2,1)}, u32[]{:S(2)}) copy-start(bf16[128,1024]{1,0:T(8,128)(2,1)} %param.11) | copy-start | bytes 786436
  86.9 86.4 %all-to-all-start.1 = ((bf16[16,128,1024]{2,1,0:T(8,128)(2,1)}), bf16[16,128,1024]{2,1,0:T(8,128)(2,1)}, u32[]{:S(2)}, u32[]{:S(2)}) async-start(bf16[16,128,1024]{2,1,0:T(8,128)(2,1)} %broadcast_in_dim.104), calls=%async_computation.2 | async-start | bytes 8388608 | tf_op jit(solution)/shard_map/all_to_all | solution.py:295
  91.4 205.0 %reduce-scatter.2.cloned.1.call-start = ((), (), s32[]{:S(2)}) async-start(), calls=%async_computation.5 | async-start | bytes 4456448 | tf_op jit(solution)/shard_map/reduce_scatter | solution.py:308
  288.0 2.0 copy-start
Sparse Core Ops, SparseCore 0:
  20.8 118.4 all-gather.1
  173.4 112.8 reduce-scatter.1

commit v3 on v2

--- a/solution.py
+++ b/solution.py
@@ -5,7 +5,7 @@
 from jax.experimental.pallas import tpu as pltpu
 from jax.sharding import PartitionSpec as P
 
-STEP = 4
+STEP = 8
 SLOTS = 16
 VMEM = 56 * 1024 * 1024
 NT = (((1,), (1,)), ((), ()))
@@ -29,36 +29,26 @@
     x_ref[...] = xs.astype(jnp.bfloat16).reshape(x_ref.shape)
 
 
-def keep(expert, group, slots_ref, rows):
-    at = lax.rem(expert, group)
-    slots_ref[:, pl.ds(pl.multiple_of(at * SLOTS, SLOTS), SLOTS), :] = rows.reshape(
-        slots_ref.shape[0], SLOTS, rows.shape[1]
-    )
-
-
-def combine(expert, group, rank_ref, slots_ref, total_ref, out_ref):
-    sources, tok = rank_ref.shape[0], rank_ref.shape[2]
-    slot = slot_numbers(group, tok)
-
-    def sums(s, first):
-        place = one_hot(rank_ref[s, first : first + group, :], slot)
-        return lax.dot_general(place, slots_ref[s], TN, preferred_element_type=jnp.float32)
-
-    @pl.when(expert == group - 1)
-    def _():
-        def one(s, carry):
-            total_ref[s] = sums(s, 0)
-            return carry
-
-        lax.fori_loop(0, sources, one, 0)
-
-    @pl.when(expert == 2 * group - 1)
-    def _():
-        def one(s, carry):
-            out_ref[s, 0:tok, :] = (total_ref[s] + sums(s, group)).astype(out_ref.dtype)
-            return carry
-
-        lax.fori_loop(0, sources, one, 0)
+def keep(expert, slots_ref, rows):
+    at = pl.multiple_of(expert * SLOTS, SLOTS)
+    slots_ref[:, pl.ds(at, SLOTS), :] = rows.reshape(slots_ref.shape[0], SLOTS, rows.shape[1])
+
+
+def combine(rank_ref, slots_ref, *out_refs):
+    sources, half, tok = rank_ref.shape
+    slot = slot_numbers(half, tok)
+
+    def one(s, carry):
+        place = one_hot(rank_ref[s], slot)
+        sums = lax.dot_general(place, slots_ref[s], TN, preferred_element_type=jnp.float32)
+        start = 0
+        for out_ref in out_refs:
+            stop = start + out_ref.shape[2]
+            out_ref[s, 0:tok, :] = sums[:, start:stop].astype(out_ref.dtype)
+            start = stop
+        return carry
+
+    lax.fori_loop(0, sources, one, 0)
 
 
 def swish(pre, hidden):
@@ -68,74 +58,79 @@
     return gate, up, sig
 
 
-def forward_kernel(w_ref, x_ref, g_ref, rank_ref, out_ref, pre_ref, slots, total):
+def forward_kernel(w_ref, x_ref, g_ref, rank_ref, out_ref, pre_ref, slots):
     hidden = w_ref.shape[1] // 3
-    group = STEP * pl.num_programs(0) // 2
     first = pl.program_id(0) * STEP
+    kept = []
     for i in range(STEP):
         gate_up = w_ref[i, 0 : 2 * hidden, :]
-        down = w_ref[i, 2 * hidden : 3 * hidden, :]
         pre = lax.dot_general(x_ref[i], gate_up, NT, preferred_element_type=jnp.float32)
         pre_ref[i] = pre
         gate, up, sig = swish(pre, hidden)
+        kept.append((gate * sig * up).astype(jnp.bfloat16))
+    for i in range(STEP):
+        down = w_ref[i, 2 * hidden : 3 * hidden, :]
+        rows = jnp.dot(kept[i], down, preferred_element_type=jnp.float32)
         scale = jnp.transpose(g_ref[i])[:, 0:1]
-        scaled = (gate * sig * up * scale).astype(jnp.bfloat16)
-        rows = jnp.dot(scaled, down, preferred_element_type=jnp.float32)
-        keep(first + i, group, slots, rows.astype(jnp.bfloat16))
-    combine(first + STEP - 1, group, rank_ref, slots, total, out_ref)
-
-
-def backward_kernel(w_ref, pre_ref, g_ref, rank_ref, c_ref, out_ref, slots, total, dots):
+        keep(first + i, slots, (rows * scale).astype(jnp.bfloat16))
+
+    @pl.when(first + STEP == rank_ref.shape[1])
+    def _():
+        combine(rank_ref, slots, out_ref)
+
+
+def backward_kernel(
+    w_ref, pre_ref, g_ref, rank_ref, c_ref, out_ref, more_ref, slots, dots
+):
     hidden = w_ref.shape[1] // 3
-    half = STEP * pl.num_programs(0)
-    group = half // 2
     first = pl.program_id(0) * STEP
     sources, tok, model = c_ref.shape
-
-    @pl.when(lax.rem(first, group) == 0)
-    def _():
-        slot = slot_numbers(group, tok)
-
-        def one(s, carry):
-            ranks = rank_ref[s, pl.ds(pl.multiple_of(first, group), group), :]
-            cs = jnp.dot(one_hot(ranks, slot), c_ref[s], preferred_element_type=jnp.float32)
-            slots[s] = cs.astype(jnp.bfloat16)
-            return carry
-
-        lax.fori_loop(0, sources, one, 0)
+    half = rank_ref.shape[1]
 
     @pl.when(first == 0)
     def _():
+        slot = slot_numbers(half, tok)
+
+        def one(s, carry):
+            cs = jnp.dot(one_hot(rank_ref[s], slot), c_ref[s], preferred_element_type=jnp.float32)
+            scale = jnp.transpose(g_ref[s])[:, 0:1]
+            slots[s] = (cs * scale).astype(jnp.bfloat16)
+            return carry
+
+        lax.fori_loop(0, sources, one, 0)
         dots[...] = jnp.zeros_like(dots)
 
+    kept = []
     lane = lax.broadcasted_iota(jnp.int32, dots.shape, 1)
+    found = dots[...]
     for i in range(STEP):
-        gate_up = w_ref[i, 0 : 2 * hidden, :]
         down = w_ref[i, 2 * hidden : 3 * hidden, :]
-        at = pl.multiple_of(lax.rem(first + i, group) * SLOTS, SLOTS)
+        at = pl.multiple_of((first + i) * SLOTS, SLOTS)
         cs = slots[:, pl.ds(at, SLOTS), :].reshape(sources * SLOTS, model)
         back = lax.dot_general(cs, down, NT, preferred_element_type=jnp.float32)
         gate, up, sig = swish(pre_ref[i], hidden)
         act = gate * sig
         dot = jnp.sum(act * up * back, axis=1, keepdims=True)
-        dots[...] = jnp.where(lane == first + i, dot, dots[...])
-        scaled = back * jnp.transpose(g_ref[i])[:, 0:1]
-        grad_up = scaled * act
-        grad_gate = scaled * up * sig * (1.0 + gate * (1.0 - sig))
-        pair = jnp.concatenate([grad_gate, grad_up], axis=1).astype(jnp.bfloat16)
-        rows = jnp.dot(pair, gate_up, preferred_element_type=jnp.float32)
-        keep(first + i, group, slots, rows.astype(jnp.bfloat16))
-    combine(first + STEP - 1, group, rank_ref, slots, total, out_ref)
+        found = jnp.where(lane == first + i, dot, found)
+        grad_up = back * act
+        grad_gate = back * up * sig * (1.0 + gate * (1.0 - sig))
+        kept.append(jnp.concatenate([grad_gate, grad_up], axis=1).astype(jnp.bfloat16))
+    dots[...] = found
+    for i in range(STEP):
+        gate_up = w_ref[i, 0 : 2 * hidden, :]
+        rows = jnp.dot(kept[i], gate_up, preferred_element_type=jnp.float32)
+        keep(first + i, slots, rows.astype(jnp.bfloat16))
 
     @pl.when(first + STEP == half)
     def _():
+        combine(rank_ref, slots, out_ref, more_ref)
         low_rows = SLOTS // 2
 
         def one(s, carry):
             part = dots[pl.ds(pl.multiple_of(s * SLOTS, SLOTS), SLOTS), 0:half]
             high = part.astype(jnp.bfloat16).astype(jnp.float32)
             low = part - high
-            blank = jnp.zeros((low_rows, model - 4 * half), jnp.float32)
+            blank = jnp.zeros((low_rows, out_ref.shape[2] - 4 * half), jnp.float32)
             line = [high[0:low_rows], low[0:low_rows], high[low_rows:], low[low_rows:], blank]
             out_ref[s, tok : tok + low_rows, :] = jnp.concatenate(line, axis=1).astype(jnp.bfloat16)
             return carry
@@ -200,8 +195,7 @@
             jax.ShapeDtypeStruct((half, rows, 2 * hidden), jnp.float32),
         ],
         scratch_shapes=[
-            pltpu.VMEM((sources, half * SLOTS // 2, model), jnp.bfloat16),
-            pltpu.VMEM((sources, tok, model), jnp.float32),
+            pltpu.VMEM((sources, half * SLOTS, model), jnp.bfloat16),
         ],
         compiler_params=params(),
         cost_estimate=pl.CostEstimate(
@@ -224,15 +218,20 @@
         in_specs=[
             pl.BlockSpec((STEP, w_rows, model), each),
             pl.BlockSpec((STEP, rows, pre.shape[2]), each),
-            pl.BlockSpec((STEP, 8, rows), each),
+            pl.BlockSpec((sources, 8, half * SLOTS), whole),
             pl.BlockSpec((sources, half, tok), whole),
             pl.BlockSpec((sources, tok, model), whole),
         ],
-        out_specs=pl.BlockSpec((sources, out_rows, model), whole),
-        out_shape=jax.ShapeDtypeStruct((sources, out_rows, model), jnp.bfloat16),
+        out_specs=[
+            pl.BlockSpec((sources, out_rows, model // 2), whole),
+            pl.BlockSpec((sources, tok, model // 2), whole),
+        ],
+        out_shape=[
+            jax.ShapeDtypeStruct((sources, out_rows, model // 2), jnp.bfloat16),
+            jax.ShapeDtypeStruct((sources, tok, model // 2), jnp.bfloat16),
+        ],
         scratch_shapes=[
-            pltpu.VMEM((sources, half * SLOTS // 2, model), jnp.bfloat16),
-            pltpu.VMEM((sources, tok, model), jnp.float32),
+            pltpu.VMEM((sources, half * SLOTS, model), jnp.bfloat16),
             pltpu.VMEM((rows, 128), jnp.float32),
         ],
         compiler_params=params(),
@@ -300,22 +299,42 @@
     first, second = half * tok, half * tok + half * SLOTS
     ranks = facts_in[:, 0:first].reshape(planes, half, tok)
     scales = facts_in[:, first:second] + facts_in[:, second : second + half * SLOTS]
+    by_source = jnp.broadcast_to(scales[:, None], (planes, 8, half * SLOTS))
     scales = scales.reshape(planes, half, SLOTS).swapaxes(0, 1).reshape(half, 1, planes * SLOTS)
     scales = jnp.broadcast_to(scales, (half, 8, planes * SLOTS))
 
+    scales = scales + 0.0 * cotangents[0, 0, 0].astype(jnp.float32)
     x_rows = gather_rows(ranks, rows)
     layer_part, pre = forward(weights, x_rows, scales, ranks)
+    along_x = [[x * side + y for x in range(planes // side)] for y in range(side)]
+    along_y = [[x * side + y for y in range(side)] for x in range(planes // side)]
+    layer_x = lax.psum_scatter(
+        layer_part.reshape(planes * tok, model),
+        "dp",
+        scatter_dimension=0,
+        axis_index_groups=along_x,
+        tiled=True,
+    )
+    first_part, second_part = backward(weights, pre, by_source, ranks, cotangents)
+    first_in = swap_rows(first_part)
     layer_output = lax.psum_scatter(
-        layer_part.reshape(planes * tok, model), "dp", scatter_dimension=0, tiled=True
-    )
-    grad_in = swap_rows(backward(weights, pre, scales, ranks, cotangents)).astype(jnp.float32)
-    token_grads = jnp.sum(grad_in[:, 0:tok], axis=0).astype(jnp.bfloat16)
-
-    dots = grad_in[:, tok:, 0 : 4 * half].reshape(2, 2, side, SLOTS // 2, 2, 2, half)
+        layer_x + 0.0 * first_in[0, 0, 0].astype(layer_x.dtype),
+        "dp",
+        scatter_dimension=0,
+        axis_index_groups=along_y,
+        tiled=True,
+    )
+    second_in = swap_rows(second_part).astype(jnp.float32)
+    first_in = first_in.astype(jnp.float32)
+    token_grads = jnp.concatenate(
+        [jnp.sum(first_in[:, 0:tok], axis=0), jnp.sum(second_in, axis=0)], axis=1
+    ).astype(jnp.bfloat16)
+
+    dots = first_in[:, tok:, 0 : 4 * half].reshape(2, 2, side, SLOTS // 2, 2, 2, half)
     dots = jnp.sum(dots, axis=(0, 2, 5))
     dots = dots.transpose(3, 0, 2, 1).reshape(experts, SLOTS)
     by_expert = jnp.sum(jnp.where(at_slot, dots[:, :, None], 0.0), axis=1)
-    gate_grads = jnp.sum(jnp.where(match, by_expert[None], 0.0), axis=1).T
+    gate_grads = jnp.sum(jnp.where(match, by_expert[None], 0.0), axis=1).T / router_gates
     return (layer_output, token_grads, gate_grads)
 
 

time: 304 us -> 326 us (1.072)
  waiting for transfers between devices: 35.1 us -> 130 us
  blocking collectives: 125 us -> 58 us
  Pallas kernels: 99.6 us -> 71.3 us
  starting transfers between devices: 8.58 us -> 25.9 us
    all_to_all x1 -> x3, waiting for transfers between devices: 0.01 us -> 116 us  [body(): lax.all_to_all(a, 'dp', split_axis=0, concat_axis=0, tiled=True)]
    all_to_all x2 -> x1, blocking collectives: 125 us -> 58 us  [body(): lax.all_to_all(a, 'dp', split_axis=0, concat_axis=0, tiled=True)]
    all_gather x1, waiting for transfers between devices: 30.3 us -> 0.01 us  [body(): weights = lax.all_gather(mine, 'expert', axis=0, tiled=False)]
    pallas_call x1, Pallas kernels: 51.2 us -> 30.9 us  [backward(): pl.pallas_call(backward_kernel, grid=(half // STEP,), in_specs=[pl.BlockS...]
    all_to_all x1 -> x3, starting transfers between devices: 4.55 us -> 21.9 us  [body(): lax.all_to_all(a, 'dp', split_axis=0, concat_axis=0, tiled=True)]
    reduce_scatter x0 -> x1, waiting for transfers between devices: none -> 8.68 us  [body(): lax.psum_scatter(layer_x + 0.0 * first_in[0, 0, 0].astype(layer_x.dtype),...]
    pallas_call x1, Pallas kernels: 33.3 us -> 25.3 us  [forward(): pl.pallas_call(forward_kernel, grid=(half // STEP,), in_specs=[pl.BlockSp...]
  transfers between devices with their start and end apart: 4 -> 7, of which waited for: 2 -> 5; matrix products, arithmetic and copies ran while one was open for 5% -> 6% of each run, Pallas kernels for 33% -> 14%
where the time goes in v3:
time: 326 us; the launch traced here: 325 us
  waiting for transfers between devices  130 us (40%)
  Pallas kernels  71.3 us (22%)
  blocking collectives  58 us (18%)
  starting transfers between devices  25.9 us (8%)
  between operations  15.4 us (5%)
  local copies, waits for them, and re-layouts  12.4 us (4%)
  other arithmetic  11.7 us (4%)
    all_to_all x3, waiting for transfers between devices, body(): lax.all_to_all(a, 'dp', split_axis=0, concat_axis=0, tiled=True)  116 us
    all_to_all x1, blocking collectives, body(): lax.all_to_all(a, 'dp', split_axis=0, concat_axis=0, tiled=True)  58 us
    pallas_call x1, Pallas kernels, backward(): pl.pallas_call(backward_kernel, grid=(half // STEP,), in_specs=[pl.BlockS...  30.9 us
    pallas_call x1, Pallas kernels, forward(): pl.pallas_call(forward_kernel, grid=(half // STEP,), in_specs=[pl.BlockSp...  25.3 us
    all_to_all x3, starting transfers between devices, body(): lax.all_to_all(a, 'dp', split_axis=0, concat_axis=0, tiled=True)  21.9 us
    pallas_call x1, Pallas kernels, gather_rows(): pl.pallas_call(gather_kernel, grid=(sources,), in_specs=[pl.BlockSpec((1,...  15.1 us
    reduce_scatter x1, waiting for transfers between devices, body(): lax.psum_scatter(layer_x + 0.0 * first_in[0, 0, 0].astype(layer_x.dtype),...  8.68 us
  transfers between devices with their start and end apart: 7, of which 5 were waited for; matrix products, arithmetic and copies ran while one was open for 6% of the time, Pallas kernels for 14%

profile of v3, /device:TPU:1, one launch (start us, length us, event | category | flops | bytes accessed | tf_op | source)
XLA Modules:
  0.0 324.7 jit_solution(9616758878372600108)
XLA Ops:
  7.2 0.0 copy-start
  7.2 0.0 all-gather.2.cloned.1.call-start
  7.2 1.3 dynamic-slice_bitcast_fusion.1
  8.5 1.4 constant_dynamic-slice_fusion.1
  9.9 0.4 pad_maximum_fusion.2
  10.3 3.9 %collective-permute-start = (bf16[3,44,1024]{2,0,1:T(4,128)(2,1)S(1)}, bf16[3,44,1024]{2,0,1:T(4,128)(2,1)S(1)}, u32[]{:S(2)}, u32[]{:S(2)}) collective-permute-start(bf16[3,44,1024]{2,0,1:T(4,128)(2,1)S(1)} %pad_maximum_fusion.2), channel_id=1, source_target_pairs={{0,128},{32,160},{64,192},{96,224},{128,0},{160,32},{192,64},{224,... | collective-permute-start | bytes 811016 | tf_op jit(solution)/shard_map/ppermute | solution.py:261
  14.2 4.8 %collective-permute-done = bf16[3,44,1024]{2,0,1:T(4,128)(2,1)S(1)} collective-permute-done((bf16[3,44,1024]{2,0,1:T(4,128)(2,1)S(1)}, bf16[3,44,1024]{2,0,1:T(4,128)(2,1)S(1)}, u32[]{:S(2)}, u32[]{:S(2)}) %collective-permute-start) | collective-permute-done | bytes 270368 | tf_op jit(solution)/shard_map/ppermute | solution.py:261
  19.0 0.5 pad_maximum_fusion.1
  19.6 1.0 copy.22
  20.6 0.0 all-gather.2.cloned.1.call-update
  20.7 0.0 copy-done
  20.7 2.6 broadcast_in_dim.106
  23.2 0.0 copy-start.2
  23.2 0.0 copy-start.3
  23.2 10.2 %all-to-all-start.1 = ((bf16[16,128,1024]{2,1,0:T(8,128)(2,1)}), bf16[16,128,1024]{2,1,0:T(8,128)(2,1)}, u32[]{:S(2)}, u32[]{:S(2)}) async-start(bf16[16,128,1024]{2,1,0:T(8,128)(2,1)} %broadcast_in_dim.106), calls=%async_computation.1 | async-start | bytes 8388608 | tf_op jit(solution)/shard_map/all_to_all | solution.py:294
  33.4 0.0 copy-done.2
  33.5 0.0 copy-done.3
  33.5 0.1 fusion.13
  33.7 0.2 select_reduce_fusion.1
  33.9 0.2 slice_reduce_fusion.3
  34.1 0.1 concatenate.54
  34.2 0.1 concatenate.55
  34.3 0.1 concatenate.58
  34.4 0.1 concatenate.59
  34.5 0.1 fusion.12
  34.6 0.0 copy-done.1
  34.6 0.5 broadcast_in_dim.96
  35.2 2.6 pad_maximum_fusion
  37.7 47.4 %all-to-all-done.1.c_ref = bf16[16,128,1024]{2,1,0:T(8,128)(2,1)} async-done(((bf16[16,128,1024]{2,1,0:T(8,128)(2,1)}), bf16[16,128,1024]{2,1,0:T(8,128)(2,1)}, u32[]{:S(2)}, u32[]{:S(2)}) %all-to-all-start.1) | async-done | bytes 4194336 | tf_op jit(solution)/shard_map/all_to_all | solution.py:294
  85.1 7.3 %all-to-all-start = ((bf16[16,136,1024]{2,1,0:T(8,128)(2,1)}), bf16[16,136,1024]{2,1,0:T(8,128)(2,1)}, u32[]{:S(2)}, u32[]{:S(2)}) async-start(bf16[16,136,1024]{2,1,0:T(8,128)(2,1)} %pad_maximum_fusion), calls=%async_computation | async-start | bytes 8912896 | tf_op jit(solution)/shard_map/all_to_all | solution.py:294
  92.4 0.0 reduce-scatter.3.cloned.1.call-start
  92.5 1.2 slice.72
  94.3 47.0 %all-to-all-done.rows_ref = bf16[16,136,1024]{2,1,0:T(8,128)(2,1)} async-done(((bf16[16,136,1024]{2,1,0:T(8,128)(2,1)}), bf16[16,136,1024]{2,1,0:T(8,128)(2,1)}, u32[]{:S(2)}, u32[]{:S(2)}) %all-to-all-start) | async-done | bytes 4456480 | tf_op jit(solution)/shard_map/all_to_all | solution.py:294
  141.3 1.0 slice_convert_fusion
  142.3 0.3 copy.27
  142.6 0.8 copy.28
  143.4 0.1 add.43
  143.5 0.1 copy.23
  143.6 0.1 copy.24
  143.7 15.1 %gather_rows.1.x_ref = bf16[32,256,1024]{2,1,0:T(8,128)(2,1)} custom-call(f32[16,32,128]{2,1,0:T(8,128)} %bitcast.34, bf16[16,136,1024]{2,1,0:T(8,128)(2,1)} %all-to-all-done.rows_ref), custom_call_target="tpu_custom_call" | custom-call | flops 2147483648 | bytes 21233664 | tf_op jit(solution)/shard_map/gather_rows/pallas_call | solution.py:156
  158.8 0.7 broadcast_in_dim.107.g_ref
  159.5 25.3 %forward_experts.1 = (bf16[16,128,1024]{2,1,0:T(8,128)(2,1)}, f32[32,256,176]{2,1,0:T(8,128)}) custom-call(bf16[32,264,1024]{2,1,0:T(8,128)(2,1)} %all-gather.2.cloned.1.call-done.w_ref, bf16[32,256,1024]{2,1,0:T(8,128)(2,1)} %gather_rows.1.x_ref, f32[32,8,256]{2,1,0:T(8,128)} %broadcast_in_dim.107.g_ref, f32[16,32,128]{2,1,0:T(8,128)} %bitcast.35), custom_call_target="tpu_custom_call" | custom-call | flops 4429185024 | bytes 34078720 | tf_op jit(solution)/shard_map/forward_experts/pallas_call | solution.py:180
  184.8 0.0 reduce-scatter.3.cloned.1.call-update
  184.8 0.7 broadcast_in_dim.108.g_ref
  185.6 30.9 %backward_experts.1 = (bf16[16,136,512]{2,1,0:T(8,128)(2,1)}, bf16[16,128,512]{2,1,0:T(8,128)(2,1)}) custom-call(bf16[32,264,1024]{2,1,0:T(8,128)(2,1)} %all-gather.2.cloned.1.call-done.w_ref, f32[32,256,176]{2,1,0:T(8,128)} %get-tuple-element.8.pre_ref, f32[16,8,512]{2,1,0:T(8,128)} %broadcast_in_dim.108.g_ref, f32[16,32,128]{2,1,0:T(8,128)} %bitcast.36, ...), custom_call_target="tpu_custom_call" | custom-call | flops 4429185024 | bytes 23068672 | tf_op jit(solution)/shard_map/backward_experts/pallas_call | solution.py:215
  216.5 58.0 %all_to_all.20 = bf16[16,136,512]{2,1,0:T(8,128)(2,1)S(1)} all-to-all(bf16[16,136,512]{2,1,0:T(8,128)(2,1)} %get-tuple-element.9), channel_id=1, replica_groups=mesh['dp'=16,'expert'=32] {'dp'}, dimensions={0} | all-to-all | bytes 4456448 | tf_op jit(solution)/shard_map/all_to_all | solution.py:294
  274.5 4.4 %all-to-all-start.3 = ((bf16[16,128,512]{2,1,0:T(8,128)(2,1)}), bf16[16,128,512]{2,1,0:T(8,128)(2,1)}, u32[]{:S(2)}, u32[]{:S(2)}) async-start(bf16[16,128,512]{2,1,0:T(8,128)(2,1)} %get-tuple-element.10), calls=%async_computation.5 | async-start | bytes 4194304 | tf_op jit(solution)/shard_map/all_to_all | solution.py:294
  278.9 0.0 reduce-scatter.5.cloned.1.call-start
  279.0 0.5 slice.73
  280.2 0.0 reduce-scatter.3.cloned.1.call-done
  280.2 2.3 broadcast_add_fusion
  282.5 0.0 reduce-scatter.5.cloned.1.call-update
  282.5 21.9 %all-to-all-done.3 = bf16[16,128,512]{2,1,0:T(8,128)(2,1)} async-done(((bf16[16,128,512]{2,1,0:T(8,128)(2,1)}), bf16[16,128,512]{2,1,0:T(8,128)(2,1)}, u32[]{:S(2)}, u32[]{:S(2)}) %all-to-all-start.3) | async-done | bytes 2097184 | tf_op jit(solution)/shard_map/all_to_all | solution.py:294
  304.4 1.9 reduce
  306.3 0.2 reshape.159
  306.5 0.1 reduce_sum.70
  306.7 0.1 copy.25
  306.8 0.1 broadcast_in_dim.109
  306.9 0.6 convert_element_type.40
  307.5 0.2 select_reduce_fusion
  307.8 0.4 slice_reduce_fusion
  308.2 0.7 pad_maximum_fusion.3
  308.9 0.6 bitcast_divide_fusion
  309.5 8.7 %reduce-scatter.5.cloned.1.call-done = bf16[128,1024]{1,0:T(8,128)(2,1)} async-done(((bf16[512,1024]{1,0:T(8,128)(2,1)}), bf16[128,1024]{1,0:T(8,128)(2,1)}) %reduce-scatter.5.cloned.1.call-update) | async-done | bytes 262160 | tf_op jit(solution)/shard_map/reduce_scatter | solution.py:320
  (13 shorter events, 0.2 us)
Async XLA Ops:
  7.2 13.5 %copy-start = (bf16[128,1024]{1,0:T(8,128)(2,1)S(1)}, bf16[128,1024]{1,0:T(8,128)(2,1)}, u32[]{:S(2)}) copy-start(bf16[128,1024]{1,0:T(8,128)(2,1)} %param.11) | copy-start | bytes 786436
  7.2 151.6 %all-gather.2.cloned.1.call-start = ((), (), s32[]{:S(2)}) async-start(), calls=%async_computation.6 | async-start | bytes 17842176 | tf_op jit(solution)/shard_map/all_gather | solution.py:263
  10.3 8.8 %collective-permute-start = (bf16[3,44,1024]{2,0,1:T(4,128)(2,1)S(1)}, bf16[3,44,1024]{2,0,1:T(4,128)(2,1)S(1)}, u32[]{:S(2)}, u32[]{:S(2)}) collective-permute-start(bf16[3,44,1024]{2,0,1:T(4,128)(2,1)S(1)} %pad_maximum_fusion.2), channel_id=1, source_target_pairs={{0,128},{32,160},{64,192},{96,224},{128,0},{160,32},{192,64},{224,... | collective-permute-start | bytes 811016 | tf_op jit(solution)/shard_map/ppermute | solution.py:261
  23.2 10.2 %copy-start.2 = (s32[128,6]{0,1:T(8,128)S(1)}, s32[128,6]{0,1:T(8,128)}, u32[]{:S(2)}) copy-start(s32[128,6]{0,1:T(8,128)} %param.7) | copy-start | bytes 9220
  23.2 10.2 %copy-start.3 = (f32[128,6]{0,1:T(8,128)S(1)}, f32[128,6]{0,1:T(8,128)}, u32[]{:S(2)}) copy-start(f32[128,6]{0,1:T(8,128)} %param.8) | copy-start | bytes 9220
  23.2 11.4 %copy-start.1 = (bf16[128,1024]{1,0:T(8,128)(2,1)S(1)}, bf16[128,1024]{1,0:T(8,128)(2,1)}, u32[]{:S(2)}) copy-start(bf16[128,1024]{1,0:T(8,128)(2,1)} %param.6) | copy-start | bytes 786436
  23.2 61.9 %all-to-all-start.1 = ((bf16[16,128,1024]{2,1,0:T(8,128)(2,1)}), bf16[16,128,1024]{2,1,0:T(8,128)(2,1)}, u32[]{:S(2)}, u32[]{:S(2)}) async-start(bf16[16,128,1024]{2,1,0:T(8,128)(2,1)} %broadcast_in_dim.106), calls=%async_computation.1 | async-start | bytes 8388608 | tf_op jit(solution)/shard_map/all_to_all | solution.py:294
  85.1 56.1 %all-to-all-start = ((bf16[16,136,1024]{2,1,0:T(8,128)(2,1)}), bf16[16,136,1024]{2,1,0:T(8,128)(2,1)}, u32[]{:S(2)}, u32[]{:S(2)}) async-start(bf16[16,136,1024]{2,1,0:T(8,128)(2,1)} %pad_maximum_fusion), calls=%async_computation | async-start | bytes 8912896 | tf_op jit(solution)/shard_map/all_to_all | solution.py:294
  92.4 187.8 %reduce-scatter.3.cloned.1.call-start = ((), (), s32[]{:S(2)}) async-start(), calls=%async_computation.7 | async-start | bytes 5242880 | tf_op jit(solution)/shard_map/reduce_scatter | solution.py:311
  274.5 29.9 %all-to-all-start.3 = ((bf16[16,128,512]{2,1,0:T(8,128)(2,1)}), bf16[16,128,512]{2,1,0:T(8,128)(2,1)}, u32[]{:S(2)}, u32[]{:S(2)}) async-start(bf16[16,128,512]{2,1,0:T(8,128)(2,1)} %get-tuple-element.10), calls=%async_computation.5 | async-start | bytes 4194304 | tf_op jit(solution)/shard_map/all_to_all | solution.py:294
  278.9 39.3 %reduce-scatter.5.cloned.1.call-start = ((), (), s32[]{:S(2)}) async-start(), calls=%async_computation.8 | async-start | bytes 1310720 | tf_op jit(solution)/shard_map/reduce_scatter | solution.py:320
Sparse Core Ops, SparseCore 0:
  20.8 118.4 all-gather.1
  185.0 89.5 reduce-scatter.2
  283.4 34.7 reduce-scatter.4

commit v4 on v3

--- a/solution.py
+++ b/solution.py
@@ -34,18 +34,14 @@
     slots_ref[:, pl.ds(at, SLOTS), :] = rows.reshape(slots_ref.shape[0], SLOTS, rows.shape[1])
 
 
-def combine(rank_ref, slots_ref, *out_refs):
+def combine(rank_ref, slots_ref, out_ref):
     sources, half, tok = rank_ref.shape
     slot = slot_numbers(half, tok)
 
     def one(s, carry):
         place = one_hot(rank_ref[s], slot)
         sums = lax.dot_general(place, slots_ref[s], TN, preferred_element_type=jnp.float32)
-        start = 0
-        for out_ref in out_refs:
-            stop = start + out_ref.shape[2]
-            out_ref[s, 0:tok, :] = sums[:, start:stop].astype(out_ref.dtype)
-            start = stop
+        out_ref[s, 0:tok, :] = sums.astype(out_ref.dtype)
         return carry
 
     lax.fori_loop(0, sources, one, 0)
@@ -79,9 +75,7 @@
         combine(rank_ref, slots, out_ref)
 
 
-def backward_kernel(
-    w_ref, pre_ref, g_ref, rank_ref, c_ref, out_ref, more_ref, slots, dots
-):
+def backward_kernel(w_ref, pre_ref, g_ref, rank_ref, c_ref, out_ref, slots, dots):
     hidden = w_ref.shape[1] // 3
     first = pl.program_id(0) * STEP
     sources, tok, model = c_ref.shape
@@ -123,14 +117,14 @@
 
     @pl.when(first + STEP == half)
     def _():
-        combine(rank_ref, slots, out_ref, more_ref)
+        combine(rank_ref, slots, out_ref)
         low_rows = SLOTS // 2
 
         def one(s, carry):
             part = dots[pl.ds(pl.multiple_of(s * SLOTS, SLOTS), SLOTS), 0:half]
             high = part.astype(jnp.bfloat16).astype(jnp.float32)
             low = part - high
-            blank = jnp.zeros((low_rows, out_ref.shape[2] - 4 * half), jnp.float32)
+            blank = jnp.zeros((low_rows, model - 4 * half), jnp.float32)
             line = [high[0:low_rows], low[0:low_rows], high[low_rows:], low[low_rows:], blank]
             out_ref[s, tok : tok + low_rows, :] = jnp.concatenate(line, axis=1).astype(jnp.bfloat16)
             return carry
@@ -222,14 +216,8 @@
             pl.BlockSpec((sources, half, tok), whole),
             pl.BlockSpec((sources, tok, model), whole),
         ],
-        out_specs=[
-            pl.BlockSpec((sources, out_rows, model // 2), whole),
-            pl.BlockSpec((sources, tok, model // 2), whole),
-        ],
-        out_shape=[
-            jax.ShapeDtypeStruct((sources, out_rows, model // 2), jnp.bfloat16),
-            jax.ShapeDtypeStruct((sources, tok, model // 2), jnp.bfloat16),
-        ],
+        out_specs=pl.BlockSpec((sources, out_rows, model), whole),
+        out_shape=jax.ShapeDtypeStruct((sources, out_rows, model), jnp.bfloat16),
         scratch_shapes=[
             pltpu.VMEM((sources, half * SLOTS, model), jnp.bfloat16),
             pltpu.VMEM((rows, 128), jnp.float32),
@@ -303,34 +291,15 @@
     scales = scales.reshape(planes, half, SLOTS).swapaxes(0, 1).reshape(half, 1, planes * SLOTS)
     scales = jnp.broadcast_to(scales, (half, 8, planes * SLOTS))
 
-    scales = scales + 0.0 * cotangents[0, 0, 0].astype(jnp.float32)
     x_rows = gather_rows(ranks, rows)
     layer_part, pre = forward(weights, x_rows, scales, ranks)
-    along_x = [[x * side + y for x in range(planes // side)] for y in range(side)]
-    along_y = [[x * side + y for y in range(side)] for x in range(planes // side)]
-    layer_x = lax.psum_scatter(
-        layer_part.reshape(planes * tok, model),
-        "dp",
-        scatter_dimension=0,
-        axis_index_groups=along_x,
-        tiled=True,
+    layer_output = lax.psum_scatter(
+        layer_part.reshape(planes * tok, model), "dp", scatter_dimension=0, tiled=True
     )
-    first_part, second_part = backward(weights, pre, by_source, ranks, cotangents)
-    first_in = swap_rows(first_part)
-    layer_output = lax.psum_scatter(
-        layer_x + 0.0 * first_in[0, 0, 0].astype(layer_x.dtype),
-        "dp",
-        scatter_dimension=0,
-        axis_index_groups=along_y,
-        tiled=True,
-    )
-    second_in = swap_rows(second_part).astype(jnp.float32)
-    first_in = first_in.astype(jnp.float32)
-    token_grads = jnp.concatenate(
-        [jnp.sum(first_in[:, 0:tok], axis=0), jnp.sum(second_in, axis=0)], axis=1
-    ).astype(jnp.bfloat16)
-
-    dots = first_in[:, tok:, 0 : 4 * half].reshape(2, 2, side, SLOTS // 2, 2, 2, half)
+    grad_in = swap_rows(backward(weights, pre, by_source, ranks, cotangents)).astype(jnp.float32)
+    token_grads = jnp.sum(grad_in[:, 0:tok], axis=0).astype(jnp.bfloat16)
+
+    dots = grad_in[:, tok:, 0 : 4 * half].reshape(2, 2, side, SLOTS // 2, 2, 2, half)
     dots = jnp.sum(dots, axis=(0, 2, 5))
     dots = dots.transpose(3, 0, 2, 1).reshape(experts, SLOTS)
     by_expert = jnp.sum(jnp.where(at_slot, dots[:, :, None], 0.0), axis=1)

time: 326 us -> 298 us (0.914)
  waiting for transfers between devices: 130 us -> 54.2 us
  blocking collectives: 58 us -> 126 us
  starting transfers between devices: 25.9 us -> 8.58 us
    all_to_all x3 -> x1, waiting for transfers between devices: 116 us -> 0.01 us  [body(): lax.all_to_all(a, 'dp', split_axis=0, concat_axis=0, tiled=True)]
    all_to_all x1 -> x2, blocking collectives: 58 us -> 126 us  [body(): lax.all_to_all(a, 'dp', split_axis=0, concat_axis=0, tiled=True)]
    all_gather x1, waiting for transfers between devices: 0.01 us -> 30.3 us  [body(): weights = lax.all_gather(mine, 'expert', axis=0, tiled=False)]
    reduce_scatter x1, waiting for transfers between devices: 0.02 us -> 19.1 us  [body(): lax.psum_scatter(layer_part.reshape(planes * tok, model), 'dp', scatter_d...]
    all_to_all x3 -> x1, starting transfers between devices: 21.9 us -> 4.55 us  [body(): lax.all_to_all(a, 'dp', split_axis=0, concat_axis=0, tiled=True)]
    reduce_scatter x1 -> x0, waiting for transfers between devices: 8.68 us -> none  [body(): lax.psum_scatter(layer_x + 0.0 * first_in[0, 0, 0].astype(layer_x.dtype),...]
  transfers between devices with their start and end apart: 7 -> 4, of which waited for: 5 -> 3; matrix products, arithmetic and copies ran while one was open for 6% -> 5% of each run, Pallas kernels for 14% -> 24%
where the time goes in v4:
time: 298 us; the launch traced here: 296 us
  blocking collectives  126 us (42%)
  Pallas kernels  71.4 us (24%)
  waiting for transfers between devices  54.2 us (18%)
  between operations  14.3 us (5%)
  local copies, waits for them, and re-layouts  12.8 us (4%)
  other arithmetic  8.83 us (3%)
  starting transfers between devices  8.58 us (3%)
    all_to_all x2, blocking collectives, body(): lax.all_to_all(a, 'dp', split_axis=0, concat_axis=0, tiled=True)  126 us
    pallas_call x1, Pallas kernels, backward(): pl.pallas_call(backward_kernel, grid=(half // STEP,), in_specs=[pl.BlockS...  30.9 us
    all_gather x1, waiting for transfers between devices, body(): weights = lax.all_gather(mine, 'expert', axis=0, tiled=False)  30.3 us
    pallas_call x1, Pallas kernels, forward(): pl.pallas_call(forward_kernel, grid=(half // STEP,), in_specs=[pl.BlockSp...  25.3 us
    reduce_scatter x1, waiting for transfers between devices, body(): lax.psum_scatter(layer_part.reshape(planes * tok, model), 'dp', scatter_d...  19.1 us
    pallas_call x1, Pallas kernels, gather_rows(): pl.pallas_call(gather_kernel, grid=(sources,), in_specs=[pl.BlockSpec((1,...  15.1 us
  transfers between devices with their start and end apart: 4, of which 3 were waited for; matrix products, arithmetic and copies ran while one was open for 5% of the time, Pallas kernels for 24%

profile of v4, /device:TPU:1, one launch (start us, length us, event | category | flops | bytes accessed | tf_op | source)
XLA Modules:
  0.0 296.4 jit_solution(14443829436936412218)
XLA Ops:
  7.2 0.0 copy-start.3
  7.2 0.0 copy-start.4
  7.2 0.0 copy-start.1
  7.2 0.0 all-gather.2.cloned.1.call-start
  7.3 1.3 dynamic-slice_bitcast_fusion.1
  8.6 1.4 constant_dynamic-slice_fusion.1
  10.0 0.4 pad_maximum_fusion.2
  10.3 3.9 %collective-permute-start = (bf16[3,44,1024]{2,0,1:T(4,128)(2,1)S(1)}, bf16[3,44,1024]{2,0,1:T(4,128)(2,1)S(1)}, u32[]{:S(2)}, u32[]{:S(2)}) collective-permute-start(bf16[3,44,1024]{2,0,1:T(4,128)(2,1)S(1)} %pad_maximum_fusion.2), channel_id=1, source_target_pairs={{0,128},{32,160},{64,192},{96,224},{128,0},{160,32},{192,64},{224,... | collective-permute-start | bytes 811016 | tf_op jit(solution)/shard_map/ppermute | solution.py:249
  14.3 4.8 %collective-permute-done = bf16[3,44,1024]{2,0,1:T(4,128)(2,1)S(1)} collective-permute-done((bf16[3,44,1024]{2,0,1:T(4,128)(2,1)S(1)}, bf16[3,44,1024]{2,0,1:T(4,128)(2,1)S(1)}, u32[]{:S(2)}, u32[]{:S(2)}) %collective-permute-start) | collective-permute-done | bytes 270368 | tf_op jit(solution)/shard_map/ppermute | solution.py:249
  19.1 0.5 pad_maximum_fusion.1
  19.6 1.0 copy.22
  20.7 0.0 all-gather.2.cloned.1.call-update
  20.7 0.0 copy-done.3
  20.7 0.0 copy-done.4
  20.8 0.1 fusion.13
  20.9 0.2 select_reduce_fusion.1
  21.2 0.2 slice_reduce_fusion.3
  21.4 0.1 concatenate.50
  21.5 0.1 concatenate.51
  21.6 0.1 concatenate.54
  21.6 0.1 concatenate.55
  21.8 0.1 fusion.12
  21.9 0.0 copy-done.1
  21.9 0.5 broadcast_in_dim.98
  22.4 0.7 pad_maximum_fusion
  23.2 0.0 copy-start.2
  23.2 61.1 %all_to_all.15.rows_ref = bf16[16,136,1024]{2,1,0:T(8,128)(2,1)} all-to-all(bf16[16,136,1024]{2,1,0:T(8,128)(2,1)S(1)} %pad_maximum_fusion), channel_id=1, replica_groups=mesh['dp'=16,'expert'=32] {'dp'}, dimensions={0} | all-to-all | bytes 8912896 | tf_op jit(solution)/shard_map/all_to_all | solution.py:282
  84.3 0.0 copy-done.2
  84.3 2.6 broadcast_in_dim.111
  86.9 4.6 %all-to-all-start.1 = ((bf16[16,128,1024]{2,1,0:T(8,128)(2,1)}), bf16[16,128,1024]{2,1,0:T(8,128)(2,1)}, u32[]{:S(2)}, u32[]{:S(2)}) async-start(bf16[16,128,1024]{2,1,0:T(8,128)(2,1)} %broadcast_in_dim.111), calls=%async_computation.2 | async-start | bytes 8388608 | tf_op jit(solution)/shard_map/all_to_all | solution.py:282
  91.4 0.0 reduce-scatter.2.cloned.1.call-start
  91.5 1.0 slice_convert_fusion
  92.5 0.3 copy.27
  92.8 0.8 copy.28
  93.6 0.1 reshape.151
  93.7 0.1 copy.23
  93.8 0.1 copy.24
  93.9 15.1 %gather_rows.1.x_ref = bf16[32,256,1024]{2,1,0:T(8,128)(2,1)} custom-call(f32[16,32,128]{2,1,0:T(8,128)} %bitcast.31, bf16[16,136,1024]{2,1,0:T(8,128)(2,1)} %all_to_all.15.rows_ref), custom_call_target="tpu_custom_call" | custom-call | flops 2147483648 | bytes 21233664 | tf_op jit(solution)/shard_map/gather_rows/pallas_call | solution.py:150
  109.0 30.3 %all-gather.2.cloned.1.call-done.w_ref = bf16[32,264,1024]{2,1,0:T(8,128)(2,1)} async-done(((bf16[1,264,1024]{2,1,0:T(8,128)(2,1)}), bf16[32,264,1024]{2,1,0:T(8,128)(2,1)}) %all-gather.2.cloned.1.call-update) | async-done | bytes 17301520 | tf_op jit(solution)/shard_map/all_gather | solution.py:251
  139.3 0.7 broadcast_in_dim.109.g_ref
  140.0 25.3 %forward_experts.1 = (bf16[16,128,1024]{2,1,0:T(8,128)(2,1)}, f32[32,256,176]{2,1,0:T(8,128)}) custom-call(bf16[32,264,1024]{2,1,0:T(8,128)(2,1)} %all-gather.2.cloned.1.call-done.w_ref, bf16[32,256,1024]{2,1,0:T(8,128)(2,1)} %gather_rows.1.x_ref, f32[32,8,256]{2,1,0:T(8,128)} %broadcast_in_dim.109.g_ref, f32[16,32,128]{2,1,0:T(8,128)} %bitcast.32), custom_call_target="tpu_custom_call" | custom-call | flops 4429185024 | bytes 34078720 | tf_op jit(solution)/shard_map/forward_experts/pallas_call | solution.py:174
  165.3 0.0 reduce-scatter.2.cloned.1.call-update
  165.3 0.0 all-to-all-done.1.c_ref
  165.4 0.7 broadcast_in_dim.110.g_ref
  166.1 30.9 %backward_experts.1 = bf16[16,136,1024]{2,1,0:T(8,128)(2,1)} custom-call(bf16[32,264,1024]{2,1,0:T(8,128)(2,1)} %all-gather.2.cloned.1.call-done.w_ref, f32[32,256,176]{2,1,0:T(8,128)} %get-tuple-element.6.pre_ref, f32[16,8,512]{2,1,0:T(8,128)} %broadcast_in_dim.110.g_ref, f32[16,32,128]{2,1,0:T(8,128)} %bitcast.33, bf16[16,128,1024]{2,1,0:T(8,128)(2,1)} %all-to-all-done.1.c_ref), custom_call_target="tpu_custom_call" | custom-call | flops 4429185024 | bytes 23068672 | tf_op jit(solution)/shard_map/backward_experts/pallas_call | solution.py:209
  197.0 65.0 %all_to_all.16 = bf16[16,136,1024]{2,1,0:T(8,128)(2,1)S(1)} all-to-all(bf16[16,136,1024]{2,1,0:T(8,128)(2,1)} %backward_experts.1), channel_id=1, replica_groups=mesh['dp'=16,'expert'=32] {'dp'}, dimensions={0} | all-to-all | bytes 8912896 | tf_op jit(solution)/shard_map/all_to_all | solution.py:282
  262.1 0.0 copy-start
  262.1 2.0 copy-done
  264.1 0.2 reshape.153
  264.4 0.1 reduce_sum.60
  264.5 0.1 copy.25
  264.6 0.1 broadcast_in_dim.112
  264.7 3.3 %convert_element_type.34 = f32[16,136,1024]{2,1,0:T(8,128)S(1)} convert(bf16[16,136,1024]{2,1,0:T(8,128)(2,1)} %copy-done) | non-fusion elementwise | flops 2228224 | bytes 13369344 | tf_op jit(solution)/shard_map/convert_element_type | solution.py:299
  268.1 0.2 select_reduce_fusion
  268.4 0.6 bitcast_divide_fusion
  269.0 1.5 slice_reduce_fusion
  270.5 19.1 %reduce-scatter.2.cloned.1.call-done = bf16[128,1024]{1,0:T(8,128)(2,1)} async-done(((bf16[2048,1024]{1,0:T(8,128)(2,1)}), bf16[128,1024]{1,0:T(8,128)(2,1)}) %reduce-scatter.2.cloned.1.call-update) | async-done | bytes 262160 | tf_op jit(solution)/shard_map/reduce_scatter | solution.py:296
  (11 shorter events, 0.2 us)
Async XLA Ops:
  7.2 13.5 %copy-start.3 = (s32[128,6]{0,1:T(8,128)S(1)}, s32[128,6]{0,1:T(8,128)}, u32[]{:S(2)}) copy-start(s32[128,6]{0,1:T(8,128)} %param.7) | copy-start | bytes 9220
  7.2 13.6 %copy-start.4 = (f32[128,6]{0,1:T(8,128)S(1)}, f32[128,6]{0,1:T(8,128)}, u32[]{:S(2)}) copy-start(f32[128,6]{0,1:T(8,128)} %param.8) | copy-start | bytes 9220
  7.2 14.7 %copy-start.1 = (bf16[128,1024]{1,0:T(8,128)(2,1)S(1)}, bf16[128,1024]{1,0:T(8,128)(2,1)}, u32[]{:S(2)}) copy-start(bf16[128,1024]{1,0:T(8,128)(2,1)} %param.6) | copy-start | bytes 786436
  7.2 132.1 %all-gather.2.cloned.1.call-start = ((), (), s32[]{:S(2)}) async-start(), calls=%async_computation.4 | async-start | bytes 17842176 | tf_op jit(solution)/shard_map/all_gather | solution.py:251
  10.3 8.8 %collective-permute-start = (bf16[3,44,1024]{2,0,1:T(4,128)(2,1)S(1)}, bf16[3,44,1024]{2,0,1:T(4,128)(2,1)S(1)}, u32[]{:S(2)}, u32[]{:S(2)}) collective-permute-start(bf16[3,44,1024]{2,0,1:T(4,128)(2,1)S(1)} %pad_maximum_fusion.2), channel_id=1, source_target_pairs={{0,128},{32,160},{64,192},{96,224},{128,0},{160,32},{192,64},{224,... | collective-permute-start | bytes 811016 | tf_op jit(solution)/shard_map/ppermute | solution.py:249
  23.2 61.1 %copy-start.2 = (bf16[128,1024]{1,0:T(8,128)(2,1)S(1)}, bf16[128,1024]{1,0:T(8,128)(2,1)}, u32[]{:S(2)}) copy-start(bf16[128,1024]{1,0:T(8,128)(2,1)} %param.11) | copy-start | bytes 786436
  86.9 78.5 %all-to-all-start.1 = ((bf16[16,128,1024]{2,1,0:T(8,128)(2,1)}), bf16[16,128,1024]{2,1,0:T(8,128)(2,1)}, u32[]{:S(2)}, u32[]{:S(2)}) async-start(bf16[16,128,1024]{2,1,0:T(8,128)(2,1)} %broadcast_in_dim.111), calls=%async_computation.2 | async-start | bytes 8388608 | tf_op jit(solution)/shard_map/all_to_all | solution.py:282
  91.4 198.1 %reduce-scatter.2.cloned.1.call-start = ((), (), s32[]{:S(2)}) async-start(), calls=%async_computation.5 | async-start | bytes 4456448 | tf_op jit(solution)/shard_map/reduce_scatter | solution.py:296
  262.1 2.0 copy-start
Sparse Core Ops, SparseCore 0:
  20.8 118.4 all-gather.1
  165.5 124.0 reduce-scatter.1

commit v5 on v4

--- a/solution.py
+++ b/solution.py
@@ -34,14 +34,23 @@
     slots_ref[:, pl.ds(at, SLOTS), :] = rows.reshape(slots_ref.shape[0], SLOTS, rows.shape[1])
 
 
-def combine(rank_ref, slots_ref, out_ref):
+def combine(rank_ref, slots_ref, *out_refs):
     sources, half, tok = rank_ref.shape
     slot = slot_numbers(half, tok)
 
     def one(s, carry):
         place = one_hot(rank_ref[s], slot)
         sums = lax.dot_general(place, slots_ref[s], TN, preferred_element_type=jnp.float32)
-        out_ref[s, 0:tok, :] = sums.astype(out_ref.dtype)
+        start = 0
+        for out_ref in out_refs:
+            stop = start + out_ref.shape[-1]
+            part = sums[:, start:stop].astype(out_ref.dtype)
+            if len(out_ref.shape) == 3:
+                out_ref[s, 0:tok, :] = part
+            else:
+                side = out_ref.shape[0]
+                out_ref[lax.rem(s, side), lax.div(s, side), 0:tok, :] = part
+            start = stop
         return carry
 
     lax.fori_loop(0, sources, one, 0)
@@ -75,7 +84,9 @@
         combine(rank_ref, slots, out_ref)
 
 
-def backward_kernel(w_ref, pre_ref, g_ref, rank_ref, c_ref, out_ref, slots, dots):
+def backward_kernel(
+    w_ref, pre_ref, g_ref, rank_ref, c_ref, out_ref, more_ref, slots, dots
+):
     hidden = w_ref.shape[1] // 3
     first = pl.program_id(0) * STEP
     sources, tok, model = c_ref.shape
@@ -117,16 +128,17 @@
 
     @pl.when(first + STEP == half)
     def _():
-        combine(rank_ref, slots, out_ref)
-        low_rows = SLOTS // 2
+        combine(rank_ref, slots, out_ref, more_ref)
+        low_rows, side = SLOTS // 2, out_ref.shape[0]
 
         def one(s, carry):
             part = dots[pl.ds(pl.multiple_of(s * SLOTS, SLOTS), SLOTS), 0:half]
             high = part.astype(jnp.bfloat16).astype(jnp.float32)
             low = part - high
-            blank = jnp.zeros((low_rows, model - 4 * half), jnp.float32)
+            blank = jnp.zeros((low_rows, out_ref.shape[3] - 4 * half), jnp.float32)
             line = [high[0:low_rows], low[0:low_rows], high[low_rows:], low[low_rows:], blank]
-            out_ref[s, tok : tok + low_rows, :] = jnp.concatenate(line, axis=1).astype(jnp.bfloat16)
+            line = jnp.concatenate(line, axis=1).astype(jnp.bfloat16)
+            out_ref[lax.rem(s, side), lax.div(s, side), tok : tok + low_rows, :] = line
             return carry
 
         lax.fori_loop(0, sources, one, 0)
@@ -201,7 +213,7 @@
     )(weights, x_rows, scales, ranks)
 
 
-def backward(weights, pre, scales, ranks, cotangents):
+def backward(weights, pre, scales, ranks, cotangents, side):
     half, w_rows, model = weights.shape
     sources, _, tok = ranks.shape
     rows = sources * SLOTS
@@ -216,8 +228,14 @@
             pl.BlockSpec((sources, half, tok), whole),
             pl.BlockSpec((sources, tok, model), whole),
         ],
-        out_specs=pl.BlockSpec((sources, out_rows, model), whole),
-        out_shape=jax.ShapeDtypeStruct((sources, out_rows, model), jnp.bfloat16),
+        out_specs=[
+            pl.BlockSpec((side, sources // side, out_rows, model // 2), lambda e: (0, 0, 0, 0)),
+            pl.BlockSpec((side, sources // side, tok, model // 2), lambda e: (0, 0, 0, 0)),
+        ],
+        out_shape=[
+            jax.ShapeDtypeStruct((side, sources // side, out_rows, model // 2), jnp.bfloat16),
+            jax.ShapeDtypeStruct((side, sources // side, tok, model // 2), jnp.bfloat16),
+        ],
         scratch_shapes=[
             pltpu.VMEM((sources, half * SLOTS, model), jnp.bfloat16),
             pltpu.VMEM((rows, 128), jnp.float32),
@@ -281,7 +299,7 @@
     spread = lambda a: jnp.broadcast_to(a[None], (planes, tok, model))
     swap_rows = lambda a: lax.all_to_all(a, "dp", split_axis=0, concat_axis=0, tiled=True)
     rows = swap_rows(jnp.concatenate([spread(tokens), known], axis=1))
-    cotangents = swap_rows(spread(cotangent))
+    cotangents = swap_rows(spread(cotangent + 0.0 * rows[0, 0, 0]))
 
     facts_in = rows[:, tok:, :].reshape(planes, fact_rows * model).astype(jnp.float32)
     first, second = half * tok, half * tok + half * SLOTS
@@ -291,16 +309,42 @@
     scales = scales.reshape(planes, half, SLOTS).swapaxes(0, 1).reshape(half, 1, planes * SLOTS)
     scales = jnp.broadcast_to(scales, (half, 8, planes * SLOTS))
 
+    scales = scales + 0.0 * cotangents[0, 0, 0].astype(jnp.float32)
     x_rows = gather_rows(ranks, rows)
     layer_part, pre = forward(weights, x_rows, scales, ranks)
-    layer_output = lax.psum_scatter(
-        layer_part.reshape(planes * tok, model), "dp", scatter_dimension=0, tiled=True
-    )
-    grad_in = swap_rows(backward(weights, pre, by_source, ranks, cotangents)).astype(jnp.float32)
+    along_x = [[x * side + y for x in range(planes // side)] for y in range(side)]
+    along_y = [[x * side + y for y in range(side)] for x in range(planes // side)]
+
+    def reduce_rows(a, groups):
+        return lax.psum_scatter(
+            a, "dp", scatter_dimension=0, axis_index_groups=groups, tiled=True
+        )
+
+    def swap_along(a, groups):
+        return lax.all_to_all(
+            a, "dp", split_axis=0, concat_axis=0, axis_index_groups=groups, tiled=True
+        )
+
+    layer_x = reduce_rows(layer_part.reshape(planes * tok, model), along_x)
+    first_part, second_part = backward(weights, pre, by_source, ranks, cotangents, side)
+    first_in = swap_along(first_part, along_y)
+    layer_x = layer_x + 0.0 * first_in[0, 0, 0, 0]
+    layer_output = reduce_rows(layer_x, along_y)
+    second_in = swap_along(second_part + 0.0 * layer_x[0, 0], along_y)
+
+    first_in = first_in.astype(jnp.float32)
+    dots = jnp.sum(first_in[:, :, tok:, 0 : 4 * half], axis=0)
+    dots = jnp.sum(dots.reshape(-1, SLOTS // 2, 2, 2, half), axis=3)
+    high = lax.reduce_precision(dots, 8, 7)
+    dots = jnp.stack([high, dots - high], axis=3).reshape(-1, SLOTS // 2, 4 * half)
+    dots = jnp.pad(dots, ((0, 0), (0, 0), (0, model - 4 * half)))
+    halves = [first_in[:, :, 0:tok], second_in.astype(jnp.float32)]
+    grad_sums = jnp.concatenate([jnp.sum(a, axis=0) for a in halves], axis=2)
+    grad_in = jnp.concatenate([grad_sums, dots], axis=1).astype(jnp.bfloat16)
+    grad_in = swap_along(grad_in, along_x).astype(jnp.float32)
     token_grads = jnp.sum(grad_in[:, 0:tok], axis=0).astype(jnp.bfloat16)
-
-    dots = grad_in[:, tok:, 0 : 4 * half].reshape(2, 2, side, SLOTS // 2, 2, 2, half)
-    dots = jnp.sum(dots, axis=(0, 2, 5))
+    dots = grad_in[:, tok:, 0 : 4 * half].reshape(-1, 2, SLOTS // 2, 2, 2, half)
+    dots = jnp.sum(dots, axis=(0, 4))
     dots = dots.transpose(3, 0, 2, 1).reshape(experts, SLOTS)
     by_expert = jnp.sum(jnp.where(at_slot, dots[:, :, None], 0.0), axis=1)
     gate_grads = jnp.sum(jnp.where(match, by_expert[None], 0.0), axis=1).T / router_gates

time: 298 us -> 305 us (1.023)
  the two profiles are of different devices: /device:TPU:1 before, /device:TPU:416 now
where the time goes in v5:
time: 305 us; the launch traced here: 304 us
  blocking collectives  110 us (36%)
  Pallas kernels  71.3 us (23%)
  waiting for transfers between devices  60.2 us (20%)
  local copies, waits for them, and re-layouts  17.7 us (6%)
  between operations  16.8 us (6%)
  other arithmetic  15.1 us (5%)
  starting transfers between devices  12.7 us (4%)
    all_to_all x1, blocking collectives, body(): lax.all_to_all(a, 'dp', split_axis=0, concat_axis=0, tiled=True)  59.5 us
    all_to_all x2, blocking collectives, swap_along(): lax.all_to_all(a, 'dp', split_axis=0, concat_axis=0, axis_index_groups=gr...  50.5 us
    all_to_all x1, waiting for transfers between devices, body(): lax.all_to_all(a, 'dp', split_axis=0, concat_axis=0, tiled=True)  35.1 us
    pallas_call x1, Pallas kernels, backward(): pl.pallas_call(backward_kernel, grid=(half // STEP,), in_specs=[pl.BlockS...  30.9 us
    pallas_call x1, Pallas kernels, forward(): pl.pallas_call(forward_kernel, grid=(half // STEP,), in_specs=[pl.BlockSp...  25.3 us
    all_to_all x1, waiting for transfers between devices, swap_along(): lax.all_to_all(a, 'dp', split_axis=0, concat_axis=0, axis_index_groups=gr...  16.4 us
    pallas_call x1, Pallas kernels, gather_rows(): pl.pallas_call(gather_kernel, grid=(sources,), in_specs=[pl.BlockSpec((1,...  15.1 us
    ppermute x1, waiting for transfers between devices, body(): other = lax.ppermute(both_slices(1 - parity), 'dp', swap)  8.64 us
  transfers between devices with their start and end apart: 6, of which 3 were waited for; matrix products, arithmetic and copies ran while one was open for 6% of the time, Pallas kernels for 15%

profile of v5, /device:TPU:416, one launch (start us, length us, event | category | flops | bytes accessed | tf_op | source)
XLA Modules:
  0.0 304.0 jit_solution(6586489124603202838)
XLA Ops:
  7.2 0.0 all-gather.2.cloned.1.call-start
  7.2 1.3 dynamic-slice_bitcast_fusion.1
  8.5 1.4 constant_dynamic-slice_fusion.1
  9.9 0.4 pad_maximum_fusion.2
  10.3 3.4 %collective-permute-start = (bf16[3,44,1024]{2,0,1:T(4,128)(2,1)S(1)}, bf16[3,44,1024]{2,0,1:T(4,128)(2,1)S(1)}, u32[]{:S(2)}, u32[]{:S(2)}) collective-permute-start(bf16[3,44,1024]{2,0,1:T(4,128)(2,1)S(1)} %pad_maximum_fusion.2), channel_id=1, source_target_pairs={{0,128},{32,160},{64,192},{96,224},{128,0},{160,32},{192,64},{224,... | collective-permute-start | bytes 811016 | tf_op jit(solution)/shard_map/ppermute | solution.py:267
  13.7 8.6 %collective-permute-done = bf16[3,44,1024]{2,0,1:T(4,128)(2,1)S(1)} collective-permute-done((bf16[3,44,1024]{2,0,1:T(4,128)(2,1)S(1)}, bf16[3,44,1024]{2,0,1:T(4,128)(2,1)S(1)}, u32[]{:S(2)}, u32[]{:S(2)}) %collective-permute-start) | collective-permute-done | bytes 270368 | tf_op jit(solution)/shard_map/ppermute | solution.py:267
  22.4 0.5 pad_maximum_fusion.1
  22.9 1.0 copy.24
  24.0 0.1 fusion.16
  24.2 0.2 select_reduce_fusion.1
  24.4 0.2 slice_reduce_fusion.5
  24.6 0.1 concatenate.58
  24.7 0.1 concatenate.59
  24.8 0.1 concatenate.62
  24.9 0.1 concatenate.63
  25.0 0.1 fusion.15
  25.2 0.5 broadcast_in_dim.96
  25.7 0.7 pad_maximum_fusion
  26.4 59.5 %all_to_all.25.rows_ref = bf16[16,136,1024]{2,1,0:T(8,128)(2,1)S(1)} all-to-all(bf16[16,136,1024]{2,1,0:T(8,128)(2,1)S(1)} %pad_maximum_fusion), channel_id=1, replica_groups=mesh['dp'=16,'expert'=32] {'dp'}, dimensions={0} | all-to-all | bytes 8912896 | tf_op jit(solution)/shard_map/all_to_all | solution.py:300
  86.0 2.1 copy-done
  88.1 0.5 slice.88
  89.3 2.5 broadcast_in_dim.106
  91.8 4.6 %all-to-all-start.1 = ((bf16[16,128,1024]{2,1,0:T(8,128)(2,1)}), bf16[16,128,1024]{2,1,0:T(8,128)(2,1)}, u32[]{:S(2)}, u32[]{:S(2)}) async-start(bf16[16,128,1024]{2,1,0:T(8,128)(2,1)} %broadcast_in_dim.106), calls=%async_computation.1 | async-start | bytes 8388608 | tf_op jit(solution)/shard_map/all_to_all | solution.py:300
  96.4 0.0 reduce-scatter.3.cloned.1.call-start
  96.4 1.0 slice_convert_fusion
  97.4 0.3 copy.34
  97.8 0.8 copy.35
  98.5 15.1 %gather_rows.1.x_ref = bf16[32,256,1024]{2,1,0:T(8,128)(2,1)} custom-call(f32[16,32,128]{2,1,0:T(8,128)} %bitcast.44, bf16[16,136,1024]{2,1,0:T(8,128)(2,1)} %copy-done), custom_call_target="tpu_custom_call" | custom-call | flops 2147483648 | bytes 21233664 | tf_op jit(solution)/shard_map/gather_rows/pallas_call | solution.py:162
  113.6 35.1 %all-to-all-done.1.c_ref = bf16[16,128,1024]{2,1,0:T(8,128)(2,1)} async-done(((bf16[16,128,1024]{2,1,0:T(8,128)(2,1)}), bf16[16,128,1024]{2,1,0:T(8,128)(2,1)}, u32[]{:S(2)}, u32[]{:S(2)}) %all-to-all-start.1) | async-done | bytes 4194336 | tf_op jit(solution)/shard_map/all_to_all | solution.py:300
  148.7 1.2 slice.89
  150.6 0.1 add.59
  150.7 0.1 copy.25
  150.8 0.1 copy.26
  150.9 0.7 broadcast_in_dim.107.g_ref
  151.6 25.3 %forward_experts.1 = (bf16[16,128,1024]{2,1,0:T(8,128)(2,1)}, f32[32,256,176]{2,1,0:T(8,128)}) custom-call(bf16[32,264,1024]{2,1,0:T(8,128)(2,1)} %all-gather.2.cloned.1.call-done.w_ref, bf16[32,256,1024]{2,1,0:T(8,128)(2,1)} %gather_rows.1.x_ref, f32[32,8,256]{2,1,0:T(8,128)} %broadcast_in_dim.107.g_ref, f32[16,32,128]{2,1,0:T(8,128)} %bitcast.45), custom_call_target="tpu_custom_call" | custom-call | flops 4429185024 | bytes 34078720 | tf_op jit(solution)/shard_map/forward_experts/pallas_call | solution.py:186
  177.0 0.7 broadcast_in_dim.108.g_ref
  177.7 30.9 %backward_experts.1 = (bf16[4,4,136,512]{3,2,1,0:T(8,128)(2,1)}, bf16[4,4,128,512]{3,2,1,0:T(8,128)(2,1)}) custom-call(bf16[32,264,1024]{2,1,0:T(8,128)(2,1)} %all-gather.2.cloned.1.call-done.w_ref, f32[32,256,176]{2,1,0:T(8,128)} %get-tuple-element.8.pre_ref, f32[16,8,512]{2,1,0:T(8,128)} %broadcast_in_dim.108.g_ref, f32[16,32,128]{2,1,0:T(8,128)} %bitcast.46, ...), custom_call_target="tpu_custom_call" | custom-call | flops 4429185024 | bytes 23068672 | tf_op jit(solution)/shard_map/backward_experts/pallas_call | solution.py:221
  208.6 23.7 %all_to_all.26 = bf16[4,4,136,512]{3,2,1,0:T(8,128)(2,1)S(1)} all-to-all(bf16[4,4,136,512]{3,2,1,0:T(8,128)(2,1)} %get-tuple-element.9), channel_id=1, replica_groups={{0,32,64,96},{128,160,192,224},{256,288,320,352},{384,416,448,480},{1,3..., dimensions={0} | all-to-all | bytes 4456448 | tf_op jit(solution)/shard_map/all_to_all | solution.py:324
  232.3 0.5 slice.90
  233.5 0.0 reduce-scatter.3.cloned.1.call-done
  233.5 1.3 broadcast_add_fusion.1
  234.8 0.6 slice.92
  236.1 3.1 %broadcast_add_fusion = bf16[4,4,128,512]{3,2,1,0:T(8,128)(2,1)} fusion(bf16[4,4,128,512]{3,2,1,0:T(8,128)(2,1)} %get-tuple-element.10, bf16[]{:T(256)} %bitcast.17), kind=kLoop, calls=%fused_computation.7 | loop fusion | flops 1048576 | bytes 4194306 | tf_op jit(solution)/shard_map/add | solution.py:333
  239.1 4.6 %all-to-all-start.3 = ((bf16[4,4,128,512]{3,2,1,0:T(8,128)(2,1)}), bf16[4,4,128,512]{3,2,1,0:T(8,128)(2,1)}, u32[]{:S(2)}, u32[]{:S(2)}) async-start(bf16[4,4,128,512]{3,2,1,0:T(8,128)(2,1)} %broadcast_add_fusion), calls=%async_computation.5 | async-start | bytes 4194304 | tf_op jit(solution)/shard_map/all_to_all | solution.py:324
  243.8 0.0 reduce-scatter.5.cloned.1.call-start
  243.8 0.6 convert_element_type.48
  244.5 2.0 copy-done.1
  246.5 0.1 reshape.184
  246.6 0.1 reduce_sum.100
  246.7 0.0 reduce-scatter.5.cloned.1.call-update
  246.8 0.1 reshape.185
  246.9 2.7 slice_reduce_fusion
  249.6 16.4 %all-to-all-done.3 = bf16[4,4,128,512]{3,2,1,0:T(8,128)(2,1)} async-done(((bf16[4,4,128,512]{3,2,1,0:T(8,128)(2,1)}), bf16[4,4,128,512]{3,2,1,0:T(8,128)(2,1)}, u32[]{:S(2)}, u32[]{:S(2)}) %all-to-all-start.3) | async-done | bytes 2097184 | tf_op jit(solution)/shard_map/all_to_all | solution.py:324
  266.0 2.0 reduce
  268.1 0.1 fusion.1
  268.2 26.8 %all_to_all.27 = bf16[4,136,1024]{2,1,0:T(8,128)(2,1)S(1)} all-to-all(bf16[4,136,1024]{2,1,0:T(8,128)(2,1)S(1)} %fusion.1), channel_id=1, replica_groups={{0,128,256,384},{32,160,288,416},{64,192,320,448},{96,224,352,480},{1,1..., dimensions={0} | all-to-all | bytes 2228224 | tf_op jit(solution)/shard_map/all_to_all | solution.py:324
  295.0 0.1 reshape.186
  295.1 0.1 reduce_sum.103
  295.2 0.1 copy.30
  295.3 0.1 broadcast_in_dim.109
  295.4 0.3 convert_element_type.50
  295.7 0.2 select_reduce_fusion
  296.0 0.9 slice_reduce_fusion.1
  296.8 0.6 bitcast_divide_fusion
  (33 shorter events, 0.4 us)
Async XLA Ops:
  7.2 143.7 %all-gather.2.cloned.1.call-start = ((), (), s32[]{:S(2)}) async-start(), calls=%async_computation.7 | async-start | bytes 17842176 | tf_op jit(solution)/shard_map/all_gather | solution.py:269
  8.5 15.5 %copy-start.5 = (s32[128,6]{0,1:T(8,128)S(1)}, s32[128,6]{0,1:T(8,128)}, u32[]{:S(2)}) copy-start(s32[128,6]{0,1:T(8,128)} %param.7) | copy-start | bytes 9220
  8.5 15.5 %copy-start.6 = (f32[128,6]{0,1:T(8,128)S(1)}, f32[128,6]{0,1:T(8,128)}, u32[]{:S(2)}) copy-start(f32[128,6]{0,1:T(8,128)} %param.8) | copy-start | bytes 9220
  10.3 12.0 %collective-permute-start = (bf16[3,44,1024]{2,0,1:T(4,128)(2,1)S(1)}, bf16[3,44,1024]{2,0,1:T(4,128)(2,1)S(1)}, u32[]{:S(2)}, u32[]{:S(2)}) collective-permute-start(bf16[3,44,1024]{2,0,1:T(4,128)(2,1)S(1)} %pad_maximum_fusion.2), channel_id=1, source_target_pairs={{0,128},{32,160},{64,192},{96,224},{128,0},{160,32},{192,64},{224,... | collective-permute-start | bytes 811016 | tf_op jit(solution)/shard_map/ppermute | solution.py:267
  22.4 2.8 copy-start.3
  26.4 62.9 %copy-start.4 = (bf16[128,1024]{1,0:T(8,128)(2,1)S(1)}, bf16[128,1024]{1,0:T(8,128)(2,1)}, u32[]{:S(2)}) copy-start(bf16[128,1024]{1,0:T(8,128)(2,1)} %param.11) | copy-start | bytes 786436
  86.0 2.1 copy-start
  91.8 56.9 %all-to-all-start.1 = ((bf16[16,128,1024]{2,1,0:T(8,128)(2,1)}), bf16[16,128,1024]{2,1,0:T(8,128)(2,1)}, u32[]{:S(2)}, u32[]{:S(2)}) async-start(bf16[16,128,1024]{2,1,0:T(8,128)(2,1)} %broadcast_in_dim.106), calls=%async_computation.1 | async-start | bytes 8388608 | tf_op jit(solution)/shard_map/all_to_all | solution.py:300
  96.4 137.1 %reduce-scatter.3.cloned.1.call-start = ((), (), s32[]{:S(2)}) async-start(), calls=%async_computation.8 | async-start | bytes 5242880 | tf_op jit(solution)/shard_map/reduce_scatter | solution.py:319
  234.8 4.3 %copy-start.2 = (bf16[512,1024]{1,0:T(8,128)(2,1)}, bf16[512,1024]{1,0:T(8,128)(2,1)S(1)}, u32[]{:S(2)}) copy-start(bf16[512,1024]{1,0:T(8,128)(2,1)S(1)} %broadcast_add_fusion.1) | copy-start | bytes 3145732
  239.1 26.9 %all-to-all-start.3 = ((bf16[4,4,128,512]{3,2,1,0:T(8,128)(2,1)}), bf16[4,4,128,512]{3,2,1,0:T(8,128)(2,1)}, u32[]{:S(2)}, u32[]{:S(2)}) async-start(bf16[4,4,128,512]{3,2,1,0:T(8,128)(2,1)} %broadcast_add_fusion), calls=%async_computation.5 | async-start | bytes 4194304 | tf_op jit(solution)/shard_map/all_to_all | solution.py:324
  243.8 53.7 %reduce-scatter.5.cloned.1.call-start = ((), (), s32[]{:S(2)}) async-start(), calls=%async_computation.9 | async-start | bytes 1310720 | tf_op jit(solution)/shard_map/reduce_scatter | solution.py:319
  244.4 2.0 copy-start.1
Sparse Core Ops, SparseCore 0:
  24.1 106.4 all-gather.1
  177.1 51.9 reduce-scatter.2
  248.3 33.8 reduce-scatter.4

commit v6 on v5

--- a/solution.py
+++ b/solution.py
@@ -34,23 +34,18 @@
     slots_ref[:, pl.ds(at, SLOTS), :] = rows.reshape(slots_ref.shape[0], SLOTS, rows.shape[1])
 
 
-def combine(rank_ref, slots_ref, *out_refs):
+def combine(rank_ref, slots_ref, out_ref):
     sources, half, tok = rank_ref.shape
     slot = slot_numbers(half, tok)
 
     def one(s, carry):
         place = one_hot(rank_ref[s], slot)
         sums = lax.dot_general(place, slots_ref[s], TN, preferred_element_type=jnp.float32)
-        start = 0
-        for out_ref in out_refs:
-            stop = start + out_ref.shape[-1]
-            part = sums[:, start:stop].astype(out_ref.dtype)
-            if len(out_ref.shape) == 3:
-                out_ref[s, 0:tok, :] = part
-            else:
-                side = out_ref.shape[0]
-                out_ref[lax.rem(s, side), lax.div(s, side), 0:tok, :] = part
-            start = stop
+        if len(out_ref.shape) == 3:
+            out_ref[s] = sums.astype(out_ref.dtype)
+        else:
+            side = out_ref.shape[0]
+            out_ref[lax.rem(s, side), lax.div(s, side), 0:tok, :] = sums.astype(out_ref.dtype)
         return carry
 
     lax.fori_loop(0, sources, one, 0)
@@ -84,9 +79,7 @@
         combine(rank_ref, slots, out_ref)
 
 
-def backward_kernel(
-    w_ref, pre_ref, g_ref, rank_ref, c_ref, out_ref, more_ref, slots, dots
-):
+def backward_kernel(w_ref, pre_ref, g_ref, rank_ref, c_ref, out_ref, slots, dots):
     hidden = w_ref.shape[1] // 3
     first = pl.program_id(0) * STEP
     sources, tok, model = c_ref.shape
@@ -128,7 +121,7 @@
 
     @pl.when(first + STEP == half)
     def _():
-        combine(rank_ref, slots, out_ref, more_ref)
+        combine(rank_ref, slots, out_ref)
         low_rows, side = SLOTS // 2, out_ref.shape[0]
 
         def one(s, carry):
@@ -228,21 +221,15 @@
             pl.BlockSpec((sources, half, tok), whole),
             pl.BlockSpec((sources, tok, model), whole),
         ],
-        out_specs=[
-            pl.BlockSpec((side, sources // side, out_rows, model // 2), lambda e: (0, 0, 0, 0)),
-            pl.BlockSpec((side, sources // side, tok, model // 2), lambda e: (0, 0, 0, 0)),
-        ],
-        out_shape=[
-            jax.ShapeDtypeStruct((side, sources // side, out_rows, model // 2), jnp.bfloat16),
-            jax.ShapeDtypeStruct((side, sources // side, tok, model // 2), jnp.bfloat16),
-        ],
+        out_specs=pl.BlockSpec((side, sources // side, out_rows, model), lambda e: (0, 0, 0, 0)),
+        out_shape=jax.ShapeDtypeStruct((side, sources // side, out_rows, model), jnp.bfloat16),
         scratch_shapes=[
             pltpu.VMEM((sources, half * SLOTS, model), jnp.bfloat16),
             pltpu.VMEM((rows, 128), jnp.float32),
         ],
         compiler_params=params(),
         cost_estimate=pl.CostEstimate(
-            flops=6 * half * rows * (w_rows // 3) * model,
+            flops=60 * half * rows * (w_rows // 3) * model,
             bytes_accessed=2 * (weights.size + 2 * pre.size),
             transcendentals=half * rows * (w_rows // 3),
         ),
@@ -299,7 +286,7 @@
     spread = lambda a: jnp.broadcast_to(a[None], (planes, tok, model))
     swap_rows = lambda a: lax.all_to_all(a, "dp", split_axis=0, concat_axis=0, tiled=True)
     rows = swap_rows(jnp.concatenate([spread(tokens), known], axis=1))
-    cotangents = swap_rows(spread(cotangent + 0.0 * rows[0, 0, 0]))
+    cotangents = swap_rows(spread(cotangent))
 
     facts_in = rows[:, tok:, :].reshape(planes, fact_rows * model).astype(jnp.float32)
     first, second = half * tok, half * tok + half * SLOTS
@@ -309,7 +296,6 @@
     scales = scales.reshape(planes, half, SLOTS).swapaxes(0, 1).reshape(half, 1, planes * SLOTS)
     scales = jnp.broadcast_to(scales, (half, 8, planes * SLOTS))
 
-    scales = scales + 0.0 * cotangents[0, 0, 0].astype(jnp.float32)
     x_rows = gather_rows(ranks, rows)
     layer_part, pre = forward(weights, x_rows, scales, ranks)
     along_x = [[x * side + y for x in range(planes // side)] for y in range(side)]
@@ -326,20 +312,17 @@
         )
 
     layer_x = reduce_rows(layer_part.reshape(planes * tok, model), along_x)
-    first_part, second_part = backward(weights, pre, by_source, ranks, cotangents, side)
-    first_in = swap_along(first_part, along_y)
-    layer_x = layer_x + 0.0 * first_in[0, 0, 0, 0]
+    grad_part = backward(weights, pre, by_source, ranks, cotangents, side)
     layer_output = reduce_rows(layer_x, along_y)
-    second_in = swap_along(second_part + 0.0 * layer_x[0, 0], along_y)
-
-    first_in = first_in.astype(jnp.float32)
-    dots = jnp.sum(first_in[:, :, tok:, 0 : 4 * half], axis=0)
+    grad_in = swap_along(grad_part, along_y).astype(jnp.float32)
+
+    dots = jnp.sum(grad_in[:, :, tok:, 0 : 4 * half], axis=0)
     dots = jnp.sum(dots.reshape(-1, SLOTS // 2, 2, 2, half), axis=3)
     high = lax.reduce_precision(dots, 8, 7)
     dots = jnp.stack([high, dots - high], axis=3).reshape(-1, SLOTS // 2, 4 * half)
     dots = jnp.pad(dots, ((0, 0), (0, 0), (0, model - 4 * half)))
-    halves = [first_in[:, :, 0:tok], second_in.astype(jnp.float32)]
-    grad_sums = jnp.concatenate([jnp.sum(a, axis=0) for a in halves], axis=2)
+    dots = dots + 0.0 * layer_output[0, 0].astype(jnp.float32)
+    grad_sums = jnp.sum(grad_in[:, :, 0:tok], axis=0)
     grad_in = jnp.concatenate([grad_sums, dots], axis=1).astype(jnp.bfloat16)
     grad_in = swap_along(grad_in, along_x).astype(jnp.float32)
     token_grads = jnp.sum(grad_in[:, 0:tok], axis=0).astype(jnp.bfloat16)

time: 305 us -> 304 us (level)
  the two profiles are of different devices: /device:TPU:416 before, /device:TPU:1 now
where the time goes in v6:
time: 304 us; the launch traced here: 303 us
  waiting for transfers between devices  94.3 us (31%)
  blocking collectives  80.1 us (26%)
  Pallas kernels  71.3 us (23%)
  local copies, waits for them, and re-layouts  15.5 us (5%)
  between operations  14.8 us (5%)
  starting transfers between devices  13.7 us (5%)
  other arithmetic  13.1 us (4%)
    all_to_all x1, blocking collectives, body(): lax.all_to_all(a, 'dp', split_axis=0, concat_axis=0, tiled=True)  61.1 us
    all_to_all x1, waiting for transfers between devices, swap_along(): lax.all_to_all(a, 'dp', split_axis=0, concat_axis=0, axis_index_groups=gr...  43.8 us
    pallas_call x1, Pallas kernels, backward(): pl.pallas_call(backward_kernel, grid=(half // STEP,), in_specs=[pl.BlockS...  30.9 us
    all_gather x1, waiting for transfers between devices, body(): weights = lax.all_gather(mine, 'expert', axis=0, tiled=False)  30.3 us
    pallas_call x1, Pallas kernels, forward(): pl.pallas_call(forward_kernel, grid=(half // STEP,), in_specs=[pl.BlockSp...  25.3 us
    all_to_all x1, blocking collectives, swap_along(): lax.all_to_all(a, 'dp', split_axis=0, concat_axis=0, axis_index_groups=gr...  19 us
    reduce_scatter x2, waiting for transfers between devices, reduce_rows(): lax.psum_scatter(a, 'dp', scatter_dimension=0, axis_index_groups=groups,...  15.4 us
    pallas_call x1, Pallas kernels, gather_rows(): pl.pallas_call(gather_kernel, grid=(sources,), in_specs=[pl.BlockSpec((1,...  15.1 us
  transfers between devices with their start and end apart: 6, of which 4 were waited for; matrix products, arithmetic and copies ran while one was open for 6% of the time, Pallas kernels for 24%

profile of v6, /device:TPU:1, one launch (start us, length us, event | category | flops | bytes accessed | tf_op | source)
XLA Modules:
  0.0 302.9 jit_solution(17563743221829158256)
XLA Ops:
  7.2 0.0 copy-start.3
  7.2 0.0 copy-start.4
  7.2 0.0 all-gather.2.cloned.1.call-start
  7.3 1.3 dynamic-slice_bitcast_fusion.1
  8.6 1.4 constant_dynamic-slice_fusion.1
  10.0 0.4 pad_maximum_fusion.3
  10.3 3.9 %collective-permute-start = (bf16[3,44,1024]{2,0,1:T(4,128)(2,1)S(1)}, bf16[3,44,1024]{2,0,1:T(4,128)(2,1)S(1)}, u32[]{:S(2)}, u32[]{:S(2)}) collective-permute-start(bf16[3,44,1024]{2,0,1:T(4,128)(2,1)S(1)} %pad_maximum_fusion.3), channel_id=1, source_target_pairs={{0,128},{32,160},{64,192},{96,224},{128,0},{160,32},{192,64},{224,... | collective-permute-start | bytes 811016 | tf_op jit(solution)/shard_map/ppermute | solution.py:254
  14.3 4.8 %collective-permute-done = bf16[3,44,1024]{2,0,1:T(4,128)(2,1)S(1)} collective-permute-done((bf16[3,44,1024]{2,0,1:T(4,128)(2,1)S(1)}, bf16[3,44,1024]{2,0,1:T(4,128)(2,1)S(1)}, u32[]{:S(2)}, u32[]{:S(2)}) %collective-permute-start) | collective-permute-done | bytes 270368 | tf_op jit(solution)/shard_map/ppermute | solution.py:254
  19.1 0.5 pad_maximum_fusion.2
  19.6 1.0 copy.24
  20.7 0.0 all-gather.2.cloned.1.call-update
  20.8 0.1 fusion.15
  20.9 0.2 select_reduce_fusion.1
  21.2 0.2 slice_reduce_fusion.5
  21.4 0.1 concatenate.54
  21.5 0.1 concatenate.55
  21.6 0.1 concatenate.58
  21.6 0.1 concatenate.59
  21.8 0.1 fusion.12
  21.9 0.5 broadcast_in_dim.98
  22.4 0.7 pad_maximum_fusion
  23.2 0.0 copy-start.2
  23.2 61.1 %all_to_all.20.rows_ref = bf16[16,136,1024]{2,1,0:T(8,128)(2,1)} all-to-all(bf16[16,136,1024]{2,1,0:T(8,128)(2,1)S(1)} %pad_maximum_fusion), channel_id=1, replica_groups=mesh['dp'=16,'expert'=32] {'dp'}, dimensions={0} | all-to-all | bytes 8912896 | tf_op jit(solution)/shard_map/all_to_all | solution.py:287
  84.3 2.6 broadcast_in_dim.111
  86.9 4.6 %all-to-all-start.1 = ((bf16[16,128,1024]{2,1,0:T(8,128)(2,1)}), bf16[16,128,1024]{2,1,0:T(8,128)(2,1)}, u32[]{:S(2)}, u32[]{:S(2)}) async-start(bf16[16,128,1024]{2,1,0:T(8,128)(2,1)} %broadcast_in_dim.111), calls=%async_computation.3 | async-start | bytes 8388608 | tf_op jit(solution)/shard_map/all_to_all | solution.py:287
  91.4 0.0 reduce-scatter.3.cloned.1.call-start
  91.5 1.0 slice_convert_fusion
  92.5 0.3 copy.34
  92.8 0.8 copy.35
  93.6 0.1 reshape.174
  93.7 0.1 copy.25
  93.8 0.1 copy.26
  93.9 15.1 %gather_rows.1.x_ref = bf16[32,256,1024]{2,1,0:T(8,128)(2,1)} custom-call(f32[16,32,128]{2,1,0:T(8,128)} %bitcast.43, bf16[16,136,1024]{2,1,0:T(8,128)(2,1)} %all_to_all.20.rows_ref), custom_call_target="tpu_custom_call" | custom-call | flops 2147483648 | bytes 21233664 | tf_op jit(solution)/shard_map/gather_rows/pallas_call | solution.py:155
  109.0 30.3 %all-gather.2.cloned.1.call-done.w_ref = bf16[32,264,1024]{2,1,0:T(8,128)(2,1)} async-done(((bf16[1,264,1024]{2,1,0:T(8,128)(2,1)}), bf16[32,264,1024]{2,1,0:T(8,128)(2,1)}) %all-gather.2.cloned.1.call-update) | async-done | bytes 17301520 | tf_op jit(solution)/shard_map/all_gather | solution.py:256
  139.3 0.7 broadcast_in_dim.109.g_ref
  140.0 25.3 %forward_experts.1 = (bf16[16,128,1024]{2,1,0:T(8,128)(2,1)}, f32[32,256,176]{2,1,0:T(8,128)}) custom-call(bf16[32,264,1024]{2,1,0:T(8,128)(2,1)} %all-gather.2.cloned.1.call-done.w_ref, bf16[32,256,1024]{2,1,0:T(8,128)(2,1)} %gather_rows.1.x_ref, f32[32,8,256]{2,1,0:T(8,128)} %broadcast_in_dim.109.g_ref, f32[16,32,128]{2,1,0:T(8,128)} %bitcast.44), custom_call_target="tpu_custom_call" | custom-call | flops 4429185024 | bytes 34078720 | tf_op jit(solution)/shard_map/forward_experts/pallas_call | solution.py:179
  165.3 0.0 reduce-scatter.3.cloned.1.call-update
  165.3 0.0 all-to-all-done.1.c_ref
  165.4 0.7 broadcast_in_dim.110.g_ref
  166.1 30.9 %backward_experts.1 = bf16[4,4,136,1024]{3,2,1,0:T(8,128)(2,1)} custom-call(bf16[32,264,1024]{2,1,0:T(8,128)(2,1)} %all-gather.2.cloned.1.call-done.w_ref, f32[32,256,176]{2,1,0:T(8,128)} %get-tuple-element.6.pre_ref, f32[16,8,512]{2,1,0:T(8,128)} %broadcast_in_dim.110.g_ref, f32[16,32,128]{2,1,0:T(8,128)} %bitcast.45, ...), custom_call_target="tpu_custom_call" | custom-call | flops 44291850240 | bytes 23068672 | tf_op jit(solution)/shard_map/backward_experts/pallas_call | solution.py:214
  197.0 4.9 %all-to-all-start.2 = ((bf16[4,4,136,1024]{3,2,1,0:T(8,128)(2,1)}), bf16[4,4,136,1024]{3,2,1,0:T(8,128)(2,1)}, u32[]{:S(2)}, u32[]{:S(2)}) async-start(bf16[4,4,136,1024]{3,2,1,0:T(8,128)(2,1)} %backward_experts.1), calls=%async_computation.4 | async-start | bytes 8912896 | tf_op jit(solution)/shard_map/all_to_all | solution.py:310
  201.9 0.2 reduce-scatter.5.cloned.1.call-start
  202.1 15.4 %reduce-scatter.3.cloned.1.call-done = bf16[512,1024]{1,0:T(8,128)(2,1)} async-done(((bf16[2048,1024]{1,0:T(8,128)(2,1)}), bf16[512,1024]{1,0:T(8,128)(2,1)}) %reduce-scatter.3.cloned.1.call-update) | async-done | bytes 1048592 | tf_op jit(solution)/shard_map/reduce_scatter | solution.py:305
  217.5 0.0 reduce-scatter.5.cloned.1.call-update
  217.5 43.8 %all-to-all-done.2 = bf16[4,4,136,1024]{3,2,1,0:T(8,128)(2,1)} async-done(((bf16[4,4,136,1024]{3,2,1,0:T(8,128)(2,1)}), bf16[4,4,136,1024]{3,2,1,0:T(8,128)(2,1)}, u32[]{:S(2)}, u32[]{:S(2)}) %all-to-all-start.2) | async-done | bytes 4456480 | tf_op jit(solution)/shard_map/all_to_all | solution.py:310
  261.3 3.3 %convert_element_type.44 = f32[4,4,136,1024]{3,2,1,0:T(8,128)S(1)} convert(bf16[4,4,136,1024]{3,2,1,0:T(8,128)(2,1)} %all-to-all-done.2) | non-fusion elementwise | flops 2228224 | bytes 13369344 | tf_op jit(solution)/shard_map/convert_element_type | solution.py:317
  264.6 3.4 %copy-done = f32[4,4,136,1024]{3,2,1,0:T(8,128)} copy-done((f32[4,4,136,1024]{3,2,1,0:T(8,128)}, f32[4,4,136,1024]{3,2,1,0:T(8,128)S(1)}, u32[]{:S(2)}) %copy-start) | copy-done | bytes 8912920
  268.0 0.1 reshape.176
  268.2 0.1 reduce_sum.90
  268.3 0.1 copy.28
  268.4 0.1 reshape.177
  268.5 4.5 %slice_reduce_fusion = bf16[4,128,1024]{2,1,0:T(8,128)(2,1)S(1)} fusion(f32[4,4,136,1024]{3,2,1,0:T(8,128)} %copy-done), kind=kLoop, calls=%fused_computation | loop fusion | flops 1572864 | bytes 9437184 | tf_op jit(solution)/shard_map/reduce_sum | solution.py:325
  273.0 0.0 reduce-scatter.5.cloned.1.call-done
  273.0 1.2 slice.78
  274.9 0.1 pad_maximum_fusion.1
  275.0 19.0 %all_to_all.21 = bf16[4,136,1024]{2,1,0:T(8,128)(2,1)S(1)} all-to-all(bf16[4,136,1024]{2,1,0:T(8,128)(2,1)S(1)} %pad_maximum_fusion.1), channel_id=1, replica_groups={{0,128,256,384},{32,160,288,416},{64,192,320,448},{96,224,352,480},{1,1..., dimensions={0} | all-to-all | bytes 2228224 | tf_op jit(solution)/shard_map/all_to_all | solution.py:310
  294.0 0.3 convert_element_type.46
  294.2 0.9 slice_reduce_fusion.1
  295.1 0.1 reshape.178
  295.3 0.1 reduce_sum.93
  295.3 0.1 copy.30
  295.4 0.1 broadcast_in_dim.112
  295.5 0.2 select_reduce_fusion
  295.8 0.6 bitcast_divide_fusion
  (22 shorter events, 0.3 us)
Async XLA Ops:
  7.2 13.5 %copy-start.3 = (s32[128,6]{0,1:T(8,128)S(1)}, s32[128,6]{0,1:T(8,128)}, u32[]{:S(2)}) copy-start(s32[128,6]{0,1:T(8,128)} %param.7) | copy-start | bytes 9220
  7.2 13.6 %copy-start.4 = (f32[128,6]{0,1:T(8,128)S(1)}, f32[128,6]{0,1:T(8,128)}, u32[]{:S(2)}) copy-start(f32[128,6]{0,1:T(8,128)} %param.8) | copy-start | bytes 9220
  7.2 14.7 %copy-start.1 = (bf16[128,1024]{1,0:T(8,128)(2,1)S(1)}, bf16[128,1024]{1,0:T(8,128)(2,1)}, u32[]{:S(2)}) copy-start(bf16[128,1024]{1,0:T(8,128)(2,1)} %param.6) | copy-start | bytes 786436
  7.2 132.1 %all-gather.2.cloned.1.call-start = ((), (), s32[]{:S(2)}) async-start(), calls=%async_computation.6 | async-start | bytes 17842176 | tf_op jit(solution)/shard_map/all_gather | solution.py:256
  10.3 8.8 %collective-permute-start = (bf16[3,44,1024]{2,0,1:T(4,128)(2,1)S(1)}, bf16[3,44,1024]{2,0,1:T(4,128)(2,1)S(1)}, u32[]{:S(2)}, u32[]{:S(2)}) collective-permute-start(bf16[3,44,1024]{2,0,1:T(4,128)(2,1)S(1)} %pad_maximum_fusion.3), channel_id=1, source_target_pairs={{0,128},{32,160},{64,192},{96,224},{128,0},{160,32},{192,64},{224,... | collective-permute-start | bytes 811016 | tf_op jit(solution)/shard_map/ppermute | solution.py:254
  23.2 61.1 %copy-start.2 = (bf16[128,1024]{1,0:T(8,128)(2,1)S(1)}, bf16[128,1024]{1,0:T(8,128)(2,1)}, u32[]{:S(2)}) copy-start(bf16[128,1024]{1,0:T(8,128)(2,1)} %param.11) | copy-start | bytes 786436
  86.9 78.5 %all-to-all-start.1 = ((bf16[16,128,1024]{2,1,0:T(8,128)(2,1)}), bf16[16,128,1024]{2,1,0:T(8,128)(2,1)}, u32[]{:S(2)}, u32[]{:S(2)}) async-start(bf16[16,128,1024]{2,1,0:T(8,128)(2,1)} %broadcast_in_dim.111), calls=%async_computation.3 | async-start | bytes 8388608 | tf_op jit(solution)/shard_map/all_to_all | solution.py:287
  91.4 126.0 %reduce-scatter.3.cloned.1.call-start = ((), (), s32[]{:S(2)}) async-start(), calls=%async_computation.7 | async-start | bytes 5242880 | tf_op jit(solution)/shard_map/reduce_scatter | solution.py:305
  197.0 64.3 %all-to-all-start.2 = ((bf16[4,4,136,1024]{3,2,1,0:T(8,128)(2,1)}), bf16[4,4,136,1024]{3,2,1,0:T(8,128)(2,1)}, u32[]{:S(2)}, u32[]{:S(2)}) async-start(bf16[4,4,136,1024]{3,2,1,0:T(8,128)(2,1)} %backward_experts.1), calls=%async_computation.4 | async-start | bytes 8912896 | tf_op jit(solution)/shard_map/all_to_all | solution.py:310
  201.9 71.1 %reduce-scatter.5.cloned.1.call-start = ((), (), s32[]{:S(2)}) async-start(), calls=%async_computation.8 | async-start | bytes 1310720 | tf_op jit(solution)/shard_map/reduce_scatter | solution.py:305
  264.6 3.4 %copy-start = (f32[4,4,136,1024]{3,2,1,0:T(8,128)}, f32[4,4,136,1024]{3,2,1,0:T(8,128)S(1)}, u32[]{:S(2)}) copy-start(f32[4,4,136,1024]{3,2,1,0:T(8,128)S(1)} %convert_element_type.44) | copy-start | bytes 26738692
Sparse Core Ops, SparseCore 0:
  20.8 118.4 all-gather.1
  165.5 51.9 reduce-scatter.2
  221.1 37.6 reduce-scatter.4

commit v7 on v4

--- a/solution.py
+++ b/solution.py
@@ -224,7 +224,7 @@
         ],
         compiler_params=params(),
         cost_estimate=pl.CostEstimate(
-            flops=6 * half * rows * (w_rows // 3) * model,
+            flops=60 * half * rows * (w_rows // 3) * model,
             bytes_accessed=2 * (weights.size + 2 * pre.size),
             transcendentals=half * rows * (w_rows // 3),
         ),
@@ -293,10 +293,15 @@
 
     x_rows = gather_rows(ranks, rows)
     layer_part, pre = forward(weights, x_rows, scales, ranks)
-    layer_output = lax.psum_scatter(
-        layer_part.reshape(planes * tok, model), "dp", scatter_dimension=0, tiled=True
-    )
-    grad_in = swap_rows(backward(weights, pre, by_source, ranks, cotangents)).astype(jnp.float32)
+    along_x = [[x * side + y for x in range(planes // side)] for y in range(side)]
+    along_y = [[x * side + y for y in range(side)] for x in range(planes // side)]
+    grad_part = backward(weights, pre, by_source, ranks, cotangents)
+    layer_output = layer_part.reshape(planes * tok, model)
+    for groups in (along_x, along_y):
+        layer_output = lax.psum_scatter(
+            layer_output, "dp", scatter_dimension=0, axis_index_groups=groups, tiled=True
+        )
+    grad_in = swap_rows(grad_part).astype(jnp.float32)
     token_grads = jnp.sum(grad_in[:, 0:tok], axis=0).astype(jnp.bfloat16)
 
     dots = grad_in[:, tok:, 0 : 4 * half].reshape(2, 2, side, SLOTS // 2, 2, 2, half)

time: 298 us -> 294 us (0.987)
  the two profiles are of different devices: /device:TPU:1 before, /device:TPU:48 now
where the time goes in v7:
time: 294 us; the launch traced here: 293 us
  waiting for transfers between devices  112 us (38%)
  Pallas kernels  72 us (24%)
  blocking collectives  57.9 us (20%)
  starting transfers between devices  17.3 us (6%)
  between operations  14 us (5%)
  local copies, waits for them, and re-layouts  11.5 us (4%)
  other arithmetic  8.89 us (3%)
    all_to_all x1, blocking collectives, body(): lax.all_to_all(a, 'dp', split_axis=0, concat_axis=0, tiled=True)  57.9 us
    all_to_all x2, waiting for transfers between devices, body(): lax.all_to_all(a, 'dp', split_axis=0, concat_axis=0, tiled=True)  41.4 us
    reduce_scatter x2, waiting for transfers between devices, body(): lax.psum_scatter(layer_output, 'dp', scatter_dimension=0, axis_index_grou...  37.5 us
    pallas_call x1, Pallas kernels, backward(): pl.pallas_call(backward_kernel, grid=(half // STEP,), in_specs=[pl.BlockS...  31.6 us
    pallas_call x1, Pallas kernels, forward(): pl.pallas_call(forward_kernel, grid=(half // STEP,), in_specs=[pl.BlockSp...  25.3 us
    all_gather x1, waiting for transfers between devices, body(): weights = lax.all_gather(mine, 'expert', axis=0, tiled=False)  24.1 us
    pallas_call x1, Pallas kernels, gather_rows(): pl.pallas_call(gather_kernel, grid=(sources,), in_specs=[pl.BlockSpec((1,...  15.1 us
    all_to_all x2, starting transfers between devices, body(): lax.all_to_all(a, 'dp', split_axis=0, concat_axis=0, tiled=True)  13.6 us
  transfers between devices with their start and end apart: 6, of which 4 were waited for; matrix products, arithmetic and copies ran while one was open for 5% of the time, Pallas kernels for 25%

profile of v7, /device:TPU:48, one launch (start us, length us, event | category | flops | bytes accessed | tf_op | source)
XLA Modules:
  0.0 293.5 jit_solution(353333806409560632)
XLA Ops:
  7.2 0.0 copy-start.2
  7.2 0.0 copy-start.3
  7.2 0.0 copy-start
  7.2 0.0 all-gather.2.cloned.1.call-start
  7.3 1.3 dynamic-slice_bitcast_fusion.1
  8.6 1.4 constant_dynamic-slice_fusion.1
  10.0 0.4 pad_maximum_fusion.2
  10.3 3.4 %collective-permute-start = (bf16[3,44,1024]{2,0,1:T(4,128)(2,1)S(1)}, bf16[3,44,1024]{2,0,1:T(4,128)(2,1)S(1)}, u32[]{:S(2)}, u32[]{:S(2)}) collective-permute-start(bf16[3,44,1024]{2,0,1:T(4,128)(2,1)S(1)} %pad_maximum_fusion.2), channel_id=1, source_target_pairs={{0,128},{32,160},{64,192},{96,224},{128,0},{160,32},{192,64},{224,... | collective-permute-start | bytes 811016 | tf_op jit(solution)/shard_map/ppermute | solution.py:249
  13.7 8.6 %collective-permute-done = bf16[3,44,1024]{2,0,1:T(4,128)(2,1)S(1)} collective-permute-done((bf16[3,44,1024]{2,0,1:T(4,128)(2,1)S(1)}, bf16[3,44,1024]{2,0,1:T(4,128)(2,1)S(1)}, u32[]{:S(2)}, u32[]{:S(2)}) %collective-permute-start) | collective-permute-done | bytes 270368 | tf_op jit(solution)/shard_map/ppermute | solution.py:249
  22.4 0.5 pad_maximum_fusion.1
  22.9 1.0 copy.22
  24.0 0.0 all-gather.2.cloned.1.call-update
  24.0 0.0 copy-done.2
  24.0 0.0 copy-done.3
  24.1 0.1 fusion.13
  24.2 0.2 select_reduce_fusion.1
  24.5 0.2 slice_reduce_fusion.3
  24.7 0.1 concatenate.50
  24.8 0.1 concatenate.51
  24.8 0.1 concatenate.54
  24.9 0.1 concatenate.55
  25.1 0.1 fusion.12
  25.2 0.0 copy-done
  25.2 0.5 broadcast_in_dim.98
  25.7 0.7 pad_maximum_fusion
  26.4 0.0 copy-start.1
  26.5 57.9 %all_to_all.15.rows_ref = bf16[16,136,1024]{2,1,0:T(8,128)(2,1)} all-to-all(bf16[16,136,1024]{2,1,0:T(8,128)(2,1)S(1)} %pad_maximum_fusion), channel_id=1, replica_groups=mesh['dp'=16,'expert'=32] {'dp'}, dimensions={0} | all-to-all | bytes 8912896 | tf_op jit(solution)/shard_map/all_to_all | solution.py:282
  84.4 0.0 copy-done.1
  84.4 2.6 broadcast_in_dim.111
  87.0 6.3 %all-to-all-start.1 = ((bf16[16,128,1024]{2,1,0:T(8,128)(2,1)}), bf16[16,128,1024]{2,1,0:T(8,128)(2,1)}, u32[]{:S(2)}, u32[]{:S(2)}) async-start(bf16[16,128,1024]{2,1,0:T(8,128)(2,1)} %broadcast_in_dim.111), calls=%async_computation.3 | async-start | bytes 8388608 | tf_op jit(solution)/shard_map/all_to_all | solution.py:282
  93.3 0.0 reduce-scatter.3.cloned.1.call-start
  93.4 1.0 slice_convert_fusion
  94.4 0.3 copy.27
  94.7 0.8 copy.28
  95.5 0.1 reshape.151
  95.6 0.1 copy.23
  95.7 0.1 copy.24
  95.8 15.1 %gather_rows.1.x_ref = bf16[32,256,1024]{2,1,0:T(8,128)(2,1)} custom-call(f32[16,32,128]{2,1,0:T(8,128)} %bitcast.32, bf16[16,136,1024]{2,1,0:T(8,128)(2,1)} %all_to_all.15.rows_ref), custom_call_target="tpu_custom_call" | custom-call | flops 2147483648 | bytes 21233664 | tf_op jit(solution)/shard_map/gather_rows/pallas_call | solution.py:150
  110.9 24.1 %all-gather.2.cloned.1.call-done.w_ref = bf16[32,264,1024]{2,1,0:T(8,128)(2,1)} async-done(((bf16[1,264,1024]{2,1,0:T(8,128)(2,1)}), bf16[32,264,1024]{2,1,0:T(8,128)(2,1)}) %all-gather.2.cloned.1.call-update) | async-done | bytes 17301520 | tf_op jit(solution)/shard_map/all_gather | solution.py:251
  135.0 0.7 broadcast_in_dim.109.g_ref
  135.7 25.3 %forward_experts.1 = (bf16[16,128,1024]{2,1,0:T(8,128)(2,1)}, f32[32,256,176]{2,1,0:T(8,128)}) custom-call(bf16[32,264,1024]{2,1,0:T(8,128)(2,1)} %all-gather.2.cloned.1.call-done.w_ref, bf16[32,256,1024]{2,1,0:T(8,128)(2,1)} %gather_rows.1.x_ref, f32[32,8,256]{2,1,0:T(8,128)} %broadcast_in_dim.109.g_ref, f32[16,32,128]{2,1,0:T(8,128)} %bitcast.33), custom_call_target="tpu_custom_call" | custom-call | flops 4429185024 | bytes 34078720 | tf_op jit(solution)/shard_map/forward_experts/pallas_call | solution.py:174
  161.0 0.0 reduce-scatter.3.cloned.1.call-update
  161.1 0.0 all-to-all-done.1.c_ref
  161.1 0.7 broadcast_in_dim.110.g_ref
  161.8 31.6 %backward_experts.1 = bf16[16,136,1024]{2,1,0:T(8,128)(2,1)} custom-call(bf16[32,264,1024]{2,1,0:T(8,128)(2,1)} %all-gather.2.cloned.1.call-done.w_ref, f32[32,256,176]{2,1,0:T(8,128)} %get-tuple-element.6.pre_ref, f32[16,8,512]{2,1,0:T(8,128)} %broadcast_in_dim.110.g_ref, f32[16,32,128]{2,1,0:T(8,128)} %bitcast.34, bf16[16,128,1024]{2,1,0:T(8,128)(2,1)} %all-to-all-done.1.c_ref), custom_call_target="tpu_custom_call" | custom-call | flops 44291850240 | bytes 23068672 | tf_op jit(solution)/shard_map/backward_experts/pallas_call | solution.py:209
  193.4 7.2 %all-to-all-start.2 = ((bf16[16,136,1024]{2,1,0:T(8,128)(2,1)}), bf16[16,136,1024]{2,1,0:T(8,128)(2,1)}, u32[]{:S(2)}, u32[]{:S(2)}) async-start(bf16[16,136,1024]{2,1,0:T(8,128)(2,1)} %backward_experts.1), calls=%async_computation.4 | async-start | bytes 8912896 | tf_op jit(solution)/shard_map/all_to_all | solution.py:282
  200.6 0.2 reduce-scatter.5.cloned.1.call-start
  200.8 37.5 %reduce-scatter.3.cloned.1.call-done = bf16[512,1024]{1,0:T(8,128)(2,1)} async-done(((bf16[2048,1024]{1,0:T(8,128)(2,1)}), bf16[512,1024]{1,0:T(8,128)(2,1)}) %reduce-scatter.3.cloned.1.call-update) | async-done | bytes 1048592 | tf_op jit(solution)/shard_map/reduce_scatter | solution.py:301
  238.3 0.0 reduce-scatter.5.cloned.1.call-update
  238.4 41.4 %all-to-all-done.2 = bf16[16,136,1024]{2,1,0:T(8,128)(2,1)} async-done(((bf16[16,136,1024]{2,1,0:T(8,128)(2,1)}), bf16[16,136,1024]{2,1,0:T(8,128)(2,1)}, u32[]{:S(2)}, u32[]{:S(2)}) %all-to-all-start.2) | async-done | bytes 4456480 | tf_op jit(solution)/shard_map/all_to_all | solution.py:282
  279.7 0.8 slice.65
  280.5 0.2 reshape.153
  280.8 0.1 reduce_sum.60
  280.9 0.1 copy.25
  281.0 0.1 broadcast_in_dim.112
  281.1 3.4 %convert_element_type.34 = f32[16,136,1024]{2,1,0:T(8,128)S(1)} convert(bf16[16,136,1024]{2,1,0:T(8,128)(2,1)} %all-to-all-done.2) | non-fusion elementwise | flops 2228224 | bytes 13369344 | tf_op jit(solution)/shard_map/convert_element_type | solution.py:304
  284.5 0.2 select_reduce_fusion
  284.8 0.6 bitcast_divide_fusion
  285.4 1.5 slice_reduce_fusion
  286.9 0.0 reduce-scatter.5.cloned.1.call-done
  (10 shorter events, 0.2 us)
Async XLA Ops:
  7.2 16.8 %copy-start.2 = (s32[128,6]{0,1:T(8,128)S(1)}, s32[128,6]{0,1:T(8,128)}, u32[]{:S(2)}) copy-start(s32[128,6]{0,1:T(8,128)} %param.7) | copy-start | bytes 9220
  7.2 16.9 %copy-start.3 = (f32[128,6]{0,1:T(8,128)S(1)}, f32[128,6]{0,1:T(8,128)}, u32[]{:S(2)}) copy-start(f32[128,6]{0,1:T(8,128)} %param.8) | copy-start | bytes 9220
  7.2 18.0 %copy-start = (bf16[128,1024]{1,0:T(8,128)(2,1)S(1)}, bf16[128,1024]{1,0:T(8,128)(2,1)}, u32[]{:S(2)}) copy-start(bf16[128,1024]{1,0:T(8,128)(2,1)} %param.6) | copy-start | bytes 786436
  7.2 127.8 %all-gather.2.cloned.1.call-start = ((), (), s32[]{:S(2)}) async-start(), calls=%async_computation.5 | async-start | bytes 17842176 | tf_op jit(solution)/shard_map/all_gather | solution.py:251
  10.3 12.0 %collective-permute-start = (bf16[3,44,1024]{2,0,1:T(4,128)(2,1)S(1)}, bf16[3,44,1024]{2,0,1:T(4,128)(2,1)S(1)}, u32[]{:S(2)}, u32[]{:S(2)}) collective-permute-start(bf16[3,44,1024]{2,0,1:T(4,128)(2,1)S(1)} %pad_maximum_fusion.2), channel_id=1, source_target_pairs={{0,128},{32,160},{64,192},{96,224},{128,0},{160,32},{192,64},{224,... | collective-permute-start | bytes 811016 | tf_op jit(solution)/shard_map/ppermute | solution.py:249
  26.4 57.9 %copy-start.1 = (bf16[128,1024]{1,0:T(8,128)(2,1)S(1)}, bf16[128,1024]{1,0:T(8,128)(2,1)}, u32[]{:S(2)}) copy-start(bf16[128,1024]{1,0:T(8,128)(2,1)} %param.11) | copy-start | bytes 786436
  87.0 74.1 %all-to-all-start.1 = ((bf16[16,128,1024]{2,1,0:T(8,128)(2,1)}), bf16[16,128,1024]{2,1,0:T(8,128)(2,1)}, u32[]{:S(2)}, u32[]{:S(2)}) async-start(bf16[16,128,1024]{2,1,0:T(8,128)(2,1)} %broadcast_in_dim.111), calls=%async_computation.3 | async-start | bytes 8388608 | tf_op jit(solution)/shard_map/all_to_all | solution.py:282
  93.3 145.0 %reduce-scatter.3.cloned.1.call-start = ((), (), s32[]{:S(2)}) async-start(), calls=%async_computation.6 | async-start | bytes 5242880 | tf_op jit(solution)/shard_map/reduce_scatter | solution.py:301
  193.4 86.4 %all-to-all-start.2 = ((bf16[16,136,1024]{2,1,0:T(8,128)(2,1)}), bf16[16,136,1024]{2,1,0:T(8,128)(2,1)}, u32[]{:S(2)}, u32[]{:S(2)}) async-start(bf16[16,136,1024]{2,1,0:T(8,128)(2,1)} %backward_experts.1), calls=%async_computation.4 | async-start | bytes 8912896 | tf_op jit(solution)/shard_map/all_to_all | solution.py:282
  200.6 86.3 %reduce-scatter.5.cloned.1.call-start = ((), (), s32[]{:S(2)}) async-start(), calls=%async_computation.7 | async-start | bytes 1310720 | tf_op jit(solution)/shard_map/reduce_scatter | solution.py:301
Sparse Core Ops, SparseCore 0:
  24.1 110.8 all-gather.1
  161.2 77.1 reduce-scatter.2
  242.0 41.2 reduce-scatter.4

commit v8 on v7

--- a/solution.py
+++ b/solution.py
@@ -44,7 +44,7 @@
         out_ref[s, 0:tok, :] = sums.astype(out_ref.dtype)
         return carry
 
-    lax.fori_loop(0, sources, one, 0)
+    lax.fori_loop(0, sources, one, 0, unroll=4)
 
 
 def swish(pre, hidden):
@@ -91,7 +91,7 @@
             slots[s] = (cs * scale).astype(jnp.bfloat16)
             return carry
 
-        lax.fori_loop(0, sources, one, 0)
+        lax.fori_loop(0, sources, one, 0, unroll=4)
         dots[...] = jnp.zeros_like(dots)
 
     kept = []
@@ -129,7 +129,7 @@
             out_ref[s, tok : tok + low_rows, :] = jnp.concatenate(line, axis=1).astype(jnp.bfloat16)
             return carry
 
-        lax.fori_loop(0, sources, one, 0)
+        lax.fori_loop(0, sources, one, 0, unroll=4)
 
 
 def params():

time: 294 us -> 298 us (1.014)
  the two profiles are of different devices: /device:TPU:48 before, /device:TPU:1 now
where the time goes in v8:
time: 298 us; the launch traced here: 297 us
  waiting for transfers between devices  122 us (41%)
  Pallas kernels  64.3 us (22%)
  blocking collectives  61.1 us (21%)
  starting transfers between devices  15.4 us (5%)
  between operations  14 us (5%)
  local copies, waits for them, and re-layouts  11.5 us (4%)
  other arithmetic  8.83 us (3%)
    all_to_all x1, blocking collectives, body(): lax.all_to_all(a, 'dp', split_axis=0, concat_axis=0, tiled=True)  61.1 us
    reduce_scatter x2, waiting for transfers between devices, body(): lax.psum_scatter(layer_output, 'dp', scatter_dimension=0, axis_index_grou...  56.3 us
    all_to_all x2, waiting for transfers between devices, body(): lax.all_to_all(a, 'dp', split_axis=0, concat_axis=0, tiled=True)  30.5 us
    all_gather x1, waiting for transfers between devices, body(): weights = lax.all_gather(mine, 'expert', axis=0, tiled=False)  30 us
    pallas_call x1, Pallas kernels, backward(): pl.pallas_call(backward_kernel, grid=(half // STEP,), in_specs=[pl.BlockS...  26.3 us
    pallas_call x1, Pallas kernels, forward(): pl.pallas_call(forward_kernel, grid=(half // STEP,), in_specs=[pl.BlockSp...  22.8 us
    pallas_call x1, Pallas kernels, gather_rows(): pl.pallas_call(gather_kernel, grid=(sources,), in_specs=[pl.BlockSpec((1,...  15.2 us
    all_to_all x2, starting transfers between devices, body(): lax.all_to_all(a, 'dp', split_axis=0, concat_axis=0, tiled=True)  11.1 us
  transfers between devices with their start and end apart: 6, of which 5 were waited for; matrix products, arithmetic and copies ran while one was open for 5% of the time, Pallas kernels for 22%

profile of v8, /device:TPU:1, one launch (start us, length us, event | category | flops | bytes accessed | tf_op | source)
XLA Modules:
  0.0 297.0 jit_solution(7858805353013458738)
XLA Ops:
  7.2 0.0 copy-start.2
  7.2 0.0 copy-start.3
  7.2 0.0 copy-start
  7.2 0.0 all-gather.2.cloned.1.call-start
  7.3 1.3 dynamic-slice_bitcast_fusion.1
  8.6 1.4 constant_dynamic-slice_fusion.1
  10.0 0.4 pad_maximum_fusion.2
  10.3 3.9 %collective-permute-start = (bf16[3,44,1024]{2,0,1:T(4,128)(2,1)S(1)}, bf16[3,44,1024]{2,0,1:T(4,128)(2,1)S(1)}, u32[]{:S(2)}, u32[]{:S(2)}) collective-permute-start(bf16[3,44,1024]{2,0,1:T(4,128)(2,1)S(1)} %pad_maximum_fusion.2), channel_id=1, source_target_pairs={{0,128},{32,160},{64,192},{96,224},{128,0},{160,32},{192,64},{224,... | collective-permute-start | bytes 811016 | tf_op jit(solution)/shard_map/ppermute | solution.py:249
  14.3 4.8 %collective-permute-done = bf16[3,44,1024]{2,0,1:T(4,128)(2,1)S(1)} collective-permute-done((bf16[3,44,1024]{2,0,1:T(4,128)(2,1)S(1)}, bf16[3,44,1024]{2,0,1:T(4,128)(2,1)S(1)}, u32[]{:S(2)}, u32[]{:S(2)}) %collective-permute-start) | collective-permute-done | bytes 270368 | tf_op jit(solution)/shard_map/ppermute | solution.py:249
  19.1 0.5 pad_maximum_fusion.1
  19.6 1.0 copy.22
  20.7 0.0 all-gather.2.cloned.1.call-update
  20.7 0.0 copy-done.2
  20.7 0.0 copy-done.3
  20.8 0.1 fusion.13
  20.9 0.2 select_reduce_fusion.1
  21.2 0.2 slice_reduce_fusion.3
  21.4 0.1 concatenate.50
  21.5 0.1 concatenate.51
  21.6 0.1 concatenate.54
  21.6 0.1 concatenate.55
  21.8 0.1 fusion.12
  21.9 0.0 copy-done
  21.9 0.5 broadcast_in_dim.98
  22.4 0.7 pad_maximum_fusion
  23.2 0.0 copy-start.1
  23.2 61.1 %all_to_all.15.rows_ref = bf16[16,136,1024]{2,1,0:T(8,128)(2,1)} all-to-all(bf16[16,136,1024]{2,1,0:T(8,128)(2,1)S(1)} %pad_maximum_fusion), channel_id=1, replica_groups=mesh['dp'=16,'expert'=32] {'dp'}, dimensions={0} | all-to-all | bytes 8912896 | tf_op jit(solution)/shard_map/all_to_all | solution.py:282
  84.3 0.0 copy-done.1
  84.3 2.6 broadcast_in_dim.111
  86.9 4.6 %all-to-all-start.1 = ((bf16[16,128,1024]{2,1,0:T(8,128)(2,1)}), bf16[16,128,1024]{2,1,0:T(8,128)(2,1)}, u32[]{:S(2)}, u32[]{:S(2)}) async-start(bf16[16,128,1024]{2,1,0:T(8,128)(2,1)} %broadcast_in_dim.111), calls=%async_computation.3 | async-start | bytes 8388608 | tf_op jit(solution)/shard_map/all_to_all | solution.py:282
  91.4 0.2 reduce-scatter.3.cloned.1.call-start
  91.7 1.0 slice_convert_fusion
  92.7 0.3 copy.27
  93.0 0.8 copy.28
  93.8 0.1 reshape.151
  93.9 0.1 copy.23
  94.0 0.1 copy.24
  94.1 15.2 %gather_rows.1.x_ref = bf16[32,256,1024]{2,1,0:T(8,128)(2,1)} custom-call(f32[16,32,128]{2,1,0:T(8,128)} %bitcast.32, bf16[16,136,1024]{2,1,0:T(8,128)(2,1)} %all_to_all.15.rows_ref), custom_call_target="tpu_custom_call" | custom-call | flops 2147483648 | bytes 21233664 | tf_op jit(solution)/shard_map/gather_rows/pallas_call | solution.py:150
  109.3 30.0 %all-gather.2.cloned.1.call-done.w_ref = bf16[32,264,1024]{2,1,0:T(8,128)(2,1)} async-done(((bf16[1,264,1024]{2,1,0:T(8,128)(2,1)}), bf16[32,264,1024]{2,1,0:T(8,128)(2,1)}) %all-gather.2.cloned.1.call-update) | async-done | bytes 17301520 | tf_op jit(solution)/shard_map/all_gather | solution.py:251
  139.3 0.7 broadcast_in_dim.109.g_ref
  140.0 22.8 %forward_experts.1 = (bf16[16,128,1024]{2,1,0:T(8,128)(2,1)}, f32[32,256,176]{2,1,0:T(8,128)}) custom-call(bf16[32,264,1024]{2,1,0:T(8,128)(2,1)} %all-gather.2.cloned.1.call-done.w_ref, bf16[32,256,1024]{2,1,0:T(8,128)(2,1)} %gather_rows.1.x_ref, f32[32,8,256]{2,1,0:T(8,128)} %broadcast_in_dim.109.g_ref, f32[16,32,128]{2,1,0:T(8,128)} %bitcast.33), custom_call_target="tpu_custom_call" | custom-call | flops 4429185024 | bytes 34078720 | tf_op jit(solution)/shard_map/forward_experts/pallas_call | solution.py:174
  162.8 0.0 reduce-scatter.3.cloned.1.call-update
  162.8 0.0 all-to-all-done.1.c_ref
  162.9 0.7 broadcast_in_dim.110.g_ref
  163.6 26.3 %backward_experts.1 = bf16[16,136,1024]{2,1,0:T(8,128)(2,1)} custom-call(bf16[32,264,1024]{2,1,0:T(8,128)(2,1)} %all-gather.2.cloned.1.call-done.w_ref, f32[32,256,176]{2,1,0:T(8,128)} %get-tuple-element.6.pre_ref, f32[16,8,512]{2,1,0:T(8,128)} %broadcast_in_dim.110.g_ref, f32[16,32,128]{2,1,0:T(8,128)} %bitcast.34, bf16[16,128,1024]{2,1,0:T(8,128)(2,1)} %all-to-all-done.1.c_ref), custom_call_target="tpu_custom_call" | custom-call | flops 44291850240 | bytes 23068672 | tf_op jit(solution)/shard_map/backward_experts/pallas_call | solution.py:209
  189.9 6.6 %all-to-all-start.2 = ((bf16[16,136,1024]{2,1,0:T(8,128)(2,1)}), bf16[16,136,1024]{2,1,0:T(8,128)(2,1)}, u32[]{:S(2)}, u32[]{:S(2)}) async-start(bf16[16,136,1024]{2,1,0:T(8,128)(2,1)} %backward_experts.1), calls=%async_computation.4 | async-start | bytes 8912896 | tf_op jit(solution)/shard_map/all_to_all | solution.py:282
  196.5 0.0 reduce-scatter.5.cloned.1.call-start
  196.5 45.6 %reduce-scatter.3.cloned.1.call-done = bf16[512,1024]{1,0:T(8,128)(2,1)} async-done(((bf16[2048,1024]{1,0:T(8,128)(2,1)}), bf16[512,1024]{1,0:T(8,128)(2,1)}) %reduce-scatter.3.cloned.1.call-update) | async-done | bytes 1048592 | tf_op jit(solution)/shard_map/reduce_scatter | solution.py:301
  242.1 0.0 reduce-scatter.5.cloned.1.call-update
  242.1 30.5 %all-to-all-done.2 = bf16[16,136,1024]{2,1,0:T(8,128)(2,1)} async-done(((bf16[16,136,1024]{2,1,0:T(8,128)(2,1)}), bf16[16,136,1024]{2,1,0:T(8,128)(2,1)}, u32[]{:S(2)}, u32[]{:S(2)}) %all-to-all-start.2) | async-done | bytes 4456480 | tf_op jit(solution)/shard_map/all_to_all | solution.py:282
  272.6 0.8 slice.65
  273.4 0.2 reshape.153
  273.6 0.1 reduce_sum.60
  273.8 0.1 copy.25
  273.9 0.1 broadcast_in_dim.112
  274.0 3.3 %convert_element_type.34 = f32[16,136,1024]{2,1,0:T(8,128)S(1)} convert(bf16[16,136,1024]{2,1,0:T(8,128)(2,1)} %all-to-all-done.2) | non-fusion elementwise | flops 2228224 | bytes 13369344 | tf_op jit(solution)/shard_map/convert_element_type | solution.py:304
  277.3 0.2 select_reduce_fusion
  277.6 0.6 bitcast_divide_fusion
  278.2 1.5 slice_reduce_fusion
  279.7 10.7 %reduce-scatter.5.cloned.1.call-done = bf16[128,1024]{1,0:T(8,128)(2,1)} async-done(((bf16[512,1024]{1,0:T(8,128)(2,1)}), bf16[128,1024]{1,0:T(8,128)(2,1)}) %reduce-scatter.5.cloned.1.call-update) | async-done | bytes 262160 | tf_op jit(solution)/shard_map/reduce_scatter | solution.py:301
  (10 shorter events, 0.2 us)
Async XLA Ops:
  7.2 13.5 %copy-start.2 = (s32[128,6]{0,1:T(8,128)S(1)}, s32[128,6]{0,1:T(8,128)}, u32[]{:S(2)}) copy-start(s32[128,6]{0,1:T(8,128)} %param.7) | copy-start | bytes 9220
  7.2 13.6 %copy-start.3 = (f32[128,6]{0,1:T(8,128)S(1)}, f32[128,6]{0,1:T(8,128)}, u32[]{:S(2)}) copy-start(f32[128,6]{0,1:T(8,128)} %param.8) | copy-start | bytes 9220
  7.2 14.7 %copy-start = (bf16[128,1024]{1,0:T(8,128)(2,1)S(1)}, bf16[128,1024]{1,0:T(8,128)(2,1)}, u32[]{:S(2)}) copy-start(bf16[128,1024]{1,0:T(8,128)(2,1)} %param.6) | copy-start | bytes 786436
  7.2 132.1 %all-gather.2.cloned.1.call-start = ((), (), s32[]{:S(2)}) async-start(), calls=%async_computation.5 | async-start | bytes 17842176 | tf_op jit(solution)/shard_map/all_gather | solution.py:251
  10.3 8.8 %collective-permute-start = (bf16[3,44,1024]{2,0,1:T(4,128)(2,1)S(1)}, bf16[3,44,1024]{2,0,1:T(4,128)(2,1)S(1)}, u32[]{:S(2)}, u32[]{:S(2)}) collective-permute-start(bf16[3,44,1024]{2,0,1:T(4,128)(2,1)S(1)} %pad_maximum_fusion.2), channel_id=1, source_target_pairs={{0,128},{32,160},{64,192},{96,224},{128,0},{160,32},{192,64},{224,... | collective-permute-start | bytes 811016 | tf_op jit(solution)/shard_map/ppermute | solution.py:249
  23.2 61.1 %copy-start.1 = (bf16[128,1024]{1,0:T(8,128)(2,1)S(1)}, bf16[128,1024]{1,0:T(8,128)(2,1)}, u32[]{:S(2)}) copy-start(bf16[128,1024]{1,0:T(8,128)(2,1)} %param.11) | copy-start | bytes 786436
  86.9 76.0 %all-to-all-start.1 = ((bf16[16,128,1024]{2,1,0:T(8,128)(2,1)}), bf16[16,128,1024]{2,1,0:T(8,128)(2,1)}, u32[]{:S(2)}, u32[]{:S(2)}) async-start(bf16[16,128,1024]{2,1,0:T(8,128)(2,1)} %broadcast_in_dim.111), calls=%async_computation.3 | async-start | bytes 8388608 | tf_op jit(solution)/shard_map/all_to_all | solution.py:282
  91.4 150.7 %reduce-scatter.3.cloned.1.call-start = ((), (), s32[]{:S(2)}) async-start(), calls=%async_computation.6 | async-start | bytes 5242880 | tf_op jit(solution)/shard_map/reduce_scatter | solution.py:301
  189.9 82.7 %all-to-all-start.2 = ((bf16[16,136,1024]{2,1,0:T(8,128)(2,1)}), bf16[16,136,1024]{2,1,0:T(8,128)(2,1)}, u32[]{:S(2)}, u32[]{:S(2)}) async-start(bf16[16,136,1024]{2,1,0:T(8,128)(2,1)} %backward_experts.1), calls=%async_computation.4 | async-start | bytes 8912896 | tf_op jit(solution)/shard_map/all_to_all | solution.py:282
  196.5 94.0 %reduce-scatter.5.cloned.1.call-start = ((), (), s32[]{:S(2)}) async-start(), calls=%async_computation.7 | async-start | bytes 1310720 | tf_op jit(solution)/shard_map/reduce_scatter | solution.py:301
Sparse Core Ops, SparseCore 0:
  20.8 118.4 all-gather.1
  163.0 79.0 reduce-scatter.2
  245.7 44.6 reduce-scatter.4
